TPU v7x, 256 devices: a whole 4x4x8 slice. The times are simulated.
256 devices in a mesh: video: 32 (over z, x), audio: 8 (over y, core).
Axes of the slice: x: 4, y: 4, z: 8, core: 2. Of those that a mesh axis runs over, the one named last changes fastest.
Arguments:
- video_query: bfloat16 [16384, 3072], P('video', 'audio'), as said below
- video_kv: bfloat16 [2, 16384, 3072], P(None, 'video', 'audio'), may hold values from -6 to 6
- audio_qkv: bfloat16 [3, 2048, 3072], P(None, 'audio')
- video_count: int32 [64], P('video'), may hold values from 64 to 256, as said below
- audio_count: int32 [32], replicated, may hold values from 16 to 64, as said below
- video_range: int32 [32, 2], replicated, may hold values from 0 to 64, as said below
Outputs:
- video_out: bfloat16 [16384, 3072], P('video', 'audio')
- audio_out: bfloat16 [2048, 3072], P(None, 'audio')
Inputs may be any that keep to these rules, and one draw needn't show every extreme that they name: `video_query`: queries. `video_count`: some video block is full. `audio_count`: some audio block is full. `video_range`: audio block i meets video blocks i * 2 to (i + 1) * 2 - 1 and possibly more, all within (i - 2) * 2 to (i + 3) * 2 - 1; start before end.
All inputs are finite; a program needn't handle non-finite values.
Results may differ from a plain program's by a relative error of at most 0.0045.
Values may be sent and summed in bfloat16 or wider, within the bound.
No kernel may reach another device: no remote copies, remote signals or barrier semaphores. Data moves between devices by JAX's collectives and lax.ppermute only.
A program may use at most 256 MiB of HBM per device.

v0:
```python
import math

import jax
import jax.numpy as jnp
from jax import lax
from jax.sharding import PartitionSpec as P

HEADS = 24
VBS = 256
ABS = 64
REACH = 2


def joined(part, axis, combine):
    gathered = jax.tree.map(lambda a: lax.all_gather(a, axis), part)

    def take(source):
        return jax.tree.map(lambda a: lax.dynamic_index_in_dim(a, source, 0, False), gathered)

    return lax.fori_loop(
        1, lax.axis_size(axis), lambda source, state: combine(state, take(source)), take(0)
    )


def pair_rules(segment_index, count_here, audio_count, video_range, period, seg_rows, win_rows):
    blocks_total = audio_count.shape[0]
    win_index = jnp.arange(win_rows, dtype=jnp.int32)
    audio_block = segment_index * period - REACH * period + win_index // ABS
    inside = (audio_block >= 0) & (audio_block < blocks_total)
    matches = audio_block[:, None] == jnp.arange(blocks_total, dtype=jnp.int32)[None, :]
    range_start = jnp.sum(jnp.where(matches, video_range[None, :, 0], 0), axis=1)
    range_end = jnp.sum(jnp.where(matches, video_range[None, :, 1], 0), axis=1)
    live_count = jnp.sum(jnp.where(matches, audio_count[None, :], 0), axis=1)
    audio_live = inside & (win_index % ABS < live_count)
    tok_index = jnp.arange(seg_rows, dtype=jnp.int32)
    video_block = segment_index * (seg_rows // VBS) + tok_index // VBS
    video_live = tok_index % VBS < jnp.repeat(count_here, VBS)
    paired = (
        inside[:, None]
        & (range_start[:, None] <= video_block[None, :])
        & (video_block[None, :] < range_end[:, None])
    )
    return (paired, audio_live, video_live)


def soft_parts(scores, allowed):
    masked = jnp.where(allowed, scores, -1e30)
    row_peak = jnp.max(masked, axis=-1, keepdims=True)
    raised = jnp.where(allowed, jnp.exp(scores - row_peak), 0.0)
    return (row_peak[..., 0], jnp.sum(raised, axis=-1), raised.astype(jnp.bfloat16))


def merge_parts(former, latter):
    row_peak = jnp.maximum(former[0], latter[0])
    keep_former = jnp.exp(former[0] - row_peak)
    keep_latter = jnp.exp(latter[0] - row_peak)
    row_total = former[1] * keep_former + latter[1] * keep_latter
    per_head = former[2].shape[1] // row_peak.shape[0]
    blended = former[2] * jnp.repeat(keep_former.T, per_head, axis=1) + latter[2] * jnp.repeat(
        keep_latter.T, per_head, axis=1
    )
    return (row_peak, row_total, blended)


def finish_rows(parts, head_dim):
    return (parts[2] / jnp.repeat(parts[1].T, head_dim, axis=1)).astype(jnp.bfloat16)


def local(video_query, video_kv, audio_qkv, video_count, audio_count, video_range):
    video_devices = lax.axis_size("video")
    audio_devices = lax.axis_size("audio")
    own_index = lax.axis_index("video")
    seg_rows, columns = video_query.shape
    audio_local = audio_qkv.shape[1]
    audio_total = audio_local * audio_devices
    heads_here = HEADS // audio_devices
    head_dim = columns // heads_here
    period = audio_local // ABS * audio_devices // video_devices
    span_rows = period * ABS
    lead_rows = REACH * span_rows
    win_rows = (2 * REACH + 1) * span_rows
    score_scale = 1.0 / math.sqrt(head_dim)
    by_group = audio_qkv.reshape(3, audio_local, audio_devices, columns)
    exchanged = lax.all_to_all(by_group, "audio", split_axis=2, concat_axis=1, tiled=True)
    audio_all = exchanged.reshape(3, audio_total, columns)
    padding = jnp.zeros((3, lead_rows, columns), audio_all.dtype)
    padded = jnp.concatenate([padding, audio_all, padding], axis=1)
    window = lax.dynamic_slice_in_dim(padded, own_index * span_rows, win_rows, 1)
    paired, audio_live, video_live = pair_rules(
        own_index, video_count, audio_count, video_range, period, seg_rows, win_rows
    )
    queries = video_query.reshape(seg_rows, heads_here, head_dim)
    audio_keys = window[1].reshape(win_rows, heads_here, head_dim)
    audio_values = window[2].reshape(win_rows, heads_here, head_dim)
    scores = (
        jnp.einsum("thd,rhd->htr", queries, audio_keys, preferred_element_type=jnp.float32)
        * score_scale
    )
    row_peak, row_total, weights = soft_parts(scores, (paired.T & audio_live[None, :])[None])
    blended = (
        jnp.einsum("htr,rhd->thd", weights, audio_values, preferred_element_type=jnp.float32)
        / row_total.T[:, :, None]
    )
    video_out = blended.reshape(seg_rows, columns).astype(jnp.bfloat16)
    audio_queries = window[0].reshape(win_rows, heads_here, head_dim)
    video_keys = video_kv[0].reshape(seg_rows, heads_here, head_dim)
    video_values = video_kv[1].reshape(seg_rows, heads_here, head_dim)
    scores_back = (
        jnp.einsum("rhd,thd->hrt", audio_queries, video_keys, preferred_element_type=jnp.float32)
        * score_scale
    )
    part_peak, part_total, part_weights = soft_parts(
        scores_back, (paired & video_live[None, :])[None]
    )
    part_out = jnp.einsum(
        "hrt,thd->rhd", part_weights, video_values, preferred_element_type=jnp.float32
    ).reshape(win_rows, columns)
    padded_rows = audio_total + 2 * lead_rows
    start_row = own_index * span_rows
    full_peak = lax.dynamic_update_slice_in_dim(
        jnp.full((heads_here, padded_rows), -1e30, jnp.float32), part_peak, start_row, 1
    )
    full_total = lax.dynamic_update_slice_in_dim(
        jnp.zeros((heads_here, padded_rows), jnp.float32), part_total, start_row, 1
    )
    full_out = lax.dynamic_update_slice_in_dim(
        jnp.zeros((padded_rows, columns), jnp.float32), part_out, start_row, 0
    )
    merged = joined(
        (
            full_peak[:, lead_rows : lead_rows + audio_total],
            full_total[:, lead_rows : lead_rows + audio_total],
            full_out[lead_rows : lead_rows + audio_total],
        ),
        "video",
        merge_parts,
    )
    audio_out = finish_rows(merged, head_dim)
    return (video_out, audio_out)


def solution(mesh):
    return jax.shard_map(
        local,
        mesh=mesh,
        in_specs=(
            P("video", "audio"),
            P(None, "video", "audio"),
            P(None, "audio", None),
            P("video"),
            P(),
            P(),
        ),
        out_specs=(P("video", "audio"), P(None, "audio")),
        check_vma=False,
    )
```

profile of v0, /device:TPU:8, one launch (start us, length us, event | category | flops | bytes accessed | tf_op | source)
XLA Modules:
  0.0 1105.6 jit_solution(3351088226304225758)
XLA Ops:
  7.2 6.7 copy.69
  13.8 5.0 copy.70
  18.8 6.8 all-to-all-start
  27.4 52.1 %all-to-all-done = bf16[3,256,8,384]{1,3,0,2:T(8,128)(2,1)} async-done(((bf16[3,256,8,384]{1,3,0,2:T(8,128)(2,1)}), bf16[3,256,8,384]{1,3,0,2:T(8,128)(2,1)}, u32[]{:S(2)}, u32[]{:S(2)}) %all-to-all-start) | async-done | bytes 4718624 | tf_op jit(solution)/shard_map/all_to_all | solution.py:84
  79.6 6.7 copy.71
  96.9 3.2 fusion.53
  103.8 53.6 %all-gather.4 = f32[32,3,2048]{2,1,0:T(4,128)S(1)} all-gather(f32[1,3,2048]{2,1,0:T(4,128)S(1)} %slice_bitcast_fusion.1), channel_id=3, replica_groups=mesh['video'=32,'audio'=8] {'video'}, dimensions={0}, use_global_device_ids=true | all-gather | bytes 811008 | tf_op jit(solution)/shard_map/all_gather | solution.py:15
  157.4 51.0 %all-gather.3 = f32[32,3,2048]{2,1,0:T(4,128)S(1)} all-gather(f32[1,3,2048]{2,1,0:T(4,128)S(1)} %slice_bitcast_fusion.3), channel_id=2, replica_groups=mesh['video'=32,'audio'=8] {'video'}, dimensions={0}, use_global_device_ids=true | all-gather | bytes 811008 | tf_op jit(solution)/shard_map/all_gather | solution.py:15
  209.4 525.9 %all-gather.7.cloned.1.call-done = f32[65536,384]{1,0:T(8,128)} async-done(((f32[2048,384]{1,0:T(8,128)}), f32[65536,384]{1,0:T(8,128)}) %all-gather.7.cloned.1.call-update) | async-done | bytes 100663312 | tf_op jit(solution)/shard_map/all_gather | solution.py:15
  737.4 2.3 copy.86
  739.8 355.2 %while.19 = (s32[]{:T(128)}, f32[3,2048]{1,0:T(4,128)S(1)}, f32[3,2048]{1,0:T(4,128)S(1)}, f32[2048,384]{0,1:T(8,128)}, f32[32,3,2048]{2,1,0:T(4,128)}, /*index=...) while((s32[]{:T(128)}, f32[3,2048]{1,0:T(4,128)S(1)}, ...), condition=%wide.region_8.9_spmd, body=%wide.region_7.8_spmd.sunk | while | flops 2402309 | bytes 22388884 | solution.py:20
  743.5 2.3 copy.101
  745.8 5.4 fusion.68
  755.0 2.3 copy.101
  757.3 5.4 fusion.68
  766.4 2.3 copy.101
  768.7 5.4 fusion.68
  777.9 2.3 copy.101
  780.2 5.4 fusion.68
  789.3 2.3 copy.101
  791.7 5.4 fusion.68
  800.8 2.3 copy.101
  803.1 5.4 fusion.68
  812.2 2.3 copy.101
  814.6 5.4 fusion.68
  823.7 2.3 copy.101
  826.0 5.4 fusion.68
  835.2 2.3 copy.101
  837.5 5.4 fusion.68
  846.6 2.3 copy.101
  848.9 5.4 fusion.68
  858.1 2.3 copy.101
  860.4 5.4 fusion.68
  869.5 2.3 copy.101
  871.9 5.4 fusion.68
  881.0 2.3 copy.101
  883.3 5.4 fusion.68
  892.4 2.3 copy.101
  894.8 5.4 fusion.68
  903.9 2.3 copy.101
  906.2 5.4 fusion.68
  915.4 2.3 copy.101
  917.7 5.4 fusion.68
  926.8 2.3 copy.101
  929.1 5.4 fusion.68
  938.3 2.3 copy.101
  940.6 5.4 fusion.68
  949.7 2.3 copy.101
  952.1 5.4 fusion.68
  961.2 2.3 copy.101
  963.5 5.4 fusion.68
  972.7 2.3 copy.101
  975.0 5.4 fusion.68
  986.4 5.4 fusion.68
  997.9 5.4 fusion.68
  1009.3 5.4 fusion.68
  1018.5 2.3 copy.101
  1020.8 5.4 fusion.68
  1032.3 5.4 fusion.68
  1043.7 5.4 fusion.68
  1055.2 5.4 fusion.68
  1066.6 5.4 fusion.68
  1078.1 5.4 fusion.68
  1089.6 5.4 fusion.68
  (194 shorter events, 159.1 us)
Async XLA Ops:
  7.2 18.5 %copy-start = (s32[2]{0:T(128)S(1)}, s32[2]{0:T(128)}, u32[]{:S(2)}) copy-start(s32[2]{0:T(128)} %param.11) | copy-start | bytes 28
  18.8 6.9 copy-start.4
  18.8 60.8 %all-to-all-start = ((bf16[3,256,8,384]{1,3,0,2:T(8,128)(2,1)}), bf16[3,256,8,384]{1,3,0,2:T(8,128)(2,1)}, u32[]{:S(2)}, u32[]{:S(2)}) async-start(bf16[3,256,8,384]{1,3,0,2:T(8,128)(2,1)} %copy.70), calls=%async_computation | async-start | bytes 9437184 | tf_op jit(solution)/shard_map/all_to_all | solution.py:84
  25.6 1.4 copy-start.7
  25.6 1.4 copy-start.8
  25.6 709.7 %all-gather.7.cloned.1.call-start = ((), (), s32[]{:S(2)}) async-start(), calls=%async_computation.1 | async-start | bytes 103809024 | tf_op jit(solution)/shard_map/all_gather | solution.py:15
  93.6 1.0 copy-start.5
  93.6 2.1 copy-start.3
  96.9 3.2 copy-start.6
  157.4 51.0 %copy-start.2 = (f32[32,3,2048]{2,1,0:T(4,128)}, f32[32,3,2048]{2,1,0:T(4,128)S(1)}, u32[]{:S(2)}) copy-start(f32[32,3,2048]{2,1,0:T(4,128)S(1)} %all-gather.4) | copy-start | bytes 2359300
  208.5 1.0 copy-start.1
Sparse Core Ops, SparseCore 0:
  93.8 641.4 all-gather.6
where the time goes:
time: 1110 us
  waiting for transfers between devices  578 us (52%)
  other arithmetic  223 us (20%)
  local copies, waits for them, and re-layouts  171 us (15%)
  blocking collectives  105 us (9%)
  between operations  14.2 us (1%)
    all_gather x1, waiting for transfers between devices, joined(): gathered = jax.tree.map(lambda a: lax.all_gather(a, axis), part)  526 us
    add x31, other arithmetic, merge_parts(): former[2] * jnp.repeat(keep_former.T, per_head, axis=1)  168 us
    dynamic_slice x65, local copies, waits for them, and re-layouts, take(): lax.dynamic_index_in_dim(a, source, 0, False)  139 us
    all_gather x2, blocking collectives, joined(): gathered = jax.tree.map(lambda a: lax.all_gather(a, axis), part)  105 us
    all_to_all x1, waiting for transfers between devices, local(): lax.all_to_all(by_group, 'audio', split_axis=2, concat_axis=1, tiled=True)  52.1 us
    transpose x62, other arithmetic, merge_parts(): blended = former[2] * jnp.repeat(keep_former.T, per_head, axis=1) + latte...  50 us
  transfers between devices with their start and end apart: 2, of which 2 were waited for; matrix products, arithmetic and copies ran while one was open for 1% of the time, Pallas kernels for 0%

commit v1 on v0

v1 whole, which is shorter than its diff:
```python
import math

import jax
import jax.numpy as jnp
from jax import lax
from jax.experimental import pallas as pl
from jax.experimental.pallas import tpu as pltpu
from jax.sharding import PartitionSpec as P

HEADS = 24
VBS = 256
ABS = 64
REACH = 2
ZS = 8
XS = 4
NEG = -1e30
LOG2E = 1.4426950408889634
BOTH = ("video", "audio")

VMEM = pl.BlockSpec(memory_space=pltpu.VMEM)
SMEM = pl.BlockSpec(memory_space=pltpu.SMEM)
ANY = pl.BlockSpec(memory_space=pl.ANY)


def params():
    return pltpu.CompilerParams(vmem_limit_bytes=24 * 1024 * 1024)


def place():
    v = lax.axis_index("video")
    return v, v // XS, v % XS


def pack_kernel(src, q_own, q_out, kv_own, kv_out, sems):
    _, z, x = place()
    columns = q_own.shape[1]
    cols = pl.ds(pl.multiple_of(z * columns, 128), columns)
    half = q_out.shape[0]
    rows = pl.ds(pl.multiple_of(jnp.where(x < REACH, half, 0), half), half)
    copies = [
        pltpu.make_async_copy(src.at[0, :, cols], q_own, sems.at[0]),
        pltpu.make_async_copy(src.at[0, rows, cols], q_out, sems.at[1]),
        pltpu.make_async_copy(src.at[pl.ds(1, 2), :, cols], kv_own, sems.at[2]),
        pltpu.make_async_copy(src.at[pl.ds(1, 2), rows, cols], kv_out, sems.at[3]),
    ]
    for c in copies:
        c.start()
    for c in copies:
        c.wait()


def split3(value):
    hi = value.astype(jnp.bfloat16).astype(jnp.float32)
    rest = value - hi
    mid = rest.astype(jnp.bfloat16).astype(jnp.float32)
    return hi, mid, rest - mid


def audio_kernel(scale, count, ranges, q_own, q_out, kv, *refs):
    outs, (queries, bias) = refs[:5], refs[5:]
    v, z, x = place()
    blocks = ranges.shape[0]
    columns = q_own.shape[1]
    heads = columns // 128
    lane = lax.broadcasted_iota(jnp.int32, (ABS, 2 * VBS), 1)
    for slot in range(5):
        offset = slot - REACH
        at = x + offset
        dst = pl.ds(slot * ABS, ABS)
        own = (at >= 0) & (at < XS)

        @pl.when(own)
        def _():
            queries[dst, :] = q_own[pl.ds(pl.multiple_of(at * ABS, ABS), ABS), :]

        @pl.when(jnp.logical_not(own))
        def _():
            row = jnp.where(at < 0, at + REACH, at - XS) * ABS
            queries[dst, :] = q_out[pl.ds(pl.multiple_of(row, ABS), ABS), :]

        block = v + offset
        inside = (block >= 0) & (block < blocks)
        safe = jnp.clip(block, 0, blocks - 1)
        first, last = ranges[safe, 0], ranges[safe, 1]
        live = []
        for j in range(2):
            vb = v * 2 + j
            paired = inside & (first <= vb) & (vb < last)
            live.append(jnp.where(paired, count[j], 0))
        allowed = (lane < live[0]) | ((lane >= VBS) & (lane < VBS + live[1]))
        bias[dst, :] = jnp.where(allowed, 0.0, NEG)
    stat_lane = lax.broadcasted_iota(jnp.int32, (5 * ABS, 128), 1)
    stats = jnp.zeros((5 * ABS, 128), jnp.float32)
    for h in range(heads):
        cols = slice(h * 128, (h + 1) * 128)
        s = lax.dot_general(
            queries[:, cols], kv[0, :, cols], (((1,), (1,)), ((), ())),
            preferred_element_type=jnp.float32,
        )
        s = s + bias[...]
        peak = jnp.max(s, axis=1, keepdims=True)
        e = jnp.exp2((s - peak) * scale)
        total = jnp.sum(e, axis=1, keepdims=True)
        o = lax.dot_general(
            e.astype(jnp.bfloat16), kv[1, :, cols], (((1,), (0,)), ((), ())),
            preferred_element_type=jnp.float32,
        )
        for i, part in enumerate(split3(peak * scale) + split3(total)):
            stats = jnp.where(stat_lane == h * 6 + i, part, stats)
        for slot in range(5):
            outs[slot][:, cols] = o[slot * ABS : (slot + 1) * ABS].astype(jnp.bfloat16)
    for slot in range(5):
        outs[slot][:, columns:] = stats[slot * ABS : (slot + 1) * ABS].astype(jnp.bfloat16)


def merge_kernel(*refs):
    parts, out = refs[:-1], refs[-1]
    columns = out.shape[1]
    stats = [p[:, columns:].astype(jnp.float32) for p in parts]
    for h in range(columns // 128):
        cols = slice(h * 128, (h + 1) * 128)

        def stat(s, i):
            at = h * 6 + i
            return s[:, at : at + 1] + s[:, at + 1 : at + 2] + s[:, at + 2 : at + 3]

        peaks = [stat(s, 0) for s in stats]
        peak = peaks[0]
        for p in peaks[1:]:
            peak = jnp.maximum(peak, p)
        total, blend = 0.0, 0.0
        for s, p, part in zip(stats, peaks, parts):
            keep = jnp.exp2(p - peak)
            total = total + stat(s, 3) * keep
            blend = blend + part[:, cols].astype(jnp.float32) * keep
        out[:, cols] = (blend / total).astype(jnp.bfloat16)


def video_kernel(scale, audio_count, ranges, query, kv_own, kv_out, out, bias):
    v, z, x = place()
    blocks = ranges.shape[0]
    columns = query.shape[1]
    keys = kv_own.shape[1] + kv_out.shape[1]
    own_keys = kv_own.shape[1]
    lane = lax.broadcasted_iota(jnp.int32, (8, ABS * 2), 1)
    for pair in range(keys // (2 * ABS)):
        for j in range(2):
            vb = v * 2 + j
            allowed = None
            for side in range(2):
                pos = pair * 2 + side
                if pos < XS:
                    block = z * XS + pos
                else:
                    block = z * XS + (pos - XS) + jnp.where(x < REACH, -REACH, XS)
                inside = (block >= 0) & (block < blocks)
                safe = jnp.clip(block, 0, blocks - 1)
                paired = inside & (ranges[safe, 0] <= vb) & (vb < ranges[safe, 1])
                live = jnp.where(paired, audio_count[safe], 0)
                here = (lane >= side * ABS) & (lane < side * ABS + live)
                allowed = here if allowed is None else allowed | here
            bias[j, :, pair * 2 * ABS : (pair + 1) * 2 * ABS] = jnp.where(allowed, 0.0, NEG)
    for j in range(2):
        rows = slice(j * VBS, (j + 1) * VBS)
        for h in range(columns // 128):
            cols = slice(h * 128, (h + 1) * 128)
            dims = (((1,), (1,)), ((), ()))
            s1 = lax.dot_general(
                query[rows, cols], kv_own[0, :, cols], dims, preferred_element_type=jnp.float32
            )
            s2 = lax.dot_general(
                query[rows, cols], kv_out[0, :, cols], dims, preferred_element_type=jnp.float32
            )
            s1 = s1 + bias[j, 0:1, :own_keys]
            s2 = s2 + bias[j, 0:1, own_keys:]
            peak = jnp.maximum(
                jnp.max(s1, axis=1, keepdims=True), jnp.max(s2, axis=1, keepdims=True)
            )
            e1 = jnp.exp2((s1 - peak) * scale)
            e2 = jnp.exp2((s2 - peak) * scale)
            total = jnp.sum(e1, axis=1, keepdims=True) + jnp.sum(e2, axis=1, keepdims=True)
            dims = (((1,), (0,)), ((), ()))
            o = lax.dot_general(
                e1.astype(jnp.bfloat16), kv_own[1, :, cols], dims,
                preferred_element_type=jnp.float32,
            ) + lax.dot_general(
                e2.astype(jnp.bfloat16), kv_out[1, :, cols], dims,
                preferred_element_type=jnp.float32,
            )
            out[rows, cols] = (o / total).astype(jnp.bfloat16)


ZHELD = (0, 3, -2, 1, -1, 4, 2, -3)


def assemble_kernel(*refs):
    chunks, out, sems = refs[:8], refs[8], refs[9]
    _, z, x = place()
    copies = []
    for i, rel in enumerate(ZHELD):
        zz = lax.rem(z + rel + ZS, ZS)
        for k in range(XS):
            row = (zz * XS + lax.rem(x - k + XS, XS)) * ABS
            copies.append(
                pltpu.make_async_copy(
                    chunks[i].at[pl.ds(k * ABS, ABS), :],
                    out.at[pl.ds(pl.multiple_of(row, ABS), ABS), :],
                    sems.at[i * XS + k],
                )
            )
    for c in copies:
        c.start()
    for c in copies:
        c.wait()


def shifted(value, step):
    n = ZS * XS
    return lax.ppermute(value, "video", [(v, (v + step) % n) for v in range(n)])


def along_x(value, step):
    pairs = [(z * XS + x, z * XS + (x + step) % XS) for z in range(ZS) for x in range(XS)]
    return lax.ppermute(value, "video", pairs)


def from_z(value, rel):
    return shifted(value, -rel * XS)


def local(video_query, video_kv, audio_qkv, video_count, audio_count, video_range):
    seg_rows, columns = video_query.shape
    shard_rows = audio_qkv.shape[1]
    half = REACH * ABS
    bf16 = jnp.bfloat16
    f32 = jnp.float32
    scale = LOG2E / math.sqrt(128)
    audio_devices = lax.axis_size("audio")

    def flat(z, x, a):
        return ((z % ZS) * XS + x) * audio_devices + a

    q_own, q_out, kv_own, kv_out = pl.pallas_call(
        pack_kernel,
        out_shape=(
            jax.ShapeDtypeStruct((shard_rows, columns), bf16),
            jax.ShapeDtypeStruct((half, columns), bf16),
            jax.ShapeDtypeStruct((2, shard_rows, columns), bf16),
            jax.ShapeDtypeStruct((2, half, columns), bf16),
        ),
        in_specs=[ANY],
        out_specs=(VMEM,) * 4,
        scratch_shapes=[pltpu.SemaphoreType.DMA((4,))],
        compiler_params=params(),
        name="pack",
    )(audio_qkv)
    every = [(z, x, a) for z in range(ZS) for x in range(XS) for a in range(audio_devices)]
    own_pairs = [(flat(z, x, a), flat(a, x, z)) for z, x, a in every]
    out_pairs = [
        (flat(z, x, a), flat(a + 1 if x < REACH else a - 1, x, z)) for z, x, a in every
    ]
    q_own = lax.ppermute(q_own, BOTH, own_pairs)
    q_out = lax.ppermute(q_out, BOTH, out_pairs)
    kv_own = lax.ppermute(kv_own, BOTH, own_pairs)
    kv_out = lax.ppermute(kv_out, BOTH, out_pairs)

    packed = jax.ShapeDtypeStruct((ABS, columns + 128), bf16)
    parts = pl.pallas_call(
        lambda *refs: audio_kernel(scale, *refs),
        out_shape=(packed,) * 5,
        in_specs=[SMEM, SMEM, VMEM, VMEM, VMEM],
        out_specs=(VMEM,) * 5,
        scratch_shapes=[
            pltpu.VMEM((5 * ABS, columns), bf16),
            pltpu.VMEM((5 * ABS, seg_rows), f32),
        ],
        compiler_params=params(),
        name="audio_side",
    )(video_count, video_range, q_own, q_out, video_kv)
    held = [
        shifted(part, slot - REACH) if slot != REACH else part for slot, part in enumerate(parts)
    ]
    block_out = pl.pallas_call(
        merge_kernel,
        out_shape=jax.ShapeDtypeStruct((ABS, columns), bf16),
        in_specs=[VMEM] * 5,
        out_specs=VMEM,
        compiler_params=params(),
        name="merge",
    )(*held)

    video_out = pl.pallas_call(
        lambda *refs: video_kernel(scale, *refs),
        out_shape=jax.ShapeDtypeStruct((seg_rows, columns), bf16),
        in_specs=[SMEM, SMEM, VMEM, VMEM, VMEM],
        out_specs=VMEM,
        scratch_shapes=[pltpu.VMEM((2, 8, shard_rows + half), f32)],
        compiler_params=params(),
        name="video_side",
    )(audio_count, video_range, video_query, kv_own, kv_out)

    row = jnp.concatenate([block_out] + [along_x(block_out, k) for k in range(1, XS)], axis=0)
    z3, zm2 = from_z(row, 3), from_z(row, -2)
    z1, zm1 = from_z(row, 1), from_z(row, -1)
    z4, z2, zm3 = from_z(z3, 1), from_z(z3, -1), from_z(zm2, -1)
    audio_out = pl.pallas_call(
        assemble_kernel,
        out_shape=jax.ShapeDtypeStruct((ZS * XS * ABS, columns), bf16),
        in_specs=[VMEM] * 8,
        out_specs=ANY,
        scratch_shapes=[pltpu.SemaphoreType.DMA((ZS * XS,))],
        compiler_params=params(),
        name="assemble",
    )(row, z3, zm2, z1, zm1, z4, z2, zm3)
    return (video_out, audio_out)


def solution(mesh):
    return jax.shard_map(
        local,
        mesh=mesh,
        in_specs=(
            P("video", "audio"),
            P(None, "video", "audio"),
            P(None, "audio", None),
            P("video"),
            P(),
            P(),
        ),
        out_specs=(P("video", "audio"), P(None, "audio")),
        check_vma=False,
    )
```

time: 1110 us -> 104 us (0.09)
  waiting for transfers between devices: 578 us -> 34.4 us
  other arithmetic: 223 us -> 0.02 us
  local copies, waits for them, and re-layouts: 171 us -> 2.44 us
  blocking collectives: 105 us -> 0 us
  starting transfers between devices: 6.83 us -> 57 us
  between operations: 14.2 us -> 0.9 us
    all_gather x1 -> x0, waiting for transfers between devices: 526 us -> none  [joined(): gathered = jax.tree.map(lambda a: lax.all_gather(a, axis), part)]
    add x33 -> x0, other arithmetic: 168 us -> none  [the longest x31 168 us: merge_parts(): former[2] * jnp.repeat(keep_former.T, per_head, axis=1)]
    dynamic_slice x65 -> x0, local copies, waits for them, and re-layouts: 139 us -> none  [take(): lax.dynamic_index_in_dim(a, source, 0, False)]
    all_gather x2 -> x0, blocking collectives: 105 us -> none  [joined(): gathered = jax.tree.map(lambda a: lax.all_gather(a, axis), part)]
    ppermute x0 -> x18, starting transfers between devices: none -> 57 us  [the longest x11 45.6 us: shifted(): return lax.ppermute(value, 'video', [(v, (v + step) % n) for v in range(n)])]
    all_to_all x1 -> x0, waiting for transfers between devices: 52.1 us -> none  [local(): lax.all_to_all(by_group, 'audio', split_axis=2, concat_axis=1, tiled=True)]
    transpose x62 -> x0, other arithmetic: 50 us -> none  [merge_parts(): blended = former[2] * jnp.repeat(keep_former.T, per_head, axis=1) + latte...]
    ppermute x0 -> x18, waiting for transfers between devices: none -> 34.4 us  [the longest x1 15.4 us: local(): q_out = lax.ppermute(q_out, BOTH, out_pairs)]
  transfers between devices with their start and end apart: 2 -> 18, of which waited for: 2 -> 9; matrix products, arithmetic and copies ran while one was open for 1% -> 0% of each run, Pallas kernels for 0% -> 4%
where the time goes in v1:
time: 104 us; the launch traced here: 102 us
  starting transfers between devices  57 us (55%)
  waiting for transfers between devices  34.4 us (33%)
  Pallas kernels  7.65 us (7%)
  local copies, waits for them, and re-layouts  2.44 us (2%)
    ppermute x11, starting transfers between devices, shifted(): return lax.ppermute(value, 'video', [(v, (v + step) % n) for v in range(n)])  45.6 us
    ppermute x1, waiting for transfers between devices, local(): q_out = lax.ppermute(q_out, BOTH, out_pairs)  15.4 us
    ppermute x11, waiting for transfers between devices, shifted(): return lax.ppermute(value, 'video', [(v, (v + step) % n) for v in range(n)])  6.61 us
    ppermute x1, waiting for transfers between devices, local(): kv_out = lax.ppermute(kv_out, BOTH, out_pairs)  6.14 us
    ppermute x3, waiting for transfers between devices, along_x(): return lax.ppermute(value, 'video', pairs)  5.29 us
    ppermute x1, starting transfers between devices, local(): q_own = lax.ppermute(q_own, BOTH, own_pairs)  5.2 us
    pallas_call x1, Pallas kernels, local(): pl.pallas_call(lambda *refs: video_kernel(scale, *refs), out_shape=jax.Sh...  3.54 us
    ppermute x3, starting transfers between devices, along_x(): return lax.ppermute(value, 'video', pairs)  2.78 us
  transfers between devices with their start and end apart: 18, of which 9 were waited for; matrix products, arithmetic and copies ran while one was open for 0% of the time, Pallas kernels for 4%

profile of v1, /device:TPU:8, one launch (start us, length us, event | category | flops | bytes accessed | tf_op | source)
XLA Modules:
  0.0 102.3 jit_solution(263832742917331500)
XLA Ops:
  0.6 0.0 copy-start
  0.6 2.3 %copy-done = bf16[3,256,3072]{2,1,0:T(8,128)(2,1)S(1)} copy-done((bf16[3,256,3072]{2,1,0:T(8,128)(2,1)S(1)}, bf16[3,256,3072]{2,1,0:T(8,128)(2,1)}, u32[]{:S(2)}) %copy-start) | copy-done | bytes 4718616
  3.0 0.0 copy-start.5
  3.0 0.0 copy-start.1
  3.0 0.0 copy-start.4
  3.0 0.0 copy-start.2
  3.0 0.0 copy-start.3
  3.0 0.2 pack.1
  3.2 5.2 %collective-permute-start.2 = (bf16[256,384]{1,0:T(8,128)(2,1)S(1)}, bf16[256,384]{1,0:T(8,128)(2,1)S(1)}, u32[]{:S(2)}, u32[]{:S(2)}) collective-permute-start(bf16[256,384]{1,0:T(8,128)(2,1)S(1)} %get-tuple-element.13), channel_id=1, source_target_pairs={{0,0},{1,32},{2,64},{3,96},{4,128},{5,160},{6,192},{7,224},{8,8},{... | collective-permute-start | bytes 589832 | tf_op jit(solution)/shard_map/ppermute | solution.py:262
  8.4 1.5 %collective-permute-start.3 = (bf16[128,384]{1,0:T(8,128)(2,1)S(1)}, bf16[128,384]{1,0:T(8,128)(2,1)S(1)}, u32[]{:S(2)}, u32[]{:S(2)}) collective-permute-start(bf16[128,384]{1,0:T(8,128)(2,1)S(1)} %get-tuple-element.14), channel_id=1, source_target_pairs={{0,32},{1,64},{2,96},{3,128},{4,160},{5,192},{6,224},{7,0},{8,40},... | collective-permute-start | bytes 294920 | tf_op jit(solution)/shard_map/ppermute | solution.py:263
  9.8 0.0 copy-done.5
  9.8 0.1 copy.8.refs_1_
  9.9 15.4 %collective-permute-done.3.refs_3_ = bf16[128,384]{1,0:T(8,128)(2,1)S(1)} collective-permute-done((bf16[128,384]{1,0:T(8,128)(2,1)S(1)}, bf16[128,384]{1,0:T(8,128)(2,1)S(1)}, u32[]{:S(2)}, u32[]{:S(2)}) %collective-permute-start.3) | collective-permute-done | bytes 98336 | tf_op jit(solution)/shard_map/ppermute | solution.py:263
  25.3 0.9 collective-permute-done.2.refs_2_
  26.3 0.0 copy-done.1
  26.3 0.0 copy-done.4
  26.3 2.1 %audio_side.1 = (bf16[64,512]{1,0:T(8,128)(2,1)S(1)}, bf16[64,512]{1,0:T(8,128)(2,1)S(1)}, bf16[64,512]{1,0:T(8,128)(2,1)S(1)}, bf16[64,512]{1,0:T(8,128)(2,1)S(1)}, bf16[64,512]{1,0:T(8,128)(2,1)S(1)}) custom-call(s32[2]{0:T(128)S(1)} %copy-done.4, s32[32,2]{1,0:T(8,128)S(1)} %copy.8.refs_1_, bf16[256,384]{1,0:T(8,128)(2,1)S(1)} %collective-permute-done.2.refs_2_, ...), custom_call_target="tpu_custom_call" | custom-call | tf_op jit(solution)/shard_map/audio_side/pallas_call | solution.py:268
  28.4 6.3 %collective-permute-start.4 = (bf16[64,512]{1,0:T(8,128)(2,1)S(1)}, bf16[64,512]{1,0:T(8,128)(2,1)S(1)}, u32[]{:S(2)}, u32[]{:S(2)}) collective-permute-start(bf16[64,512]{1,0:T(8,128)(2,1)S(1)} %get-tuple-element.15), channel_id=1, source_target_pairs={{0,240},{8,248},{16,0},{24,8},{32,16},{40,24},{48,32},{56,40},{64,... | collective-permute-start | bytes 196616 | tf_op jit(solution)/shard_map/ppermute | solution.py:219
  34.6 0.0 collective-permute-start.5
  34.6 2.0 %collective-permute-start.6 = (bf16[64,512]{1,0:T(8,128)(2,1)S(1)}, bf16[64,512]{1,0:T(8,128)(2,1)S(1)}, u32[]{:S(2)}, u32[]{:S(2)}) collective-permute-start(bf16[64,512]{1,0:T(8,128)(2,1)S(1)} %get-tuple-element.18), channel_id=1, source_target_pairs={{0,8},{8,16},{16,24},{24,32},{32,40},{40,48},{48,56},{56,64},{64,7... | collective-permute-start | bytes 196616 | tf_op jit(solution)/shard_map/ppermute | solution.py:219
  36.6 0.6 collective-permute-start.7
  37.3 1.9 %collective-permute-start = (bf16[2,256,384]{2,1,0:T(8,128)(2,1)S(1)}, bf16[2,256,384]{2,1,0:T(8,128)(2,1)S(1)}, u32[]{:S(2)}, u32[]{:S(2)}) collective-permute-start(bf16[2,256,384]{2,1,0:T(8,128)(2,1)S(1)} %get-tuple-element.11), channel_id=1, source_target_pairs={{0,0},{1,32},{2,64},{3,96},{4,128},{5,160},{6,192},{7,224},{8,8},{... | collective-permute-start | bytes 1179656 | tf_op jit(solution)/shard_map/ppermute | solution.py:264
  39.2 0.0 collective-permute-done.4.refs_0_
  39.2 0.0 collective-permute-done.5.refs_1_
  39.2 3.0 %collective-permute-done.6.refs_3_ = bf16[64,512]{1,0:T(8,128)(2,1)S(1)} collective-permute-done((bf16[64,512]{1,0:T(8,128)(2,1)S(1)}, bf16[64,512]{1,0:T(8,128)(2,1)S(1)}, u32[]{:S(2)}, u32[]{:S(2)}) %collective-permute-start.6) | collective-permute-done | bytes 65568 | tf_op jit(solution)/shard_map/ppermute | solution.py:219
  42.2 2.3 %collective-permute-done.7.refs_4_ = bf16[64,512]{1,0:T(8,128)(2,1)S(1)} collective-permute-done((bf16[64,512]{1,0:T(8,128)(2,1)S(1)}, bf16[64,512]{1,0:T(8,128)(2,1)S(1)}, u32[]{:S(2)}, u32[]{:S(2)}) %collective-permute-start.7) | collective-permute-done | bytes 65568 | tf_op jit(solution)/shard_map/ppermute | solution.py:219
  44.5 0.4 merge.1
  45.0 0.1 collective-permute-start.10
  45.0 2.7 %collective-permute-start.9 = (bf16[64,384]{1,0:T(8,128)(2,1)S(1)}, bf16[64,384]{1,0:T(8,128)(2,1)S(1)}, u32[]{:S(2)}, u32[]{:S(2)}) collective-permute-start(bf16[64,384]{1,0:T(8,128)(2,1)S(1)} %merge.1), channel_id=1, source_target_pairs={{0,16},{8,24},{16,0},{24,8},{32,48},{40,56},{48,32},{56,40},{64,80... | collective-permute-start | bytes 147464 | tf_op jit(solution)/shard_map/ppermute | solution.py:224
  47.7 0.0 collective-permute-start.8
  47.7 0.0 collective-permute-start.1
  47.7 1.4 %collective-permute-done.10 = bf16[64,384]{1,0:T(8,128)(2,1)S(1)} collective-permute-done((bf16[64,384]{1,0:T(8,128)(2,1)S(1)}, bf16[64,384]{1,0:T(8,128)(2,1)S(1)}, u32[]{:S(2)}, u32[]{:S(2)}) %collective-permute-start.10) | collective-permute-done | bytes 49184 | tf_op jit(solution)/shard_map/ppermute | solution.py:224
  49.1 1.6 %collective-permute-done.9 = bf16[64,384]{1,0:T(8,128)(2,1)S(1)} collective-permute-done((bf16[64,384]{1,0:T(8,128)(2,1)S(1)}, bf16[64,384]{1,0:T(8,128)(2,1)S(1)}, u32[]{:S(2)}, u32[]{:S(2)}) %collective-permute-start.9) | collective-permute-done | bytes 49184 | tf_op jit(solution)/shard_map/ppermute | solution.py:224
  50.7 2.3 %collective-permute-done.8 = bf16[64,384]{1,0:T(8,128)(2,1)S(1)} collective-permute-done((bf16[64,384]{1,0:T(8,128)(2,1)S(1)}, bf16[64,384]{1,0:T(8,128)(2,1)S(1)}, u32[]{:S(2)}, u32[]{:S(2)}) %collective-permute-start.8) | collective-permute-done | bytes 49184 | tf_op jit(solution)/shard_map/ppermute | solution.py:224
  53.1 3.1 %collective-permute-start.11 = (bf16[256,384]{1,0:T(8,128)(2,1)S(1)}, bf16[256,384]{1,0:T(8,128)(2,1)S(1)}, u32[]{:S(2)}, u32[]{:S(2)}) collective-permute-start(bf16[256,384]{1,0:T(8,128)(2,1)S(1)} %pad_maximum_fusion.refs_0_), channel_id=1, source_target_pairs={{0,160},{8,168},{16,176},{24,184},{32,192},{40,200},{48,208},{56,2... | collective-permute-start | bytes 589832 | tf_op jit(solution)/shard_map/ppermute | solution.py:219
  56.1 1.7 %collective-permute-start.12 = (bf16[256,384]{1,0:T(8,128)(2,1)S(1)}, bf16[256,384]{1,0:T(8,128)(2,1)S(1)}, u32[]{:S(2)}, u32[]{:S(2)}) collective-permute-start(bf16[256,384]{1,0:T(8,128)(2,1)S(1)} %pad_maximum_fusion.refs_0_), channel_id=1, source_target_pairs={{0,64},{8,72},{16,80},{24,88},{32,96},{40,104},{48,112},{56,120},{... | collective-permute-start | bytes 589832 | tf_op jit(solution)/shard_map/ppermute | solution.py:219
  57.8 4.9 %collective-permute-start.13 = (bf16[256,384]{1,0:T(8,128)(2,1)S(1)}, bf16[256,384]{1,0:T(8,128)(2,1)S(1)}, u32[]{:S(2)}, u32[]{:S(2)}) collective-permute-start(bf16[256,384]{1,0:T(8,128)(2,1)S(1)} %pad_maximum_fusion.refs_0_), channel_id=1, source_target_pairs={{0,224},{8,232},{16,240},{24,248},{32,0},{40,8},{48,16},{56,24},{6... | collective-permute-start | bytes 589832 | tf_op jit(solution)/shard_map/ppermute | solution.py:219
  62.7 6.1 %collective-permute-done.1.refs_4_ = bf16[2,128,384]{2,1,0:T(8,128)(2,1)S(1)} collective-permute-done((bf16[2,128,384]{2,1,0:T(8,128)(2,1)S(1)}, bf16[2,128,384]{2,1,0:T(8,128)(2,1)S(1)}, u32[]{:S(2)}, u32[]{:S(2)}) %collective-permute-start.1) | collective-permute-done | bytes 196640 | tf_op jit(solution)/shard_map/ppermute | solution.py:265
  68.9 16.0 %collective-permute-start.14 = (bf16[256,384]{1,0:T(8,128)(2,1)S(1)}, bf16[256,384]{1,0:T(8,128)(2,1)S(1)}, u32[]{:S(2)}, u32[]{:S(2)}) collective-permute-start(bf16[256,384]{1,0:T(8,128)(2,1)S(1)} %pad_maximum_fusion.refs_0_), channel_id=1, source_target_pairs={{0,32},{8,40},{16,48},{24,56},{32,64},{40,72},{48,80},{56,88},{64,... | collective-permute-start | bytes 589832 | tf_op jit(solution)/shard_map/ppermute | solution.py:219
  84.8 0.0 collective-permute-done.11.refs_1_
  84.8 0.0 collective-permute-start.15
  84.8 0.0 collective-permute-done.refs_3_
  84.9 9.0 %collective-permute-start.16 = (bf16[256,384]{1,0:T(8,128)(2,1)S(1)}, bf16[256,384]{1,0:T(8,128)(2,1)S(1)}, u32[]{:S(2)}, u32[]{:S(2)}) collective-permute-start(bf16[256,384]{1,0:T(8,128)(2,1)S(1)} %collective-permute-done.11.refs_1_), channel_id=1, source_target_pairs={{0,32},{8,40},{16,48},{24,56},{32,64},{40,72},{48,80},{56,88},{64,... | collective-permute-start | bytes 589832 | tf_op jit(solution)/shard_map/ppermute | solution.py:219
  93.9 0.0 collective-permute-done.12.refs_2_
  93.9 2.0 %collective-permute-start.17 = (bf16[256,384]{1,0:T(8,128)(2,1)S(1)}, bf16[256,384]{1,0:T(8,128)(2,1)S(1)}, u32[]{:S(2)}, u32[]{:S(2)}) collective-permute-start(bf16[256,384]{1,0:T(8,128)(2,1)S(1)} %collective-permute-done.12.refs_2_), channel_id=1, source_target_pairs={{0,32},{8,40},{16,48},{24,56},{32,64},{40,72},{48,80},{56,88},{64,... | collective-permute-start | bytes 589832 | tf_op jit(solution)/shard_map/ppermute | solution.py:219
  95.9 0.0 copy-done.2
  95.9 0.0 copy-done.3
  95.9 3.5 %video_side.1 = bf16[512,384]{1,0:T(8,128)(2,1)} custom-call(s32[32]{0:T(128)S(1)} %copy-done.3, s32[32,2]{1,0:T(8,128)S(1)} %copy.8.refs_1_, bf16[512,384]{1,0:T(8,128)(2,1)S(1)} %copy-done.2, bf16[2,256,384]{2,1,0:T(8,128)(2,1)S(1)} %collective-permute-done.refs_3_, bf16[2,128,384]{2,1,0:T(8,128)(2,1)S(1)} %collective-permute-done.1.refs_4_), custom_call_target="tpu_custom_call" | custom-call | tf_op jit(solution)/shard_map/video_side/pallas_call | solution.py:292
  99.5 0.0 collective-permute-done.13.refs_3_
  99.5 0.0 collective-permute-done.14.refs_4_
  99.5 0.0 collective-permute-done.15.refs_5_
  99.5 0.0 collective-permute-done.16.refs_6_
  99.5 1.3 %collective-permute-done.17.refs_7_ = bf16[256,384]{1,0:T(8,128)(2,1)S(1)} collective-permute-done((bf16[256,384]{1,0:T(8,128)(2,1)S(1)}, bf16[256,384]{1,0:T(8,128)(2,1)S(1)}, u32[]{:S(2)}, u32[]{:S(2)}) %collective-permute-start.17) | collective-permute-done | bytes 196640 | tf_op jit(solution)/shard_map/ppermute | solution.py:219
  100.8 1.4 %assemble.1 = bf16[2048,384]{1,0:T(8,128)(2,1)} custom-call(bf16[256,384]{1,0:T(8,128)(2,1)S(1)} %pad_maximum_fusion.refs_0_, bf16[256,384]{1,0:T(8,128)(2,1)S(1)} %collective-permute-done.11.refs_1_, bf16[256,384]{1,0:T(8,128)(2,1)S(1)} %collective-permute-done.12.refs_2_, bf16[256,384]{1,0:T(8,128)(2,1)S(1)} %collective-permute-done.13.refs_3_, ...), custom_call_target="tpu_custom_call" | custom-call | tf_op jit(solution)/shard_map/assemble/pallas_call | solution.py:306
  (1 shorter events, 0.0 us)
Async XLA Ops:
  0.6 2.3 %copy-start = (bf16[3,256,3072]{2,1,0:T(8,128)(2,1)S(1)}, bf16[3,256,3072]{2,1,0:T(8,128)(2,1)}, u32[]{:S(2)}) copy-start(bf16[3,256,3072]{2,1,0:T(8,128)(2,1)} %src.1) | copy-start | bytes 14155780
  3.0 6.9 %copy-start.5 = (s32[32,2]{0,1:T(2,128)S(1)}, s32[32,2]{0,1:T(2,128)}, u32[]{:S(2)}) copy-start(s32[32,2]{0,1:T(2,128)} %param.11) | copy-start | bytes 772
  3.0 23.3 %copy-start.1 = (bf16[2,512,384]{2,1,0:T(8,128)(2,1)S(1)}, bf16[2,512,384]{2,1,0:T(8,128)(2,1)}, u32[]{:S(2)}) copy-start(bf16[2,512,384]{2,1,0:T(8,128)(2,1)} %refs_4_.1) | copy-start | bytes 2359300
  3.0 23.3 %copy-start.4 = (s32[2]{0:T(128)S(1)}, s32[2]{0:T(128)}, u32[]{:S(2)}) copy-start(s32[2]{0:T(128)} %refs_0_.3) | copy-start | bytes 28
  3.0 92.9 %copy-start.2 = (bf16[512,384]{1,0:T(8,128)(2,1)S(1)}, bf16[512,384]{1,0:T(8,128)(2,1)}, u32[]{:S(2)}) copy-start(bf16[512,384]{1,0:T(8,128)(2,1)} %refs_2_.1) | copy-start | bytes 1179652
  3.0 92.9 %copy-start.3 = (s32[32]{0:T(128)S(1)}, s32[32]{0:T(128)}, u32[]{:S(2)}) copy-start(s32[32]{0:T(128)} %refs_0_.2) | copy-start | bytes 388
  3.2 23.1 %collective-permute-start.2 = (bf16[256,384]{1,0:T(8,128)(2,1)S(1)}, bf16[256,384]{1,0:T(8,128)(2,1)S(1)}, u32[]{:S(2)}, u32[]{:S(2)}) collective-permute-start(bf16[256,384]{1,0:T(8,128)(2,1)S(1)} %get-tuple-element.13), channel_id=1, source_target_pairs={{0,0},{1,32},{2,64},{3,96},{4,128},{5,160},{6,192},{7,224},{8,8},{... | collective-permute-start | bytes 589832 | tf_op jit(solution)/shard_map/ppermute | solution.py:262
  8.4 16.9 %collective-permute-start.3 = (bf16[128,384]{1,0:T(8,128)(2,1)S(1)}, bf16[128,384]{1,0:T(8,128)(2,1)S(1)}, u32[]{:S(2)}, u32[]{:S(2)}) collective-permute-start(bf16[128,384]{1,0:T(8,128)(2,1)S(1)} %get-tuple-element.14), channel_id=1, source_target_pairs={{0,32},{1,64},{2,96},{3,128},{4,160},{5,192},{6,224},{7,0},{8,40},... | collective-permute-start | bytes 294920 | tf_op jit(solution)/shard_map/ppermute | solution.py:263
  28.4 10.9 %collective-permute-start.4 = (bf16[64,512]{1,0:T(8,128)(2,1)S(1)}, bf16[64,512]{1,0:T(8,128)(2,1)S(1)}, u32[]{:S(2)}, u32[]{:S(2)}) collective-permute-start(bf16[64,512]{1,0:T(8,128)(2,1)S(1)} %get-tuple-element.15), channel_id=1, source_target_pairs={{0,240},{8,248},{16,0},{24,8},{32,16},{40,24},{48,32},{56,40},{64,... | collective-permute-start | bytes 196616 | tf_op jit(solution)/shard_map/ppermute | solution.py:219
  34.6 4.6 %collective-permute-start.5 = (bf16[64,512]{1,0:T(8,128)(2,1)S(1)}, bf16[64,512]{1,0:T(8,128)(2,1)S(1)}, u32[]{:S(2)}, u32[]{:S(2)}) collective-permute-start(bf16[64,512]{1,0:T(8,128)(2,1)S(1)} %get-tuple-element.16), channel_id=1, source_target_pairs={{0,248},{8,0},{16,8},{24,16},{32,24},{40,32},{48,40},{56,48},{64,5... | collective-permute-start | bytes 196616 | tf_op jit(solution)/shard_map/ppermute | solution.py:219
  34.6 7.6 %collective-permute-start.6 = (bf16[64,512]{1,0:T(8,128)(2,1)S(1)}, bf16[64,512]{1,0:T(8,128)(2,1)S(1)}, u32[]{:S(2)}, u32[]{:S(2)}) collective-permute-start(bf16[64,512]{1,0:T(8,128)(2,1)S(1)} %get-tuple-element.18), channel_id=1, source_target_pairs={{0,8},{8,16},{16,24},{24,32},{32,40},{40,48},{48,56},{56,64},{64,7... | collective-permute-start | bytes 196616 | tf_op jit(solution)/shard_map/ppermute | solution.py:219
  36.6 7.9 %collective-permute-start.7 = (bf16[64,512]{1,0:T(8,128)(2,1)S(1)}, bf16[64,512]{1,0:T(8,128)(2,1)S(1)}, u32[]{:S(2)}, u32[]{:S(2)}) collective-permute-start(bf16[64,512]{1,0:T(8,128)(2,1)S(1)} %get-tuple-element.19), channel_id=1, source_target_pairs={{0,16},{8,24},{16,32},{24,40},{32,48},{40,56},{48,64},{56,72},{64,... | collective-permute-start | bytes 196616 | tf_op jit(solution)/shard_map/ppermute | solution.py:219
  37.3 47.6 %collective-permute-start = (bf16[2,256,384]{2,1,0:T(8,128)(2,1)S(1)}, bf16[2,256,384]{2,1,0:T(8,128)(2,1)S(1)}, u32[]{:S(2)}, u32[]{:S(2)}) collective-permute-start(bf16[2,256,384]{2,1,0:T(8,128)(2,1)S(1)} %get-tuple-element.11), channel_id=1, source_target_pairs={{0,0},{1,32},{2,64},{3,96},{4,128},{5,160},{6,192},{7,224},{8,8},{... | collective-permute-start | bytes 1179656 | tf_op jit(solution)/shard_map/ppermute | solution.py:264
  45.0 4.2 %collective-permute-start.10 = (bf16[64,384]{1,0:T(8,128)(2,1)S(1)}, bf16[64,384]{1,0:T(8,128)(2,1)S(1)}, u32[]{:S(2)}, u32[]{:S(2)}) collective-permute-start(bf16[64,384]{1,0:T(8,128)(2,1)S(1)} %merge.1), channel_id=1, source_target_pairs={{0,24},{8,0},{16,8},{24,16},{32,56},{40,32},{48,40},{56,48},{64,88... | collective-permute-start | bytes 147464 | tf_op jit(solution)/shard_map/ppermute | solution.py:224
  45.0 5.7 %collective-permute-start.9 = (bf16[64,384]{1,0:T(8,128)(2,1)S(1)}, bf16[64,384]{1,0:T(8,128)(2,1)S(1)}, u32[]{:S(2)}, u32[]{:S(2)}) collective-permute-start(bf16[64,384]{1,0:T(8,128)(2,1)S(1)} %merge.1), channel_id=1, source_target_pairs={{0,16},{8,24},{16,0},{24,8},{32,48},{40,56},{48,32},{56,40},{64,80... | collective-permute-start | bytes 147464 | tf_op jit(solution)/shard_map/ppermute | solution.py:224
  47.7 5.3 %collective-permute-start.8 = (bf16[64,384]{1,0:T(8,128)(2,1)S(1)}, bf16[64,384]{1,0:T(8,128)(2,1)S(1)}, u32[]{:S(2)}, u32[]{:S(2)}) collective-permute-start(bf16[64,384]{1,0:T(8,128)(2,1)S(1)} %merge.1), channel_id=1, source_target_pairs={{0,8},{8,16},{16,24},{24,0},{32,40},{40,48},{48,56},{56,32},{64,72... | collective-permute-start | bytes 147464 | tf_op jit(solution)/shard_map/ppermute | solution.py:224
  47.7 21.1 %collective-permute-start.1 = (bf16[2,128,384]{2,1,0:T(8,128)(2,1)S(1)}, bf16[2,128,384]{2,1,0:T(8,128)(2,1)S(1)}, u32[]{:S(2)}, u32[]{:S(2)}) collective-permute-start(bf16[2,128,384]{2,1,0:T(8,128)(2,1)S(1)} %get-tuple-element.12), channel_id=1, source_target_pairs={{0,32},{1,64},{2,96},{3,128},{4,160},{5,192},{6,224},{7,0},{8,40},... | collective-permute-start | bytes 589832 | tf_op jit(solution)/shard_map/ppermute | solution.py:265
  53.1 31.8 %collective-permute-start.11 = (bf16[256,384]{1,0:T(8,128)(2,1)S(1)}, bf16[256,384]{1,0:T(8,128)(2,1)S(1)}, u32[]{:S(2)}, u32[]{:S(2)}) collective-permute-start(bf16[256,384]{1,0:T(8,128)(2,1)S(1)} %pad_maximum_fusion.refs_0_), channel_id=1, source_target_pairs={{0,160},{8,168},{16,176},{24,184},{32,192},{40,200},{48,208},{56,2... | collective-permute-start | bytes 589832 | tf_op jit(solution)/shard_map/ppermute | solution.py:219
  56.1 37.8 %collective-permute-start.12 = (bf16[256,384]{1,0:T(8,128)(2,1)S(1)}, bf16[256,384]{1,0:T(8,128)(2,1)S(1)}, u32[]{:S(2)}, u32[]{:S(2)}) collective-permute-start(bf16[256,384]{1,0:T(8,128)(2,1)S(1)} %pad_maximum_fusion.refs_0_), channel_id=1, source_target_pairs={{0,64},{8,72},{16,80},{24,88},{32,96},{40,104},{48,112},{56,120},{... | collective-permute-start | bytes 589832 | tf_op jit(solution)/shard_map/ppermute | solution.py:219
  57.8 41.6 %collective-permute-start.13 = (bf16[256,384]{1,0:T(8,128)(2,1)S(1)}, bf16[256,384]{1,0:T(8,128)(2,1)S(1)}, u32[]{:S(2)}, u32[]{:S(2)}) collective-permute-start(bf16[256,384]{1,0:T(8,128)(2,1)S(1)} %pad_maximum_fusion.refs_0_), channel_id=1, source_target_pairs={{0,224},{8,232},{16,240},{24,248},{32,0},{40,8},{48,16},{56,24},{6... | collective-permute-start | bytes 589832 | tf_op jit(solution)/shard_map/ppermute | solution.py:219
  68.9 30.6 %collective-permute-start.14 = (bf16[256,384]{1,0:T(8,128)(2,1)S(1)}, bf16[256,384]{1,0:T(8,128)(2,1)S(1)}, u32[]{:S(2)}, u32[]{:S(2)}) collective-permute-start(bf16[256,384]{1,0:T(8,128)(2,1)S(1)} %pad_maximum_fusion.refs_0_), channel_id=1, source_target_pairs={{0,32},{8,40},{16,48},{24,56},{32,64},{40,72},{48,80},{56,88},{64,... | collective-permute-start | bytes 589832 | tf_op jit(solution)/shard_map/ppermute | solution.py:219
  84.8 14.6 %collective-permute-start.15 = (bf16[256,384]{1,0:T(8,128)(2,1)S(1)}, bf16[256,384]{1,0:T(8,128)(2,1)S(1)}, u32[]{:S(2)}, u32[]{:S(2)}) collective-permute-start(bf16[256,384]{1,0:T(8,128)(2,1)S(1)} %collective-permute-done.11.refs_1_), channel_id=1, source_target_pairs={{0,224},{8,232},{16,240},{24,248},{32,0},{40,8},{48,16},{56,24},{6... | collective-permute-start | bytes 589832 | tf_op jit(solution)/shard_map/ppermute | solution.py:219
  84.9 14.6 %collective-permute-start.16 = (bf16[256,384]{1,0:T(8,128)(2,1)S(1)}, bf16[256,384]{1,0:T(8,128)(2,1)S(1)}, u32[]{:S(2)}, u32[]{:S(2)}) collective-permute-start(bf16[256,384]{1,0:T(8,128)(2,1)S(1)} %collective-permute-done.11.refs_1_), channel_id=1, source_target_pairs={{0,32},{8,40},{16,48},{24,56},{32,64},{40,72},{48,80},{56,88},{64,... | collective-permute-start | bytes 589832 | tf_op jit(solution)/shard_map/ppermute | solution.py:219
  93.9 6.9 %collective-permute-start.17 = (bf16[256,384]{1,0:T(8,128)(2,1)S(1)}, bf16[256,384]{1,0:T(8,128)(2,1)S(1)}, u32[]{:S(2)}, u32[]{:S(2)}) collective-permute-start(bf16[256,384]{1,0:T(8,128)(2,1)S(1)} %collective-permute-done.12.refs_2_), channel_id=1, source_target_pairs={{0,32},{8,40},{16,48},{24,56},{32,64},{40,72},{48,80},{56,88},{64,... | collective-permute-start | bytes 589832 | tf_op jit(solution)/shard_map/ppermute | solution.py:219

commit v2 on v1

--- a/solution.py
+++ b/solution.py
@@ -31,18 +31,29 @@
     return v, v // XS, v % XS
 
 
-def pack_kernel(src, q_own, q_out, kv_own, kv_out, sems):
-    _, z, x = place()
-    columns = q_own.shape[1]
-    cols = pl.ds(pl.multiple_of(z * columns, 128), columns)
-    half = q_out.shape[0]
-    rows = pl.ds(pl.multiple_of(jnp.where(x < REACH, half, 0), half), half)
-    copies = [
-        pltpu.make_async_copy(src.at[0, :, cols], q_own, sems.at[0]),
-        pltpu.make_async_copy(src.at[0, rows, cols], q_out, sems.at[1]),
-        pltpu.make_async_copy(src.at[pl.ds(1, 2), :, cols], kv_own, sems.at[2]),
-        pltpu.make_async_copy(src.at[pl.ds(1, 2), rows, cols], kv_out, sems.at[3]),
-    ]
+def sender_row(z, shard):
+    ahead = lax.rem(z - shard + ZS, ZS)
+    turn = jnp.where(ahead == 0, 2, jnp.where(ahead == 1, 1, jnp.where(ahead == ZS - 1, 3, 0)))
+    return lax.rem(shard // 2 + turn, 4)
+
+
+def line_of_sender(z, turn):
+    return z + (2 if z % 2 else -2, 1, 0, -1)[turn]
+
+
+def pack_kernel(first_part, parts, src, out0, out1, sems):
+    _, z, _ = place()
+    columns = out0.shape[-1]
+    first = sender_row(z, lax.axis_index("audio")) * 2 * columns
+    copies = []
+    for core, out in enumerate((out0, out1)):
+        cols = pl.ds(pl.multiple_of(first + core * columns, 128), columns)
+        for i in range(parts):
+            copies.append(
+                pltpu.make_async_copy(
+                    src.at[first_part + i, :, cols], out.at[i], sems.at[core * parts + i]
+                )
+            )
     for c in copies:
         c.start()
     for c in copies:
@@ -240,29 +251,41 @@
     def flat(z, x, a):
         return ((z % ZS) * XS + x) * audio_devices + a
 
-    q_own, q_out, kv_own, kv_out = pl.pallas_call(
-        pack_kernel,
-        out_shape=(
-            jax.ShapeDtypeStruct((shard_rows, columns), bf16),
-            jax.ShapeDtypeStruct((half, columns), bf16),
-            jax.ShapeDtypeStruct((2, shard_rows, columns), bf16),
-            jax.ShapeDtypeStruct((2, half, columns), bf16),
-        ),
-        in_specs=[ANY],
-        out_specs=(VMEM,) * 4,
-        scratch_shapes=[pltpu.SemaphoreType.DMA((4,))],
-        compiler_params=params(),
-        name="pack",
-    )(audio_qkv)
-    every = [(z, x, a) for z in range(ZS) for x in range(XS) for a in range(audio_devices)]
-    own_pairs = [(flat(z, x, a), flat(a, x, z)) for z, x, a in every]
-    out_pairs = [
-        (flat(z, x, a), flat(a + 1 if x < REACH else a - 1, x, z)) for z, x, a in every
-    ]
-    q_own = lax.ppermute(q_own, BOTH, own_pairs)
-    q_out = lax.ppermute(q_out, BOTH, out_pairs)
-    kv_own = lax.ppermute(kv_own, BOTH, own_pairs)
-    kv_out = lax.ppermute(kv_out, BOTH, out_pairs)
+    def packed_slices(first_part, parts, value, name):
+        return pl.pallas_call(
+            lambda *refs: pack_kernel(first_part, parts, *refs),
+            out_shape=(jax.ShapeDtypeStruct((parts, shard_rows, columns), bf16),) * 2,
+            in_specs=[ANY],
+            out_specs=(VMEM,) * 2,
+            scratch_shapes=[pltpu.SemaphoreType.DMA((2 * parts,))],
+            compiler_params=pltpu.CompilerParams(vmem_limit_bytes=60 * 1024 * 1024),
+            name=name,
+        )(value)
+
+    q0, q1 = packed_slices(0, 1, audio_qkv, "pack_queries")
+    q0, q1, later = lax.optimization_barrier((q0, q1, audio_qkv))
+    kv0, kv1 = packed_slices(1, 2, later, "pack_keys")
+    x = lax.axis_index("video") % XS
+    edge = jnp.where(x < REACH, half, 0)
+
+    def to_core(value, core):
+        pairs = []
+        for z in range(ZS):
+            for xx in range(XS):
+                for y in range(audio_devices // 2):
+                    sender = line_of_sender(z, (y - z // 2) % 4)
+                    pairs.append((flat(sender, xx, z), flat(z, xx, 2 * y + core)))
+        return lax.ppermute(value, BOTH, pairs)
+
+    def from_next_line(value):
+        n = ZS * XS
+        pairs = [(v, (v + XS if v % XS < REACH else v - XS) % n) for v in range(n)]
+        return lax.ppermute(value, "video", pairs)
+
+    q_own = (to_core(q0, 0) + to_core(q1, 1))[0]
+    q_out = from_next_line(lax.dynamic_slice_in_dim(q_own, edge, half, 0))
+    kv0, kv1, q_own = lax.optimization_barrier((kv0, kv1, q_own))
+    kv0, kv1 = to_core(kv0, 0), to_core(kv1, 1)
 
     packed = jax.ShapeDtypeStruct((ABS, columns + 128), bf16)
     parts = pl.pallas_call(
@@ -289,6 +312,10 @@
         name="merge",
     )(*held)
 
+    row = jnp.concatenate([block_out] + [along_x(block_out, k) for k in range(1, XS)], axis=0)
+    kv0, kv1, row = lax.optimization_barrier((kv0, kv1, row))
+    kv_own = kv0 + kv1
+    kv_out = from_next_line(lax.dynamic_slice_in_dim(kv_own, edge, half, 1))
     video_out = pl.pallas_call(
         lambda *refs: video_kernel(scale, *refs),
         out_shape=jax.ShapeDtypeStruct((seg_rows, columns), bf16),
@@ -299,7 +326,6 @@
         name="video_side",
     )(audio_count, video_range, video_query, kv_own, kv_out)
 
-    row = jnp.concatenate([block_out] + [along_x(block_out, k) for k in range(1, XS)], axis=0)
     z3, zm2 = from_z(row, 3), from_z(row, -2)
     z1, zm1 = from_z(row, 1), from_z(row, -1)
     z4, z2, zm3 = from_z(z3, 1), from_z(z3, -1), from_z(zm2, -1)

time: 104 us -> 88.6 us (0.85)
  the two profiles are of different devices: /device:TPU:8 before, /device:TPU:109 now
where the time goes in v2:
time: 88.6 us; the launch traced here: 88.4 us
  waiting for transfers between devices  40.5 us (46%)
  starting transfers between devices  35 us (40%)
  Pallas kernels  11.5 us (13%)
  between operations  1.01 us (1%)
    ppermute x11, waiting for transfers between devices, shifted(): return lax.ppermute(value, 'video', [(v, (v + step) % n) for v in range(n)])  25.7 us
    ppermute x11, starting transfers between devices, shifted(): return lax.ppermute(value, 'video', [(v, (v + step) % n) for v in range(n)])  18.1 us
    ppermute x4, starting transfers between devices, to_core(): return lax.ppermute(value, BOTH, pairs)  11.9 us
    ppermute x4, waiting for transfers between devices, to_core(): return lax.ppermute(value, BOTH, pairs)  6.89 us
    ppermute x2, waiting for transfers between devices, from_next_line(): return lax.ppermute(value, 'video', pairs)  5.02 us
    pallas_call x2, Pallas kernels, packed_slices(): pl.pallas_call(lambda *refs: pack_kernel(first_part, parts, *refs), out_s...  4.04 us
    pallas_call x1, Pallas kernels, local(): pl.pallas_call(lambda *refs: video_kernel(scale, *refs), out_shape=jax.Sh...  3.55 us
    ppermute x3, starting transfers between devices, along_x(): return lax.ppermute(value, 'video', pairs)  3.35 us
  transfers between devices with their start and end apart: 20, of which 10 were waited for; matrix products, arithmetic and copies ran while one was open for 0% of the time, Pallas kernels for 9%

profile of v2, /device:TPU:109, one launch (start us, length us, event | category | flops | bytes accessed | tf_op | source)
XLA Modules:
  0.0 88.4 jit_solution(1315546605486055125)
XLA Ops:
  0.6 0.0 copy-start.4
  0.6 0.0 copy-start.3
  0.7 0.0 copy-start
  0.7 1.9 %pack_queries.1 = (bf16[1,256,384]{2,1,0:T(8,128)(2,1)}, bf16[1,256,384]{2,1,0:T(8,128)(2,1)}) custom-call(bf16[3,256,3072]{2,1,0:T(8,128)(2,1)} %refs_0_.4), custom_call_target="tpu_custom_call" | custom-call | tf_op jit(solution)/shard_map/pack_queries/pallas_call | solution.py:255
  2.5 0.0 copy-start.1
  2.6 0.0 copy-start.2
  2.6 4.6 %collective-permute-start = (bf16[1,256,384]{2,1,0:T(8,128)(2,1)}, bf16[1,256,384]{2,1,0:T(8,128)(2,1)S(1)}, u32[]{:S(2)}, u32[]{:S(2)}) collective-permute-start(bf16[1,256,384]{2,1,0:T(8,128)(2,1)} %get-tuple-element.25), channel_id=1, source_target_pairs={{192,0},{32,2},{0,4},{224,6},{200,8},{40,10},{8,12},{232,14},{208,... | collective-permute-start | bytes 589832 | tf_op jit(solution)/shard_map/ppermute | solution.py:278
  7.2 1.9 %collective-permute-start.1 = (bf16[1,256,384]{2,1,0:T(8,128)(2,1)}, bf16[1,256,384]{2,1,0:T(8,128)(2,1)S(1)}, u32[]{:S(2)}, u32[]{:S(2)}) collective-permute-start(bf16[1,256,384]{2,1,0:T(8,128)(2,1)} %get-tuple-element.26), channel_id=1, source_target_pairs={{192,1},{32,3},{0,5},{224,7},{200,9},{40,11},{8,13},{232,15},{208,... | collective-permute-start | bytes 589832 | tf_op jit(solution)/shard_map/ppermute | solution.py:278
  9.1 4.2 %collective-permute-done = bf16[1,256,384]{2,1,0:T(8,128)(2,1)S(1)} collective-permute-done((bf16[1,256,384]{2,1,0:T(8,128)(2,1)}, bf16[1,256,384]{2,1,0:T(8,128)(2,1)S(1)}, u32[]{:S(2)}, u32[]{:S(2)}) %collective-permute-start) | collective-permute-done | bytes 196640 | tf_op jit(solution)/shard_map/ppermute | solution.py:278
  13.4 2.7 %collective-permute-done.1 = bf16[1,256,384]{2,1,0:T(8,128)(2,1)S(1)} collective-permute-done((bf16[1,256,384]{2,1,0:T(8,128)(2,1)}, bf16[1,256,384]{2,1,0:T(8,128)(2,1)S(1)}, u32[]{:S(2)}, u32[]{:S(2)}) %collective-permute-start.1) | collective-permute-done | bytes 196640 | tf_op jit(solution)/shard_map/ppermute | solution.py:278
  16.0 0.1 add.12
  16.1 0.1 collective-permute-start.4
  16.2 2.2 %pack_keys.1 = (bf16[2,256,384]{2,1,0:T(8,128)(2,1)}, bf16[2,256,384]{2,1,0:T(8,128)(2,1)}) custom-call(bf16[3,256,3072]{2,1,0:T(8,128)(2,1)} %refs_0_.4), custom_call_target="tpu_custom_call" | custom-call | tf_op jit(solution)/shard_map/pack_keys/pallas_call | solution.py:255
  18.4 3.1 %collective-permute-start.2 = (bf16[2,256,384]{2,1,0:T(8,128)(2,1)}, bf16[2,256,384]{2,1,0:T(8,128)(2,1)S(1)}, u32[]{:S(2)}, u32[]{:S(2)}) collective-permute-start(bf16[2,256,384]{2,1,0:T(8,128)(2,1)} %get-tuple-element.27), channel_id=1, source_target_pairs={{192,0},{32,2},{0,4},{224,6},{200,8},{40,10},{8,12},{232,14},{208,... | collective-permute-start | bytes 1179656 | tf_op jit(solution)/shard_map/ppermute | solution.py:278
  21.5 2.2 %collective-permute-start.3 = (bf16[2,256,384]{2,1,0:T(8,128)(2,1)}, bf16[2,256,384]{2,1,0:T(8,128)(2,1)S(1)}, u32[]{:S(2)}, u32[]{:S(2)}) collective-permute-start(bf16[2,256,384]{2,1,0:T(8,128)(2,1)} %get-tuple-element.28), channel_id=1, source_target_pairs={{192,1},{32,3},{0,5},{224,7},{200,9},{40,11},{8,13},{232,15},{208,... | collective-permute-start | bytes 1179656 | tf_op jit(solution)/shard_map/ppermute | solution.py:278
  23.7 0.0 copy-done.4
  23.7 0.1 copy.9.refs_1_
  23.8 0.1 collective-permute-done.4.refs_3_
  23.9 0.0 copy-done.3
  23.9 0.0 copy-done
  23.9 2.1 %audio_side.1 = (bf16[64,512]{1,0:T(8,128)(2,1)S(1)}, bf16[64,512]{1,0:T(8,128)(2,1)S(1)}, bf16[64,512]{1,0:T(8,128)(2,1)S(1)}, bf16[64,512]{1,0:T(8,128)(2,1)S(1)}, bf16[64,512]{1,0:T(8,128)(2,1)S(1)}) custom-call(s32[2]{0:T(128)S(1)} %copy-done.3, s32[32,2]{1,0:T(8,128)S(1)} %copy.9.refs_1_, bf16[256,384]{1,0:T(8,128)(2,1)S(1)} %bitcast.3, ...), custom_call_target="tpu_custom_call" | custom-call | tf_op jit(solution)/shard_map/audio_side/pallas_call | solution.py:291
  26.0 3.8 %collective-permute-start.5 = (bf16[64,512]{1,0:T(8,128)(2,1)S(1)}, bf16[64,512]{1,0:T(8,128)(2,1)S(1)}, u32[]{:S(2)}, u32[]{:S(2)}) collective-permute-start(bf16[64,512]{1,0:T(8,128)(2,1)S(1)} %get-tuple-element.30), channel_id=1, source_target_pairs={{0,240},{8,248},{16,0},{24,8},{32,16},{40,24},{48,32},{56,40},{64,... | collective-permute-start | bytes 196616 | tf_op jit(solution)/shard_map/ppermute | solution.py:230
  29.8 0.1 collective-permute-start.6
  29.9 1.7 %collective-permute-start.7 = (bf16[64,512]{1,0:T(8,128)(2,1)S(1)}, bf16[64,512]{1,0:T(8,128)(2,1)S(1)}, u32[]{:S(2)}, u32[]{:S(2)}) collective-permute-start(bf16[64,512]{1,0:T(8,128)(2,1)S(1)} %get-tuple-element.33), channel_id=1, source_target_pairs={{0,8},{8,16},{16,24},{24,32},{32,40},{40,48},{48,56},{56,64},{64,7... | collective-permute-start | bytes 196616 | tf_op jit(solution)/shard_map/ppermute | solution.py:230
  31.6 14.8 %collective-permute-done.5.refs_0_ = bf16[64,512]{1,0:T(8,128)(2,1)S(1)} collective-permute-done((bf16[64,512]{1,0:T(8,128)(2,1)S(1)}, bf16[64,512]{1,0:T(8,128)(2,1)S(1)}, u32[]{:S(2)}, u32[]{:S(2)}) %collective-permute-start.5) | collective-permute-done | bytes 65568 | tf_op jit(solution)/shard_map/ppermute | solution.py:230
  46.4 0.0 collective-permute-start.8
  46.4 0.0 collective-permute-done.6.refs_1_
  46.4 0.0 collective-permute-done.7.refs_3_
  46.4 4.6 %collective-permute-done.8.refs_4_ = bf16[64,512]{1,0:T(8,128)(2,1)S(1)} collective-permute-done((bf16[64,512]{1,0:T(8,128)(2,1)S(1)}, bf16[64,512]{1,0:T(8,128)(2,1)S(1)}, u32[]{:S(2)}, u32[]{:S(2)}) %collective-permute-start.8) | collective-permute-done | bytes 65568 | tf_op jit(solution)/shard_map/ppermute | solution.py:230
  51.0 0.4 merge.1
  51.4 0.1 collective-permute-start.11
  51.5 3.3 %collective-permute-start.10 = (bf16[64,384]{1,0:T(8,128)(2,1)S(1)}, bf16[64,384]{1,0:T(8,128)(2,1)S(1)}, u32[]{:S(2)}, u32[]{:S(2)}) collective-permute-start(bf16[64,384]{1,0:T(8,128)(2,1)S(1)} %merge.1), channel_id=1, source_target_pairs={{0,16},{8,24},{16,0},{24,8},{32,48},{40,56},{48,32},{56,40},{64,80... | collective-permute-start | bytes 147464 | tf_op jit(solution)/shard_map/ppermute | solution.py:235
  54.8 0.0 collective-permute-start.9
  54.8 0.0 collective-permute-done.11
  54.8 1.5 %collective-permute-done.10 = bf16[64,384]{1,0:T(8,128)(2,1)S(1)} collective-permute-done((bf16[64,384]{1,0:T(8,128)(2,1)S(1)}, bf16[64,384]{1,0:T(8,128)(2,1)S(1)}, u32[]{:S(2)}, u32[]{:S(2)}) %collective-permute-start.10) | collective-permute-done | bytes 49184 | tf_op jit(solution)/shard_map/ppermute | solution.py:235
  56.3 1.5 %collective-permute-done.9 = bf16[64,384]{1,0:T(8,128)(2,1)S(1)} collective-permute-done((bf16[64,384]{1,0:T(8,128)(2,1)S(1)}, bf16[64,384]{1,0:T(8,128)(2,1)S(1)}, u32[]{:S(2)}, u32[]{:S(2)}) %collective-permute-start.9) | collective-permute-done | bytes 49184 | tf_op jit(solution)/shard_map/ppermute | solution.py:235
  57.8 0.0 collective-permute-done.2
  57.8 0.0 collective-permute-done.3
  57.8 0.1 collective-permute-start.14
  57.9 0.1 collective-permute-start.13
  58.0 0.1 add.14.refs_3_
  58.1 1.6 %collective-permute-start.12 = (bf16[2,128,384]{2,1,0:T(8,128)(2,1)S(1)}, bf16[2,128,384]{2,1,0:T(8,128)(2,1)S(1)}, u32[]{:S(2)}, u32[]{:S(2)}) collective-permute-start(bf16[2,128,384]{2,1,0:T(8,128)(2,1)S(1)} %constant_dynamic-slice_fusion), channel_id=1, source_target_pairs={{0,32},{8,40},{16,240},{24,248},{32,64},{40,72},{48,16},{56,24},{6... | collective-permute-start | bytes 589832 | tf_op jit(solution)/shard_map/ppermute | solution.py:283
  59.7 3.2 %collective-permute-start.16 = (bf16[256,384]{1,0:T(8,128)(2,1)S(1)}, bf16[256,384]{1,0:T(8,128)(2,1)S(1)}, u32[]{:S(2)}, u32[]{:S(2)}) collective-permute-start(bf16[256,384]{1,0:T(8,128)(2,1)S(1)} %pad_maximum_fusion.refs_0_), channel_id=1, source_target_pairs={{0,32},{8,40},{16,48},{24,56},{32,64},{40,72},{48,80},{56,88},{64,... | collective-permute-start | bytes 589832 | tf_op jit(solution)/shard_map/ppermute | solution.py:230
  62.9 0.0 collective-permute-start.15
  62.9 2.8 %collective-permute-done.14.refs_2_ = bf16[256,384]{1,0:T(8,128)(2,1)S(1)} collective-permute-done((bf16[256,384]{1,0:T(8,128)(2,1)S(1)}, bf16[256,384]{1,0:T(8,128)(2,1)S(1)}, u32[]{:S(2)}, u32[]{:S(2)}) %collective-permute-start.14) | collective-permute-done | bytes 196640 | tf_op jit(solution)/shard_map/ppermute | solution.py:230
  65.8 4.6 %collective-permute-start.19 = (bf16[256,384]{1,0:T(8,128)(2,1)S(1)}, bf16[256,384]{1,0:T(8,128)(2,1)S(1)}, u32[]{:S(2)}, u32[]{:S(2)}) collective-permute-start(bf16[256,384]{1,0:T(8,128)(2,1)S(1)} %collective-permute-done.14.refs_2_), channel_id=1, source_target_pairs={{0,32},{8,40},{16,48},{24,56},{32,64},{40,72},{48,80},{56,88},{64,... | collective-permute-start | bytes 589832 | tf_op jit(solution)/shard_map/ppermute | solution.py:230
  70.4 0.0 collective-permute-done.13.refs_1_
  70.4 4.5 %collective-permute-start.18 = (bf16[256,384]{1,0:T(8,128)(2,1)S(1)}, bf16[256,384]{1,0:T(8,128)(2,1)S(1)}, u32[]{:S(2)}, u32[]{:S(2)}) collective-permute-start(bf16[256,384]{1,0:T(8,128)(2,1)S(1)} %collective-permute-done.13.refs_1_), channel_id=1, source_target_pairs={{0,32},{8,40},{16,48},{24,56},{32,64},{40,72},{48,80},{56,88},{64,... | collective-permute-start | bytes 589832 | tf_op jit(solution)/shard_map/ppermute | solution.py:230
  74.9 4.9 %collective-permute-done.12.refs_4_ = bf16[2,128,384]{2,1,0:T(8,128)(2,1)S(1)} collective-permute-done((bf16[2,128,384]{2,1,0:T(8,128)(2,1)S(1)}, bf16[2,128,384]{2,1,0:T(8,128)(2,1)S(1)}, u32[]{:S(2)}, u32[]{:S(2)}) %collective-permute-start.12) | collective-permute-done | bytes 196640 | tf_op jit(solution)/shard_map/ppermute | solution.py:283
  79.8 0.0 collective-permute-start.17
  79.8 0.0 copy-done.1
  79.8 0.0 copy-done.2
  79.8 3.5 %video_side.1 = bf16[512,384]{1,0:T(8,128)(2,1)} custom-call(s32[32]{0:T(128)S(1)} %copy-done.2, s32[32,2]{1,0:T(8,128)S(1)} %copy.9.refs_1_, bf16[512,384]{1,0:T(8,128)(2,1)S(1)} %copy-done.1, bf16[2,256,384]{2,1,0:T(8,128)(2,1)S(1)} %add.14.refs_3_, bf16[2,128,384]{2,1,0:T(8,128)(2,1)S(1)} %collective-permute-done.12.refs_4_), custom_call_target="tpu_custom_call" | custom-call | tf_op jit(solution)/shard_map/video_side/pallas_call | solution.py:319
  83.4 0.0 collective-permute-done.16.refs_4_
  83.4 0.0 collective-permute-done.15.refs_3_
  83.4 0.0 collective-permute-done.19.refs_7_
  83.4 0.0 collective-permute-done.18.refs_6_
  83.4 3.4 %collective-permute-done.17.refs_5_ = bf16[256,384]{1,0:T(8,128)(2,1)S(1)} collective-permute-done((bf16[256,384]{1,0:T(8,128)(2,1)S(1)}, bf16[256,384]{1,0:T(8,128)(2,1)S(1)}, u32[]{:S(2)}, u32[]{:S(2)}) %collective-permute-start.17) | collective-permute-done | bytes 196640 | tf_op jit(solution)/shard_map/ppermute | solution.py:230
  86.8 1.4 %assemble.1 = bf16[2048,384]{1,0:T(8,128)(2,1)} custom-call(bf16[256,384]{1,0:T(8,128)(2,1)S(1)} %pad_maximum_fusion.refs_0_, bf16[256,384]{1,0:T(8,128)(2,1)S(1)} %collective-permute-done.13.refs_1_, bf16[256,384]{1,0:T(8,128)(2,1)S(1)} %collective-permute-done.14.refs_2_, bf16[256,384]{1,0:T(8,128)(2,1)S(1)} %collective-permute-done.15.refs_3_, ...), custom_call_target="tpu_custom_call" | custom-call | tf_op jit(solution)/shard_map/assemble/pallas_call | solution.py:332
  (3 shorter events, 0.1 us)
Async XLA Ops:
  0.6 23.1 %copy-start.4 = (s32[32,2]{0,1:T(2,128)S(1)}, s32[32,2]{0,1:T(2,128)}, u32[]{:S(2)}) copy-start(s32[32,2]{0,1:T(2,128)} %param.11) | copy-start | bytes 772
  0.6 23.3 %copy-start.3 = (s32[2]{0:T(128)S(1)}, s32[2]{0:T(128)}, u32[]{:S(2)}) copy-start(s32[2]{0:T(128)} %refs_0_.5) | copy-start | bytes 28
  0.7 23.3 %copy-start = (bf16[2,512,384]{2,1,0:T(8,128)(2,1)S(1)}, bf16[2,512,384]{2,1,0:T(8,128)(2,1)}, u32[]{:S(2)}) copy-start(bf16[2,512,384]{2,1,0:T(8,128)(2,1)} %refs_4_.1) | copy-start | bytes 2359300
  2.5 77.3 %copy-start.1 = (bf16[512,384]{1,0:T(8,128)(2,1)S(1)}, bf16[512,384]{1,0:T(8,128)(2,1)}, u32[]{:S(2)}) copy-start(bf16[512,384]{1,0:T(8,128)(2,1)} %refs_2_.1) | copy-start | bytes 1179652
  2.6 77.2 %copy-start.2 = (s32[32]{0:T(128)S(1)}, s32[32]{0:T(128)}, u32[]{:S(2)}) copy-start(s32[32]{0:T(128)} %refs_0_.6) | copy-start | bytes 388
  2.6 10.8 %collective-permute-start = (bf16[1,256,384]{2,1,0:T(8,128)(2,1)}, bf16[1,256,384]{2,1,0:T(8,128)(2,1)S(1)}, u32[]{:S(2)}, u32[]{:S(2)}) collective-permute-start(bf16[1,256,384]{2,1,0:T(8,128)(2,1)} %get-tuple-element.25), channel_id=1, source_target_pairs={{192,0},{32,2},{0,4},{224,6},{200,8},{40,10},{8,12},{232,14},{208,... | collective-permute-start | bytes 589832 | tf_op jit(solution)/shard_map/ppermute | solution.py:278
  7.2 8.8 %collective-permute-start.1 = (bf16[1,256,384]{2,1,0:T(8,128)(2,1)}, bf16[1,256,384]{2,1,0:T(8,128)(2,1)S(1)}, u32[]{:S(2)}, u32[]{:S(2)}) collective-permute-start(bf16[1,256,384]{2,1,0:T(8,128)(2,1)} %get-tuple-element.26), channel_id=1, source_target_pairs={{192,1},{32,3},{0,5},{224,7},{200,9},{40,11},{8,13},{232,15},{208,... | collective-permute-start | bytes 589832 | tf_op jit(solution)/shard_map/ppermute | solution.py:278
  16.1 7.8 %collective-permute-start.4 = (bf16[128,384]{1,0:T(8,128)(2,1)S(1)}, bf16[128,384]{1,0:T(8,128)(2,1)S(1)}, u32[]{:S(2)}, u32[]{:S(2)}) collective-permute-start(bf16[128,384]{1,0:T(8,128)(2,1)S(1)} %dynamic-slice_bitcast_fusion), channel_id=1, source_target_pairs={{0,32},{8,40},{16,240},{24,248},{32,64},{40,72},{48,16},{56,24},{6... | collective-permute-start | bytes 294920 | tf_op jit(solution)/shard_map/ppermute | solution.py:283
  18.4 39.4 %collective-permute-start.2 = (bf16[2,256,384]{2,1,0:T(8,128)(2,1)}, bf16[2,256,384]{2,1,0:T(8,128)(2,1)S(1)}, u32[]{:S(2)}, u32[]{:S(2)}) collective-permute-start(bf16[2,256,384]{2,1,0:T(8,128)(2,1)} %get-tuple-element.27), channel_id=1, source_target_pairs={{192,0},{32,2},{0,4},{224,6},{200,8},{40,10},{8,12},{232,14},{208,... | collective-permute-start | bytes 1179656 | tf_op jit(solution)/shard_map/ppermute | solution.py:278
  21.5 36.2 %collective-permute-start.3 = (bf16[2,256,384]{2,1,0:T(8,128)(2,1)}, bf16[2,256,384]{2,1,0:T(8,128)(2,1)S(1)}, u32[]{:S(2)}, u32[]{:S(2)}) collective-permute-start(bf16[2,256,384]{2,1,0:T(8,128)(2,1)} %get-tuple-element.28), channel_id=1, source_target_pairs={{192,1},{32,3},{0,5},{224,7},{200,9},{40,11},{8,13},{232,15},{208,... | collective-permute-start | bytes 1179656 | tf_op jit(solution)/shard_map/ppermute | solution.py:278
  26.0 20.4 %collective-permute-start.5 = (bf16[64,512]{1,0:T(8,128)(2,1)S(1)}, bf16[64,512]{1,0:T(8,128)(2,1)S(1)}, u32[]{:S(2)}, u32[]{:S(2)}) collective-permute-start(bf16[64,512]{1,0:T(8,128)(2,1)S(1)} %get-tuple-element.30), channel_id=1, source_target_pairs={{0,240},{8,248},{16,0},{24,8},{32,16},{40,24},{48,32},{56,40},{64,... | collective-permute-start | bytes 196616 | tf_op jit(solution)/shard_map/ppermute | solution.py:230
  29.8 16.6 %collective-permute-start.6 = (bf16[64,512]{1,0:T(8,128)(2,1)S(1)}, bf16[64,512]{1,0:T(8,128)(2,1)S(1)}, u32[]{:S(2)}, u32[]{:S(2)}) collective-permute-start(bf16[64,512]{1,0:T(8,128)(2,1)S(1)} %get-tuple-element.31), channel_id=1, source_target_pairs={{0,248},{8,0},{16,8},{24,16},{32,24},{40,32},{48,40},{56,48},{64,5... | collective-permute-start | bytes 196616 | tf_op jit(solution)/shard_map/ppermute | solution.py:230
  29.9 16.5 %collective-permute-start.7 = (bf16[64,512]{1,0:T(8,128)(2,1)S(1)}, bf16[64,512]{1,0:T(8,128)(2,1)S(1)}, u32[]{:S(2)}, u32[]{:S(2)}) collective-permute-start(bf16[64,512]{1,0:T(8,128)(2,1)S(1)} %get-tuple-element.33), channel_id=1, source_target_pairs={{0,8},{8,16},{16,24},{24,32},{32,40},{40,48},{48,56},{56,64},{64,7... | collective-permute-start | bytes 196616 | tf_op jit(solution)/shard_map/ppermute | solution.py:230
  46.4 4.6 %collective-permute-start.8 = (bf16[64,512]{1,0:T(8,128)(2,1)S(1)}, bf16[64,512]{1,0:T(8,128)(2,1)S(1)}, u32[]{:S(2)}, u32[]{:S(2)}) collective-permute-start(bf16[64,512]{1,0:T(8,128)(2,1)S(1)} %get-tuple-element.34), channel_id=1, source_target_pairs={{0,16},{8,24},{16,32},{24,40},{32,48},{40,56},{48,64},{56,72},{64,... | collective-permute-start | bytes 196616 | tf_op jit(solution)/shard_map/ppermute | solution.py:230
  51.4 3.4 %collective-permute-start.11 = (bf16[64,384]{1,0:T(8,128)(2,1)S(1)}, bf16[64,384]{1,0:T(8,128)(2,1)S(1)}, u32[]{:S(2)}, u32[]{:S(2)}) collective-permute-start(bf16[64,384]{1,0:T(8,128)(2,1)S(1)} %merge.1), channel_id=1, source_target_pairs={{0,24},{8,0},{16,8},{24,16},{32,56},{40,32},{48,40},{56,48},{64,88... | collective-permute-start | bytes 147464 | tf_op jit(solution)/shard_map/ppermute | solution.py:235
  51.5 4.7 %collective-permute-start.10 = (bf16[64,384]{1,0:T(8,128)(2,1)S(1)}, bf16[64,384]{1,0:T(8,128)(2,1)S(1)}, u32[]{:S(2)}, u32[]{:S(2)}) collective-permute-start(bf16[64,384]{1,0:T(8,128)(2,1)S(1)} %merge.1), channel_id=1, source_target_pairs={{0,16},{8,24},{16,0},{24,8},{32,48},{40,56},{48,32},{56,40},{64,80... | collective-permute-start | bytes 147464 | tf_op jit(solution)/shard_map/ppermute | solution.py:235
  54.8 2.9 %collective-permute-start.9 = (bf16[64,384]{1,0:T(8,128)(2,1)S(1)}, bf16[64,384]{1,0:T(8,128)(2,1)S(1)}, u32[]{:S(2)}, u32[]{:S(2)}) collective-permute-start(bf16[64,384]{1,0:T(8,128)(2,1)S(1)} %merge.1), channel_id=1, source_target_pairs={{0,8},{8,16},{16,24},{24,0},{32,40},{40,48},{48,56},{56,32},{64,72... | collective-permute-start | bytes 147464 | tf_op jit(solution)/shard_map/ppermute | solution.py:235
  57.8 8.0 %collective-permute-start.14 = (bf16[256,384]{1,0:T(8,128)(2,1)S(1)}, bf16[256,384]{1,0:T(8,128)(2,1)S(1)}, u32[]{:S(2)}, u32[]{:S(2)}) collective-permute-start(bf16[256,384]{1,0:T(8,128)(2,1)S(1)} %pad_maximum_fusion.refs_0_), channel_id=1, source_target_pairs={{0,64},{8,72},{16,80},{24,88},{32,96},{40,104},{48,112},{56,120},{... | collective-permute-start | bytes 589832 | tf_op jit(solution)/shard_map/ppermute | solution.py:230
  57.9 12.5 %collective-permute-start.13 = (bf16[256,384]{1,0:T(8,128)(2,1)S(1)}, bf16[256,384]{1,0:T(8,128)(2,1)S(1)}, u32[]{:S(2)}, u32[]{:S(2)}) collective-permute-start(bf16[256,384]{1,0:T(8,128)(2,1)S(1)} %pad_maximum_fusion.refs_0_), channel_id=1, source_target_pairs={{0,160},{8,168},{16,176},{24,184},{32,192},{40,200},{48,208},{56,2... | collective-permute-start | bytes 589832 | tf_op jit(solution)/shard_map/ppermute | solution.py:230
  58.1 21.7 %collective-permute-start.12 = (bf16[2,128,384]{2,1,0:T(8,128)(2,1)S(1)}, bf16[2,128,384]{2,1,0:T(8,128)(2,1)S(1)}, u32[]{:S(2)}, u32[]{:S(2)}) collective-permute-start(bf16[2,128,384]{2,1,0:T(8,128)(2,1)S(1)} %constant_dynamic-slice_fusion), channel_id=1, source_target_pairs={{0,32},{8,40},{16,240},{24,248},{32,64},{40,72},{48,16},{56,24},{6... | collective-permute-start | bytes 589832 | tf_op jit(solution)/shard_map/ppermute | solution.py:283
  59.7 23.7 %collective-permute-start.16 = (bf16[256,384]{1,0:T(8,128)(2,1)S(1)}, bf16[256,384]{1,0:T(8,128)(2,1)S(1)}, u32[]{:S(2)}, u32[]{:S(2)}) collective-permute-start(bf16[256,384]{1,0:T(8,128)(2,1)S(1)} %pad_maximum_fusion.refs_0_), channel_id=1, source_target_pairs={{0,32},{8,40},{16,48},{24,56},{32,64},{40,72},{48,80},{56,88},{64,... | collective-permute-start | bytes 589832 | tf_op jit(solution)/shard_map/ppermute | solution.py:230
  62.9 20.5 %collective-permute-start.15 = (bf16[256,384]{1,0:T(8,128)(2,1)S(1)}, bf16[256,384]{1,0:T(8,128)(2,1)S(1)}, u32[]{:S(2)}, u32[]{:S(2)}) collective-permute-start(bf16[256,384]{1,0:T(8,128)(2,1)S(1)} %pad_maximum_fusion.refs_0_), channel_id=1, source_target_pairs={{0,224},{8,232},{16,240},{24,248},{32,0},{40,8},{48,16},{56,24},{6... | collective-permute-start | bytes 589832 | tf_op jit(solution)/shard_map/ppermute | solution.py:230
  65.8 17.6 %collective-permute-start.19 = (bf16[256,384]{1,0:T(8,128)(2,1)S(1)}, bf16[256,384]{1,0:T(8,128)(2,1)S(1)}, u32[]{:S(2)}, u32[]{:S(2)}) collective-permute-start(bf16[256,384]{1,0:T(8,128)(2,1)S(1)} %collective-permute-done.14.refs_2_), channel_id=1, source_target_pairs={{0,32},{8,40},{16,48},{24,56},{32,64},{40,72},{48,80},{56,88},{64,... | collective-permute-start | bytes 589832 | tf_op jit(solution)/shard_map/ppermute | solution.py:230
  70.4 13.0 %collective-permute-start.18 = (bf16[256,384]{1,0:T(8,128)(2,1)S(1)}, bf16[256,384]{1,0:T(8,128)(2,1)S(1)}, u32[]{:S(2)}, u32[]{:S(2)}) collective-permute-start(bf16[256,384]{1,0:T(8,128)(2,1)S(1)} %collective-permute-done.13.refs_1_), channel_id=1, source_target_pairs={{0,32},{8,40},{16,48},{24,56},{32,64},{40,72},{48,80},{56,88},{64,... | collective-permute-start | bytes 589832 | tf_op jit(solution)/shard_map/ppermute | solution.py:230
  79.8 7.0 %collective-permute-start.17 = (bf16[256,384]{1,0:T(8,128)(2,1)S(1)}, bf16[256,384]{1,0:T(8,128)(2,1)S(1)}, u32[]{:S(2)}, u32[]{:S(2)}) collective-permute-start(bf16[256,384]{1,0:T(8,128)(2,1)S(1)} %collective-permute-done.13.refs_1_), channel_id=1, source_target_pairs={{0,224},{8,232},{16,240},{24,248},{32,0},{40,8},{48,16},{56,24},{6... | collective-permute-start | bytes 589832 | tf_op jit(solution)/shard_map/ppermute | solution.py:230

commit v3 on v2

--- a/solution.py
+++ b/solution.py
@@ -41,17 +41,18 @@
     return z + (2 if z % 2 else -2, 1, 0, -1)[turn]
 
 
-def pack_kernel(first_part, parts, src, out0, out1, sems):
-    _, z, _ = place()
-    columns = out0.shape[-1]
+def pack_kernel(src, out0, out1, sems):
+    _, z, x = place()
+    parts, _, columns = out0.shape
     first = sender_row(z, lax.axis_index("audio")) * 2 * columns
+    rows = pl.ds(pl.multiple_of(x * ABS, ABS), ABS)
     copies = []
     for core, out in enumerate((out0, out1)):
         cols = pl.ds(pl.multiple_of(first + core * columns, 128), columns)
         for i in range(parts):
             copies.append(
                 pltpu.make_async_copy(
-                    src.at[first_part + i, :, cols], out.at[i], sems.at[core * parts + i]
+                    src.at[i, rows, cols], out.at[i], sems.at[core * parts + i]
                 )
             )
     for c in copies:
@@ -60,6 +61,10 @@
         c.wait()
 
 
+def slot_block(z, x, slot):
+    return z * XS + lax.rem(x - slot + XS, XS)
+
+
 def split3(value):
     hi = value.astype(jnp.bfloat16).astype(jnp.float32)
     rest = value - hi
@@ -67,11 +72,11 @@
     return hi, mid, rest - mid
 
 
-def audio_kernel(scale, count, ranges, q_own, q_out, kv, *refs):
-    outs, (queries, bias) = refs[:5], refs[5:]
+def audio_kernel(scale, count, ranges, kv, edge, *refs):
+    slots, outs, (queries, bias) = refs[:XS], refs[XS : XS + 5], refs[XS + 5 :]
     v, z, x = place()
     blocks = ranges.shape[0]
-    columns = q_own.shape[1]
+    columns = edge.shape[2]
     heads = columns // 128
     lane = lax.broadcasted_iota(jnp.int32, (ABS, 2 * VBS), 1)
     for slot in range(5):
@@ -82,12 +87,14 @@
 
         @pl.when(own)
         def _():
-            queries[dst, :] = q_own[pl.ds(pl.multiple_of(at * ABS, ABS), ABS), :]
-
-        @pl.when(jnp.logical_not(own))
-        def _():
-            row = jnp.where(at < 0, at + REACH, at - XS) * ABS
-            queries[dst, :] = q_out[pl.ds(pl.multiple_of(row, ABS), ABS), :]
+            queries[dst, :] = slots[-offset % XS][0]
+
+        if offset:
+
+            @pl.when(jnp.logical_not(own))
+            def _():
+                row = (-1 - at if offset < 0 else XS + 1 - at) * ABS
+                queries[dst, :] = edge[0, pl.ds(pl.multiple_of(row, ABS), ABS), :]
 
         block = v + offset
         inside = (block >= 0) & (block < blocks)
@@ -147,23 +154,20 @@
         out[:, cols] = (blend / total).astype(jnp.bfloat16)
 
 
-def video_kernel(scale, audio_count, ranges, query, kv_own, kv_out, out, bias):
+def video_kernel(scale, audio_count, ranges, query, edge, *refs):
+    slots, out, bias = refs[:XS], refs[XS], refs[XS + 1]
     v, z, x = place()
     blocks = ranges.shape[0]
     columns = query.shape[1]
-    keys = kv_own.shape[1] + kv_out.shape[1]
-    own_keys = kv_own.shape[1]
     lane = lax.broadcasted_iota(jnp.int32, (8, ABS * 2), 1)
-    for pair in range(keys // (2 * ABS)):
+    held = [slot_block(z, x, at) for at in range(XS)]
+    held += [z * XS + jnp.where(x < REACH, -1 - at, XS + 1 - at) for at in range(REACH)]
+    for pair in range(len(held) // 2):
         for j in range(2):
             vb = v * 2 + j
             allowed = None
             for side in range(2):
-                pos = pair * 2 + side
-                if pos < XS:
-                    block = z * XS + pos
-                else:
-                    block = z * XS + (pos - XS) + jnp.where(x < REACH, -REACH, XS)
+                block = held[pair * 2 + side]
                 inside = (block >= 0) & (block < blocks)
                 safe = jnp.clip(block, 0, blocks - 1)
                 paired = inside & (ranges[safe, 0] <= vb) & (vb < ranges[safe, 1])
@@ -171,31 +175,24 @@
                 here = (lane >= side * ABS) & (lane < side * ABS + live)
                 allowed = here if allowed is None else allowed | here
             bias[j, :, pair * 2 * ABS : (pair + 1) * 2 * ABS] = jnp.where(allowed, 0.0, NEG)
-    for j in range(2):
-        rows = slice(j * VBS, (j + 1) * VBS)
-        for h in range(columns // 128):
-            cols = slice(h * 128, (h + 1) * 128)
-            dims = (((1,), (1,)), ((), ()))
-            s1 = lax.dot_general(
-                query[rows, cols], kv_own[0, :, cols], dims, preferred_element_type=jnp.float32
+    for h in range(columns // 128):
+        cols = slice(h * 128, (h + 1) * 128)
+        k, values = [
+            jnp.concatenate([slot[i, :, cols] for slot in slots] + [edge[i - 1, :, cols]], axis=0)
+            for i in (1, 2)
+        ]
+        for j in range(2):
+            rows = slice(j * VBS, (j + 1) * VBS)
+            s = lax.dot_general(
+                query[rows, cols], k, (((1,), (1,)), ((), ())),
+                preferred_element_type=jnp.float32,
             )
-            s2 = lax.dot_general(
-                query[rows, cols], kv_out[0, :, cols], dims, preferred_element_type=jnp.float32
-            )
-            s1 = s1 + bias[j, 0:1, :own_keys]
-            s2 = s2 + bias[j, 0:1, own_keys:]
-            peak = jnp.maximum(
-                jnp.max(s1, axis=1, keepdims=True), jnp.max(s2, axis=1, keepdims=True)
-            )
-            e1 = jnp.exp2((s1 - peak) * scale)
-            e2 = jnp.exp2((s2 - peak) * scale)
-            total = jnp.sum(e1, axis=1, keepdims=True) + jnp.sum(e2, axis=1, keepdims=True)
-            dims = (((1,), (0,)), ((), ()))
+            s = s + bias[j, 0:1, :]
+            peak = jnp.max(s, axis=1, keepdims=True)
+            e = jnp.exp2((s - peak) * scale)
+            total = jnp.sum(e, axis=1, keepdims=True)
             o = lax.dot_general(
-                e1.astype(jnp.bfloat16), kv_own[1, :, cols], dims,
-                preferred_element_type=jnp.float32,
-            ) + lax.dot_general(
-                e2.astype(jnp.bfloat16), kv_out[1, :, cols], dims,
+                e.astype(jnp.bfloat16), values, (((1,), (0,)), ((), ())),
                 preferred_element_type=jnp.float32,
             )
             out[rows, cols] = (o / total).astype(jnp.bfloat16)
@@ -251,22 +248,15 @@
     def flat(z, x, a):
         return ((z % ZS) * XS + x) * audio_devices + a
 
-    def packed_slices(first_part, parts, value, name):
-        return pl.pallas_call(
-            lambda *refs: pack_kernel(first_part, parts, *refs),
-            out_shape=(jax.ShapeDtypeStruct((parts, shard_rows, columns), bf16),) * 2,
-            in_specs=[ANY],
-            out_specs=(VMEM,) * 2,
-            scratch_shapes=[pltpu.SemaphoreType.DMA((2 * parts,))],
-            compiler_params=pltpu.CompilerParams(vmem_limit_bytes=60 * 1024 * 1024),
-            name=name,
-        )(value)
-
-    q0, q1 = packed_slices(0, 1, audio_qkv, "pack_queries")
-    q0, q1, later = lax.optimization_barrier((q0, q1, audio_qkv))
-    kv0, kv1 = packed_slices(1, 2, later, "pack_keys")
-    x = lax.axis_index("video") % XS
-    edge = jnp.where(x < REACH, half, 0)
+    pack0, pack1 = pl.pallas_call(
+        pack_kernel,
+        out_shape=(jax.ShapeDtypeStruct((3, ABS, columns), bf16),) * 2,
+        in_specs=[ANY],
+        out_specs=(VMEM,) * 2,
+        scratch_shapes=[pltpu.SemaphoreType.DMA((6,))],
+        compiler_params=pltpu.CompilerParams(vmem_limit_bytes=60 * 1024 * 1024),
+        name="pack",
+    )(audio_qkv)
 
     def to_core(value, core):
         pairs = []
@@ -277,21 +267,23 @@
                     pairs.append((flat(sender, xx, z), flat(z, xx, 2 * y + core)))
         return lax.ppermute(value, BOTH, pairs)
 
-    def from_next_line(value):
+    def between_lines(value, step):
         n = ZS * XS
-        pairs = [(v, (v + XS if v % XS < REACH else v - XS) % n) for v in range(n)]
+        pairs = [(v, (v + step if v % XS < REACH else v - step) % n) for v in range(n)]
         return lax.ppermute(value, "video", pairs)
 
-    q_own = (to_core(q0, 0) + to_core(q1, 1))[0]
-    q_out = from_next_line(lax.dynamic_slice_in_dim(q_own, edge, half, 0))
-    kv0, kv1, q_own = lax.optimization_barrier((kv0, kv1, q_own))
-    kv0, kv1 = to_core(kv0, 0), to_core(kv1, 1)
-
-    packed = jax.ShapeDtypeStruct((ABS, columns + 128), bf16)
+    own = to_core(pack0, 0) + to_core(pack1, 1)
+    slots = [own] + [along_x(own, k) for k in range(1, XS)]
+
+    odd = lax.axis_index("video") % 2 == 1
+    near = [jnp.where(odd, slots[at + 2], slots[at + 1]) for at in range(REACH)]
+    near = jnp.concatenate(near, axis=1)
+    edge, near_kv = lax.optimization_barrier((between_lines(near[:1], XS), near[1:]))
+    edge_kv = between_lines(near_kv, XS)
     parts = pl.pallas_call(
         lambda *refs: audio_kernel(scale, *refs),
-        out_shape=(packed,) * 5,
-        in_specs=[SMEM, SMEM, VMEM, VMEM, VMEM],
+        out_shape=(jax.ShapeDtypeStruct((ABS, columns + 128), bf16),) * 5,
+        in_specs=[SMEM] * 2 + [VMEM] * (2 + XS),
         out_specs=(VMEM,) * 5,
         scratch_shapes=[
             pltpu.VMEM((5 * ABS, columns), bf16),
@@ -299,7 +291,7 @@
         ],
         compiler_params=params(),
         name="audio_side",
-    )(video_count, video_range, q_own, q_out, video_kv)
+    )(video_count, video_range, video_kv, edge, *slots)
     held = [
         shifted(part, slot - REACH) if slot != REACH else part for slot, part in enumerate(parts)
     ]
@@ -313,18 +305,16 @@
     )(*held)
 
     row = jnp.concatenate([block_out] + [along_x(block_out, k) for k in range(1, XS)], axis=0)
-    kv0, kv1, row = lax.optimization_barrier((kv0, kv1, row))
-    kv_own = kv0 + kv1
-    kv_out = from_next_line(lax.dynamic_slice_in_dim(kv_own, edge, half, 1))
+    row, edge_kv = lax.optimization_barrier((row, edge_kv))
     video_out = pl.pallas_call(
         lambda *refs: video_kernel(scale, *refs),
         out_shape=jax.ShapeDtypeStruct((seg_rows, columns), bf16),
-        in_specs=[SMEM, SMEM, VMEM, VMEM, VMEM],
+        in_specs=[SMEM, SMEM] + [VMEM] * (2 + XS),
         out_specs=VMEM,
         scratch_shapes=[pltpu.VMEM((2, 8, shard_rows + half), f32)],
         compiler_params=params(),
         name="video_side",
-    )(audio_count, video_range, video_query, kv_own, kv_out)
+    )(audio_count, video_range, video_query, edge_kv, *slots)
 
     z3, zm2 = from_z(row, 3), from_z(row, -2)
     z1, zm1 = from_z(row, 1), from_z(row, -1)

time: 88.6 us -> 84.7 us (0.956)
  the two profiles are of different devices: /device:TPU:109 before, /device:TPU:8 now
where the time goes in v3:
time: 84.7 us; the launch traced here: 84.5 us
  starting transfers between devices  38.9 us (46%)
  waiting for transfers between devices  35.3 us (42%)
  Pallas kernels  9.16 us (11%)
  between operations  0.95 us (1%)
    ppermute x11, starting transfers between devices, shifted(): return lax.ppermute(value, 'video', [(v, (v + step) % n) for v in range(n)])  19.9 us
    ppermute x11, waiting for transfers between devices, shifted(): return lax.ppermute(value, 'video', [(v, (v + step) % n) for v in range(n)])  17.1 us
    ppermute x6, waiting for transfers between devices, along_x(): return lax.ppermute(value, 'video', pairs)  10.8 us
    ppermute x2, starting transfers between devices, to_core(): return lax.ppermute(value, BOTH, pairs)  8.62 us
    ppermute x6, starting transfers between devices, along_x(): return lax.ppermute(value, 'video', pairs)  7.57 us
    ppermute x2, waiting for transfers between devices, between_lines(): return lax.ppermute(value, 'video', pairs)  4.27 us
    pallas_call x1, Pallas kernels, local(): pl.pallas_call(lambda *refs: video_kernel(scale, *refs), out_shape=jax.Sh...  3.46 us
    ppermute x2, waiting for transfers between devices, to_core(): return lax.ppermute(value, BOTH, pairs)  2.99 us
  transfers between devices with their start and end apart: 21, of which 13 were waited for; matrix products, arithmetic and copies ran while one was open for 0% of the time, Pallas kernels for 5%

profile of v3, /device:TPU:8, one launch (start us, length us, event | category | flops | bytes accessed | tf_op | source)
XLA Modules:
  0.0 84.5 jit_solution(2182248575666764562)
XLA Ops:
  0.6 0.0 copy-start.4
  0.6 0.0 copy-start.2
  0.7 0.0 copy-start
  0.7 0.0 copy-start.3
  0.7 0.0 copy-start.1
  0.7 1.8 %pack.1 = (bf16[3,64,384]{2,1,0:T(8,128)(2,1)}, bf16[3,64,384]{2,1,0:T(8,128)(2,1)}) custom-call(bf16[3,256,3072]{2,1,0:T(8,128)(2,1)} %src.1), custom_call_target="tpu_custom_call" | custom-call | tf_op jit(solution)/shard_map/pack/pallas_call | solution.py:251
  2.5 5.2 %collective-permute-start = (bf16[3,64,384]{2,1,0:T(8,128)(2,1)}, bf16[3,64,384]{2,1,0:T(8,128)(2,1)S(1)}, u32[]{:S(2)}, u32[]{:S(2)}) collective-permute-start(bf16[3,64,384]{2,1,0:T(8,128)(2,1)} %get-tuple-element.13), channel_id=1, source_target_pairs={{192,0},{32,2},{0,4},{224,6},{200,8},{40,10},{8,12},{232,14},{208,... | collective-permute-start | bytes 442376 | tf_op jit(solution)/shard_map/ppermute | solution.py:268
  7.7 3.4 %collective-permute-start.1 = (bf16[3,64,384]{2,1,0:T(8,128)(2,1)}, bf16[3,64,384]{2,1,0:T(8,128)(2,1)S(1)}, u32[]{:S(2)}, u32[]{:S(2)}) collective-permute-start(bf16[3,64,384]{2,1,0:T(8,128)(2,1)} %get-tuple-element.14), channel_id=1, source_target_pairs={{192,1},{32,3},{0,5},{224,7},{200,9},{40,11},{8,13},{232,15},{208,... | collective-permute-start | bytes 442376 | tf_op jit(solution)/shard_map/ppermute | solution.py:268
  11.1 0.0 collective-permute-done
  11.1 3.0 %collective-permute-done.1 = bf16[3,64,384]{2,1,0:T(8,128)(2,1)S(1)} collective-permute-done((bf16[3,64,384]{2,1,0:T(8,128)(2,1)}, bf16[3,64,384]{2,1,0:T(8,128)(2,1)S(1)}, u32[]{:S(2)}, u32[]{:S(2)}) %collective-permute-start.1) | collective-permute-done | bytes 147488 | tf_op jit(solution)/shard_map/ppermute | solution.py:268
  14.2 2.8 %collective-permute-start.4 = (bf16[3,64,384]{2,1,0:T(8,128)(2,1)S(1)}, bf16[3,64,384]{2,1,0:T(8,128)(2,1)S(1)}, u32[]{:S(2)}, u32[]{:S(2)}) collective-permute-start(bf16[3,64,384]{2,1,0:T(8,128)(2,1)S(1)} %add.8.refs_4_), channel_id=1, source_target_pairs={{0,24},{8,0},{16,8},{24,16},{32,56},{40,32},{48,40},{56,48},{64,88... | collective-permute-start | bytes 442376 | tf_op jit(solution)/shard_map/ppermute | solution.py:232
  17.0 0.0 collective-permute-start.3
  17.0 2.3 %collective-permute-start.2 = (bf16[3,64,384]{2,1,0:T(8,128)(2,1)S(1)}, bf16[3,64,384]{2,1,0:T(8,128)(2,1)S(1)}, u32[]{:S(2)}, u32[]{:S(2)}) collective-permute-start(bf16[3,64,384]{2,1,0:T(8,128)(2,1)S(1)} %add.8.refs_4_), channel_id=1, source_target_pairs={{0,16},{8,24},{16,0},{24,8},{32,48},{40,56},{48,32},{56,40},{64,80... | collective-permute-start | bytes 442376 | tf_op jit(solution)/shard_map/ppermute | solution.py:232
  19.3 0.0 copy-done.4
  19.3 0.1 copy.9.refs_1_
  19.4 1.9 %collective-permute-done.4.refs_7_ = bf16[3,64,384]{2,1,0:T(8,128)(2,1)S(1)} collective-permute-done((bf16[3,64,384]{2,1,0:T(8,128)(2,1)S(1)}, bf16[3,64,384]{2,1,0:T(8,128)(2,1)S(1)}, u32[]{:S(2)}, u32[]{:S(2)}) %collective-permute-start.4) | collective-permute-done | bytes 147488 | tf_op jit(solution)/shard_map/ppermute | solution.py:232
  21.3 3.7 %collective-permute-done.3.refs_5_ = bf16[3,64,384]{2,1,0:T(8,128)(2,1)S(1)} collective-permute-done((bf16[3,64,384]{2,1,0:T(8,128)(2,1)S(1)}, bf16[3,64,384]{2,1,0:T(8,128)(2,1)S(1)}, u32[]{:S(2)}, u32[]{:S(2)}) %collective-permute-start.3) | collective-permute-done | bytes 147488 | tf_op jit(solution)/shard_map/ppermute | solution.py:232
  24.9 0.0 collective-permute-done.2.refs_6_
  25.0 2.8 %collective-permute-start.5 = (bf16[1,128,384]{2,1,0:T(8,128)(2,1)S(1)}, bf16[1,128,384]{2,1,0:T(8,128)(2,1)S(1)}, u32[]{:S(2)}, u32[]{:S(2)}) collective-permute-start(bf16[1,128,384]{2,1,0:T(8,128)(2,1)S(1)} %pad_maximum_fusion.2), channel_id=1, source_target_pairs={{0,32},{8,40},{16,240},{24,248},{32,64},{40,72},{48,16},{56,24},{6... | collective-permute-start | bytes 294920 | tf_op jit(solution)/shard_map/ppermute | solution.py:273
  27.8 4.3 %collective-permute-done.5.refs_3_ = bf16[1,128,384]{2,1,0:T(8,128)(2,1)S(1)} collective-permute-done((bf16[1,128,384]{2,1,0:T(8,128)(2,1)S(1)}, bf16[1,128,384]{2,1,0:T(8,128)(2,1)S(1)}, u32[]{:S(2)}, u32[]{:S(2)}) %collective-permute-start.5) | collective-permute-done | bytes 98336 | tf_op jit(solution)/shard_map/ppermute | solution.py:273
  32.1 0.0 copy-done.2
  32.1 0.0 copy-done
  32.1 2.1 %audio_side.1 = (bf16[64,512]{1,0:T(8,128)(2,1)S(1)}, bf16[64,512]{1,0:T(8,128)(2,1)S(1)}, bf16[64,512]{1,0:T(8,128)(2,1)S(1)}, bf16[64,512]{1,0:T(8,128)(2,1)S(1)}, bf16[64,512]{1,0:T(8,128)(2,1)S(1)}) custom-call(s32[2]{0:T(128)S(1)} %copy-done.2, s32[32,2]{1,0:T(8,128)S(1)} %copy.9.refs_1_, bf16[2,512,384]{2,1,0:T(8,128)(2,1)S(1)} %copy-done, ...), custom_call_target="tpu_custom_call" | custom-call | tf_op jit(solution)/shard_map/audio_side/pallas_call | solution.py:283
  34.2 5.8 %collective-permute-start.6 = (bf16[64,512]{1,0:T(8,128)(2,1)S(1)}, bf16[64,512]{1,0:T(8,128)(2,1)S(1)}, u32[]{:S(2)}, u32[]{:S(2)}) collective-permute-start(bf16[64,512]{1,0:T(8,128)(2,1)S(1)} %get-tuple-element.16), channel_id=1, source_target_pairs={{0,240},{8,248},{16,0},{24,8},{32,16},{40,24},{48,32},{56,40},{64,... | collective-permute-start | bytes 196616 | tf_op jit(solution)/shard_map/ppermute | solution.py:227
  40.0 0.0 collective-permute-start.7
  40.0 2.0 %collective-permute-start.8 = (bf16[64,512]{1,0:T(8,128)(2,1)S(1)}, bf16[64,512]{1,0:T(8,128)(2,1)S(1)}, u32[]{:S(2)}, u32[]{:S(2)}) collective-permute-start(bf16[64,512]{1,0:T(8,128)(2,1)S(1)} %get-tuple-element.19), channel_id=1, source_target_pairs={{0,8},{8,16},{16,24},{24,32},{32,40},{40,48},{48,56},{56,64},{64,7... | collective-permute-start | bytes 196616 | tf_op jit(solution)/shard_map/ppermute | solution.py:227
  42.0 0.3 collective-permute-start.9
  42.3 0.0 collective-permute-start.13
  42.3 0.0 collective-permute-done.6.refs_0_
  42.3 2.3 %collective-permute-done.7.refs_1_ = bf16[64,512]{1,0:T(8,128)(2,1)S(1)} collective-permute-done((bf16[64,512]{1,0:T(8,128)(2,1)S(1)}, bf16[64,512]{1,0:T(8,128)(2,1)S(1)}, u32[]{:S(2)}, u32[]{:S(2)}) %collective-permute-start.7) | collective-permute-done | bytes 65568 | tf_op jit(solution)/shard_map/ppermute | solution.py:227
  44.6 4.0 %collective-permute-done.8.refs_3_ = bf16[64,512]{1,0:T(8,128)(2,1)S(1)} collective-permute-done((bf16[64,512]{1,0:T(8,128)(2,1)S(1)}, bf16[64,512]{1,0:T(8,128)(2,1)S(1)}, u32[]{:S(2)}, u32[]{:S(2)}) %collective-permute-start.8) | collective-permute-done | bytes 65568 | tf_op jit(solution)/shard_map/ppermute | solution.py:227
  48.5 1.3 %collective-permute-done.9.refs_4_ = bf16[64,512]{1,0:T(8,128)(2,1)S(1)} collective-permute-done((bf16[64,512]{1,0:T(8,128)(2,1)S(1)}, bf16[64,512]{1,0:T(8,128)(2,1)S(1)}, u32[]{:S(2)}, u32[]{:S(2)}) %collective-permute-start.9) | collective-permute-done | bytes 65568 | tf_op jit(solution)/shard_map/ppermute | solution.py:227
  49.9 0.4 merge.1
  50.3 0.1 collective-permute-start.12
  50.4 2.4 %collective-permute-start.11 = (bf16[64,384]{1,0:T(8,128)(2,1)S(1)}, bf16[64,384]{1,0:T(8,128)(2,1)S(1)}, u32[]{:S(2)}, u32[]{:S(2)}) collective-permute-start(bf16[64,384]{1,0:T(8,128)(2,1)S(1)} %merge.1), channel_id=1, source_target_pairs={{0,16},{8,24},{16,0},{24,8},{32,48},{40,56},{48,32},{56,40},{64,80... | collective-permute-start | bytes 147464 | tf_op jit(solution)/shard_map/ppermute | solution.py:232
  52.7 0.0 collective-permute-start.10
  52.7 1.7 %collective-permute-done.12 = bf16[64,384]{1,0:T(8,128)(2,1)S(1)} collective-permute-done((bf16[64,384]{1,0:T(8,128)(2,1)S(1)}, bf16[64,384]{1,0:T(8,128)(2,1)S(1)}, u32[]{:S(2)}, u32[]{:S(2)}) %collective-permute-start.12) | collective-permute-done | bytes 49184 | tf_op jit(solution)/shard_map/ppermute | solution.py:232
  54.5 1.6 %collective-permute-done.11 = bf16[64,384]{1,0:T(8,128)(2,1)S(1)} collective-permute-done((bf16[64,384]{1,0:T(8,128)(2,1)S(1)}, bf16[64,384]{1,0:T(8,128)(2,1)S(1)}, u32[]{:S(2)}, u32[]{:S(2)}) %collective-permute-start.11) | collective-permute-done | bytes 49184 | tf_op jit(solution)/shard_map/ppermute | solution.py:232
  56.1 2.0 %collective-permute-done.10 = bf16[64,384]{1,0:T(8,128)(2,1)S(1)} collective-permute-done((bf16[64,384]{1,0:T(8,128)(2,1)S(1)}, bf16[64,384]{1,0:T(8,128)(2,1)S(1)}, u32[]{:S(2)}, u32[]{:S(2)}) %collective-permute-start.10) | collective-permute-done | bytes 49184 | tf_op jit(solution)/shard_map/ppermute | solution.py:232
  58.1 0.0 collective-permute-done.13.refs_3_
  58.1 0.1 collective-permute-start.15
  58.2 2.3 %collective-permute-start.14 = (bf16[256,384]{1,0:T(8,128)(2,1)S(1)}, bf16[256,384]{1,0:T(8,128)(2,1)S(1)}, u32[]{:S(2)}, u32[]{:S(2)}) collective-permute-start(bf16[256,384]{1,0:T(8,128)(2,1)S(1)} %pad_maximum_fusion.1.refs_0_), channel_id=1, source_target_pairs={{0,160},{8,168},{16,176},{24,184},{32,192},{40,200},{48,208},{56,2... | collective-permute-start | bytes 589832 | tf_op jit(solution)/shard_map/ppermute | solution.py:227
  60.5 3.3 %collective-permute-start.17 = (bf16[256,384]{1,0:T(8,128)(2,1)S(1)}, bf16[256,384]{1,0:T(8,128)(2,1)S(1)}, u32[]{:S(2)}, u32[]{:S(2)}) collective-permute-start(bf16[256,384]{1,0:T(8,128)(2,1)S(1)} %pad_maximum_fusion.1.refs_0_), channel_id=1, source_target_pairs={{0,32},{8,40},{16,48},{24,56},{32,64},{40,72},{48,80},{56,88},{64,... | collective-permute-start | bytes 589832 | tf_op jit(solution)/shard_map/ppermute | solution.py:227
  63.8 0.0 collective-permute-start.16
  63.8 6.1 %collective-permute-done.15.refs_2_ = bf16[256,384]{1,0:T(8,128)(2,1)S(1)} collective-permute-done((bf16[256,384]{1,0:T(8,128)(2,1)S(1)}, bf16[256,384]{1,0:T(8,128)(2,1)S(1)}, u32[]{:S(2)}, u32[]{:S(2)}) %collective-permute-start.15) | collective-permute-done | bytes 196640 | tf_op jit(solution)/shard_map/ppermute | solution.py:227
  69.9 0.0 collective-permute-start.20
  69.9 1.3 %collective-permute-done.14.refs_1_ = bf16[256,384]{1,0:T(8,128)(2,1)S(1)} collective-permute-done((bf16[256,384]{1,0:T(8,128)(2,1)S(1)}, bf16[256,384]{1,0:T(8,128)(2,1)S(1)}, u32[]{:S(2)}, u32[]{:S(2)}) %collective-permute-start.14) | collective-permute-done | bytes 196640 | tf_op jit(solution)/shard_map/ppermute | solution.py:227
  71.1 6.1 %collective-permute-start.19 = (bf16[256,384]{1,0:T(8,128)(2,1)S(1)}, bf16[256,384]{1,0:T(8,128)(2,1)S(1)}, u32[]{:S(2)}, u32[]{:S(2)}) collective-permute-start(bf16[256,384]{1,0:T(8,128)(2,1)S(1)} %collective-permute-done.14.refs_1_), channel_id=1, source_target_pairs={{0,32},{8,40},{16,48},{24,56},{32,64},{40,72},{48,80},{56,88},{64,... | collective-permute-start | bytes 589832 | tf_op jit(solution)/shard_map/ppermute | solution.py:227
  77.3 0.0 collective-permute-start.18
  77.3 0.0 copy-done.3
  77.3 0.0 copy-done.1
  77.3 3.5 %video_side.1 = bf16[512,384]{1,0:T(8,128)(2,1)} custom-call(s32[32]{0:T(128)S(1)} %copy-done.3, s32[32,2]{1,0:T(8,128)S(1)} %copy.9.refs_1_, bf16[512,384]{1,0:T(8,128)(2,1)S(1)} %copy-done.1, bf16[2,128,384]{2,1,0:T(8,128)(2,1)S(1)} %collective-permute-done.13.refs_3_, bf16[3,64,384]{2,1,0:T(8,128)(2,1)S(1)} %add.8.refs_4_, ...), custom_call_target="tpu_custom_call" | custom-call | tf_op jit(solution)/shard_map/video_side/pallas_call | solution.py:309
  80.8 0.0 collective-permute-done.17.refs_4_
  80.8 0.0 collective-permute-done.16.refs_3_
  80.8 0.0 collective-permute-done.20.refs_7_
  80.8 0.0 collective-permute-done.19.refs_6_
  80.8 2.2 %collective-permute-done.18.refs_5_ = bf16[256,384]{1,0:T(8,128)(2,1)S(1)} collective-permute-done((bf16[256,384]{1,0:T(8,128)(2,1)S(1)}, bf16[256,384]{1,0:T(8,128)(2,1)S(1)}, u32[]{:S(2)}, u32[]{:S(2)}) %collective-permute-start.18) | collective-permute-done | bytes 196640 | tf_op jit(solution)/shard_map/ppermute | solution.py:227
  83.0 1.4 %assemble.1 = bf16[2048,384]{1,0:T(8,128)(2,1)} custom-call(bf16[256,384]{1,0:T(8,128)(2,1)S(1)} %pad_maximum_fusion.1.refs_0_, bf16[256,384]{1,0:T(8,128)(2,1)S(1)} %collective-permute-done.14.refs_1_, bf16[256,384]{1,0:T(8,128)(2,1)S(1)} %collective-permute-done.15.refs_2_, bf16[256,384]{1,0:T(8,128)(2,1)S(1)} %collective-permute-done.16.refs_3_, ...), custom_call_target="tpu_custom_call" | custom-call | tf_op jit(solution)/shard_map/assemble/pallas_call | solution.py:322
  (5 shorter events, 0.1 us)
Async XLA Ops:
  0.6 18.7 %copy-start.4 = (s32[32,2]{0,1:T(2,128)S(1)}, s32[32,2]{0,1:T(2,128)}, u32[]{:S(2)}) copy-start(s32[32,2]{0,1:T(2,128)} %param.11) | copy-start | bytes 772
  0.6 31.4 %copy-start.2 = (s32[2]{0:T(128)S(1)}, s32[2]{0:T(128)}, u32[]{:S(2)}) copy-start(s32[2]{0:T(128)} %refs_0_.2) | copy-start | bytes 28
  0.7 31.4 %copy-start = (bf16[2,512,384]{2,1,0:T(8,128)(2,1)S(1)}, bf16[2,512,384]{2,1,0:T(8,128)(2,1)}, u32[]{:S(2)}) copy-start(bf16[2,512,384]{2,1,0:T(8,128)(2,1)} %refs_2_.2) | copy-start | bytes 2359300
  0.7 76.6 %copy-start.3 = (s32[32]{0:T(128)S(1)}, s32[32]{0:T(128)}, u32[]{:S(2)}) copy-start(s32[32]{0:T(128)} %refs_0_.3) | copy-start | bytes 388
  0.7 76.6 %copy-start.1 = (bf16[512,384]{1,0:T(8,128)(2,1)S(1)}, bf16[512,384]{1,0:T(8,128)(2,1)}, u32[]{:S(2)}) copy-start(bf16[512,384]{1,0:T(8,128)(2,1)} %refs_2_.3) | copy-start | bytes 1179652
  2.5 8.6 %collective-permute-start = (bf16[3,64,384]{2,1,0:T(8,128)(2,1)}, bf16[3,64,384]{2,1,0:T(8,128)(2,1)S(1)}, u32[]{:S(2)}, u32[]{:S(2)}) collective-permute-start(bf16[3,64,384]{2,1,0:T(8,128)(2,1)} %get-tuple-element.13), channel_id=1, source_target_pairs={{192,0},{32,2},{0,4},{224,6},{200,8},{40,10},{8,12},{232,14},{208,... | collective-permute-start | bytes 442376 | tf_op jit(solution)/shard_map/ppermute | solution.py:268
  7.7 6.4 %collective-permute-start.1 = (bf16[3,64,384]{2,1,0:T(8,128)(2,1)}, bf16[3,64,384]{2,1,0:T(8,128)(2,1)S(1)}, u32[]{:S(2)}, u32[]{:S(2)}) collective-permute-start(bf16[3,64,384]{2,1,0:T(8,128)(2,1)} %get-tuple-element.14), channel_id=1, source_target_pairs={{192,1},{32,3},{0,5},{224,7},{200,9},{40,11},{8,13},{232,15},{208,... | collective-permute-start | bytes 442376 | tf_op jit(solution)/shard_map/ppermute | solution.py:268
  14.2 7.1 %collective-permute-start.4 = (bf16[3,64,384]{2,1,0:T(8,128)(2,1)S(1)}, bf16[3,64,384]{2,1,0:T(8,128)(2,1)S(1)}, u32[]{:S(2)}, u32[]{:S(2)}) collective-permute-start(bf16[3,64,384]{2,1,0:T(8,128)(2,1)S(1)} %add.8.refs_4_), channel_id=1, source_target_pairs={{0,24},{8,0},{16,8},{24,16},{32,56},{40,32},{48,40},{56,48},{64,88... | collective-permute-start | bytes 442376 | tf_op jit(solution)/shard_map/ppermute | solution.py:232
  17.0 7.9 %collective-permute-start.3 = (bf16[3,64,384]{2,1,0:T(8,128)(2,1)S(1)}, bf16[3,64,384]{2,1,0:T(8,128)(2,1)S(1)}, u32[]{:S(2)}, u32[]{:S(2)}) collective-permute-start(bf16[3,64,384]{2,1,0:T(8,128)(2,1)S(1)} %add.8.refs_4_), channel_id=1, source_target_pairs={{0,8},{8,16},{16,24},{24,0},{32,40},{40,48},{48,56},{56,32},{64,72... | collective-permute-start | bytes 442376 | tf_op jit(solution)/shard_map/ppermute | solution.py:232
  17.0 7.9 %collective-permute-start.2 = (bf16[3,64,384]{2,1,0:T(8,128)(2,1)S(1)}, bf16[3,64,384]{2,1,0:T(8,128)(2,1)S(1)}, u32[]{:S(2)}, u32[]{:S(2)}) collective-permute-start(bf16[3,64,384]{2,1,0:T(8,128)(2,1)S(1)} %add.8.refs_4_), channel_id=1, source_target_pairs={{0,16},{8,24},{16,0},{24,8},{32,48},{40,56},{48,32},{56,40},{64,80... | collective-permute-start | bytes 442376 | tf_op jit(solution)/shard_map/ppermute | solution.py:232
  25.0 7.1 %collective-permute-start.5 = (bf16[1,128,384]{2,1,0:T(8,128)(2,1)S(1)}, bf16[1,128,384]{2,1,0:T(8,128)(2,1)S(1)}, u32[]{:S(2)}, u32[]{:S(2)}) collective-permute-start(bf16[1,128,384]{2,1,0:T(8,128)(2,1)S(1)} %pad_maximum_fusion.2), channel_id=1, source_target_pairs={{0,32},{8,40},{16,240},{24,248},{32,64},{40,72},{48,16},{56,24},{6... | collective-permute-start | bytes 294920 | tf_op jit(solution)/shard_map/ppermute | solution.py:273
  34.2 8.1 %collective-permute-start.6 = (bf16[64,512]{1,0:T(8,128)(2,1)S(1)}, bf16[64,512]{1,0:T(8,128)(2,1)S(1)}, u32[]{:S(2)}, u32[]{:S(2)}) collective-permute-start(bf16[64,512]{1,0:T(8,128)(2,1)S(1)} %get-tuple-element.16), channel_id=1, source_target_pairs={{0,240},{8,248},{16,0},{24,8},{32,16},{40,24},{48,32},{56,40},{64,... | collective-permute-start | bytes 196616 | tf_op jit(solution)/shard_map/ppermute | solution.py:227
  40.0 4.6 %collective-permute-start.7 = (bf16[64,512]{1,0:T(8,128)(2,1)S(1)}, bf16[64,512]{1,0:T(8,128)(2,1)S(1)}, u32[]{:S(2)}, u32[]{:S(2)}) collective-permute-start(bf16[64,512]{1,0:T(8,128)(2,1)S(1)} %get-tuple-element.17), channel_id=1, source_target_pairs={{0,248},{8,0},{16,8},{24,16},{32,24},{40,32},{48,40},{56,48},{64,5... | collective-permute-start | bytes 196616 | tf_op jit(solution)/shard_map/ppermute | solution.py:227
  40.0 8.6 %collective-permute-start.8 = (bf16[64,512]{1,0:T(8,128)(2,1)S(1)}, bf16[64,512]{1,0:T(8,128)(2,1)S(1)}, u32[]{:S(2)}, u32[]{:S(2)}) collective-permute-start(bf16[64,512]{1,0:T(8,128)(2,1)S(1)} %get-tuple-element.19), channel_id=1, source_target_pairs={{0,8},{8,16},{16,24},{24,32},{32,40},{40,48},{48,56},{56,64},{64,7... | collective-permute-start | bytes 196616 | tf_op jit(solution)/shard_map/ppermute | solution.py:227
  42.0 7.9 %collective-permute-start.9 = (bf16[64,512]{1,0:T(8,128)(2,1)S(1)}, bf16[64,512]{1,0:T(8,128)(2,1)S(1)}, u32[]{:S(2)}, u32[]{:S(2)}) collective-permute-start(bf16[64,512]{1,0:T(8,128)(2,1)S(1)} %get-tuple-element.20), channel_id=1, source_target_pairs={{0,16},{8,24},{16,32},{24,40},{32,48},{40,56},{48,64},{56,72},{64,... | collective-permute-start | bytes 196616 | tf_op jit(solution)/shard_map/ppermute | solution.py:227
  42.3 15.8 %collective-permute-start.13 = (bf16[2,128,384]{2,1,0:T(8,128)(2,1)S(1)}, bf16[2,128,384]{2,1,0:T(8,128)(2,1)S(1)}, u32[]{:S(2)}, u32[]{:S(2)}) collective-permute-start(bf16[2,128,384]{2,1,0:T(8,128)(2,1)S(1)} %pad_maximum_fusion), channel_id=1, source_target_pairs={{0,32},{8,40},{16,240},{24,248},{32,64},{40,72},{48,16},{56,24},{6... | collective-permute-start | bytes 589832 | tf_op jit(solution)/shard_map/ppermute | solution.py:273
  50.3 4.2 %collective-permute-start.12 = (bf16[64,384]{1,0:T(8,128)(2,1)S(1)}, bf16[64,384]{1,0:T(8,128)(2,1)S(1)}, u32[]{:S(2)}, u32[]{:S(2)}) collective-permute-start(bf16[64,384]{1,0:T(8,128)(2,1)S(1)} %merge.1), channel_id=1, source_target_pairs={{0,24},{8,0},{16,8},{24,16},{32,56},{40,32},{48,40},{56,48},{64,88... | collective-permute-start | bytes 147464 | tf_op jit(solution)/shard_map/ppermute | solution.py:232
  50.4 5.7 %collective-permute-start.11 = (bf16[64,384]{1,0:T(8,128)(2,1)S(1)}, bf16[64,384]{1,0:T(8,128)(2,1)S(1)}, u32[]{:S(2)}, u32[]{:S(2)}) collective-permute-start(bf16[64,384]{1,0:T(8,128)(2,1)S(1)} %merge.1), channel_id=1, source_target_pairs={{0,16},{8,24},{16,0},{24,8},{32,48},{40,56},{48,32},{56,40},{64,80... | collective-permute-start | bytes 147464 | tf_op jit(solution)/shard_map/ppermute | solution.py:232
  52.7 5.3 %collective-permute-start.10 = (bf16[64,384]{1,0:T(8,128)(2,1)S(1)}, bf16[64,384]{1,0:T(8,128)(2,1)S(1)}, u32[]{:S(2)}, u32[]{:S(2)}) collective-permute-start(bf16[64,384]{1,0:T(8,128)(2,1)S(1)} %merge.1), channel_id=1, source_target_pairs={{0,8},{8,16},{16,24},{24,0},{32,40},{40,48},{48,56},{56,32},{64,72... | collective-permute-start | bytes 147464 | tf_op jit(solution)/shard_map/ppermute | solution.py:232
  58.1 11.8 %collective-permute-start.15 = (bf16[256,384]{1,0:T(8,128)(2,1)S(1)}, bf16[256,384]{1,0:T(8,128)(2,1)S(1)}, u32[]{:S(2)}, u32[]{:S(2)}) collective-permute-start(bf16[256,384]{1,0:T(8,128)(2,1)S(1)} %pad_maximum_fusion.1.refs_0_), channel_id=1, source_target_pairs={{0,64},{8,72},{16,80},{24,88},{32,96},{40,104},{48,112},{56,120},{... | collective-permute-start | bytes 589832 | tf_op jit(solution)/shard_map/ppermute | solution.py:227
  58.2 13.0 %collective-permute-start.14 = (bf16[256,384]{1,0:T(8,128)(2,1)S(1)}, bf16[256,384]{1,0:T(8,128)(2,1)S(1)}, u32[]{:S(2)}, u32[]{:S(2)}) collective-permute-start(bf16[256,384]{1,0:T(8,128)(2,1)S(1)} %pad_maximum_fusion.1.refs_0_), channel_id=1, source_target_pairs={{0,160},{8,168},{16,176},{24,184},{32,192},{40,200},{48,208},{56,2... | collective-permute-start | bytes 589832 | tf_op jit(solution)/shard_map/ppermute | solution.py:227
  60.5 20.3 %collective-permute-start.17 = (bf16[256,384]{1,0:T(8,128)(2,1)S(1)}, bf16[256,384]{1,0:T(8,128)(2,1)S(1)}, u32[]{:S(2)}, u32[]{:S(2)}) collective-permute-start(bf16[256,384]{1,0:T(8,128)(2,1)S(1)} %pad_maximum_fusion.1.refs_0_), channel_id=1, source_target_pairs={{0,32},{8,40},{16,48},{24,56},{32,64},{40,72},{48,80},{56,88},{64,... | collective-permute-start | bytes 589832 | tf_op jit(solution)/shard_map/ppermute | solution.py:227
  63.8 17.0 %collective-permute-start.16 = (bf16[256,384]{1,0:T(8,128)(2,1)S(1)}, bf16[256,384]{1,0:T(8,128)(2,1)S(1)}, u32[]{:S(2)}, u32[]{:S(2)}) collective-permute-start(bf16[256,384]{1,0:T(8,128)(2,1)S(1)} %pad_maximum_fusion.1.refs_0_), channel_id=1, source_target_pairs={{0,224},{8,232},{16,240},{24,248},{32,0},{40,8},{48,16},{56,24},{6... | collective-permute-start | bytes 589832 | tf_op jit(solution)/shard_map/ppermute | solution.py:227
  69.9 10.9 %collective-permute-start.20 = (bf16[256,384]{1,0:T(8,128)(2,1)S(1)}, bf16[256,384]{1,0:T(8,128)(2,1)S(1)}, u32[]{:S(2)}, u32[]{:S(2)}) collective-permute-start(bf16[256,384]{1,0:T(8,128)(2,1)S(1)} %collective-permute-done.15.refs_2_), channel_id=1, source_target_pairs={{0,32},{8,40},{16,48},{24,56},{32,64},{40,72},{48,80},{56,88},{64,... | collective-permute-start | bytes 589832 | tf_op jit(solution)/shard_map/ppermute | solution.py:227
  71.1 9.6 %collective-permute-start.19 = (bf16[256,384]{1,0:T(8,128)(2,1)S(1)}, bf16[256,384]{1,0:T(8,128)(2,1)S(1)}, u32[]{:S(2)}, u32[]{:S(2)}) collective-permute-start(bf16[256,384]{1,0:T(8,128)(2,1)S(1)} %collective-permute-done.14.refs_1_), channel_id=1, source_target_pairs={{0,32},{8,40},{16,48},{24,56},{32,64},{40,72},{48,80},{56,88},{64,... | collective-permute-start | bytes 589832 | tf_op jit(solution)/shard_map/ppermute | solution.py:227
  77.3 5.7 %collective-permute-start.18 = (bf16[256,384]{1,0:T(8,128)(2,1)S(1)}, bf16[256,384]{1,0:T(8,128)(2,1)S(1)}, u32[]{:S(2)}, u32[]{:S(2)}) collective-permute-start(bf16[256,384]{1,0:T(8,128)(2,1)S(1)} %collective-permute-done.14.refs_1_), channel_id=1, source_target_pairs={{0,224},{8,232},{16,240},{24,248},{32,0},{40,8},{48,16},{56,24},{6... | collective-permute-start | bytes 589832 | tf_op jit(solution)/shard_map/ppermute | solution.py:227

commit v4 on v3

--- a/solution.py
+++ b/solution.py
@@ -198,14 +198,11 @@
             out[rows, cols] = (o / total).astype(jnp.bfloat16)
 
 
-ZHELD = (0, 3, -2, 1, -1, 4, 2, -3)
-
-
-def assemble_kernel(*refs):
-    chunks, out, sems = refs[:8], refs[8], refs[9]
+def assemble_kernel(held, *refs):
+    chunks, (out, sems) = refs[: len(held)], refs[-2:]
     _, z, x = place()
     copies = []
-    for i, rel in enumerate(ZHELD):
+    for i, rel in enumerate(held):
         zz = lax.rem(z + rel + ZS, ZS)
         for k in range(XS):
             row = (zz * XS + lax.rem(x - k + XS, XS)) * ABS
@@ -318,16 +315,25 @@
 
     z3, zm2 = from_z(row, 3), from_z(row, -2)
     z1, zm1 = from_z(row, 1), from_z(row, -1)
+    z3, video_out = lax.optimization_barrier((z3, video_out))
     z4, z2, zm3 = from_z(z3, 1), from_z(z3, -1), from_z(zm2, -1)
-    audio_out = pl.pallas_call(
-        assemble_kernel,
-        out_shape=jax.ShapeDtypeStruct((ZS * XS * ABS, columns), bf16),
-        in_specs=[VMEM] * 8,
-        out_specs=ANY,
-        scratch_shapes=[pltpu.SemaphoreType.DMA((ZS * XS,))],
-        compiler_params=params(),
-        name="assemble",
-    )(row, z3, zm2, z1, zm1, z4, z2, zm3)
+    whole = jax.ShapeDtypeStruct((ZS * XS * ABS, columns), bf16)
+
+    def assembled(held, chunks, *before):
+        n = len(chunks)
+        return pl.pallas_call(
+            lambda *refs: assemble_kernel(held, *refs),
+            out_shape=whole,
+            in_specs=[VMEM] * n + [ANY] * len(before),
+            out_specs=ANY,
+            scratch_shapes=[pltpu.SemaphoreType.DMA((n * XS,))],
+            input_output_aliases={n: 0} if before else {},
+            compiler_params=params(),
+            name="assemble",
+        )(*chunks, *before)
+
+    early = assembled((0, 3, -2, 1, -1), (row, z3, zm2, z1, zm1))
+    audio_out = assembled((4, 2, -3), (z4, z2, zm3), early)
     return (video_out, audio_out)
 
 

time: 84.7 us -> 83.6 us (0.987)
  starting transfers between devices: 38.9 us -> 36.1 us
  waiting for transfers between devices: 35.3 us -> 36.5 us
    ppermute x11, starting transfers between devices: 19.9 us -> 17 us  [shifted(): return lax.ppermute(value, 'video', [(v, (v + step) % n) for v in range(n)])]
    ppermute x11, waiting for transfers between devices: 17.1 us -> 18.4 us  [shifted(): return lax.ppermute(value, 'video', [(v, (v + step) % n) for v in range(n)])]
    pallas_call x1 -> x2, Pallas kernels: 1.39 us -> 2 us  [assembled(): pl.pallas_call(lambda *refs: assemble_kernel(held, *refs), out_shape=whol...]
  transfers between devices with their start and end apart: 21 -> 21, of which waited for: 13 -> 13; matrix products, arithmetic and copies ran while one was open for 0% -> 0% of each run, Pallas kernels for 5% -> 6%
where the time goes in v4:
time: 83.6 us; the launch traced here: 83.4 us
  waiting for transfers between devices  36.5 us (44%)
  starting transfers between devices  36.1 us (43%)
  Pallas kernels  9.67 us (12%)
  between operations  0.94 us (1%)
    ppermute x11, waiting for transfers between devices, shifted(): return lax.ppermute(value, 'video', [(v, (v + step) % n) for v in range(n)])  18.4 us
    ppermute x11, starting transfers between devices, shifted(): return lax.ppermute(value, 'video', [(v, (v + step) % n) for v in range(n)])  17 us
    ppermute x6, waiting for transfers between devices, along_x(): return lax.ppermute(value, 'video', pairs)  10.8 us
    ppermute x2, starting transfers between devices, to_core(): return lax.ppermute(value, BOTH, pairs)  8.75 us
    ppermute x6, starting transfers between devices, along_x(): return lax.ppermute(value, 'video', pairs)  7.57 us
    ppermute x2, waiting for transfers between devices, between_lines(): return lax.ppermute(value, 'video', pairs)  4.27 us
    pallas_call x1, Pallas kernels, local(): pl.pallas_call(lambda *refs: video_kernel(scale, *refs), out_shape=jax.Sh...  3.45 us
    ppermute x2, waiting for transfers between devices, to_core(): return lax.ppermute(value, BOTH, pairs)  2.99 us
  transfers between devices with their start and end apart: 21, of which 13 were waited for; matrix products, arithmetic and copies ran while one was open for 0% of the time, Pallas kernels for 6%

profile of v4, /device:TPU:8, one launch (start us, length us, event | category | flops | bytes accessed | tf_op | source)
XLA Modules:
  0.0 83.4 jit_solution(490456168602622563)
XLA Ops:
  0.6 0.0 copy-start.4
  0.6 1.7 %pack.1 = (bf16[3,64,384]{2,1,0:T(8,128)(2,1)}, bf16[3,64,384]{2,1,0:T(8,128)(2,1)}) custom-call(bf16[3,256,3072]{2,1,0:T(8,128)(2,1)} %src.1), custom_call_target="tpu_custom_call" | custom-call | tf_op jit(solution)/shard_map/pack/pallas_call | solution.py:248
  2.4 0.0 copy-start
  2.4 0.0 copy-start.2
  2.4 5.3 %collective-permute-start = (bf16[3,64,384]{2,1,0:T(8,128)(2,1)}, bf16[3,64,384]{2,1,0:T(8,128)(2,1)S(1)}, u32[]{:S(2)}, u32[]{:S(2)}) collective-permute-start(bf16[3,64,384]{2,1,0:T(8,128)(2,1)} %get-tuple-element.15), channel_id=1, source_target_pairs={{192,0},{32,2},{0,4},{224,6},{200,8},{40,10},{8,12},{232,14},{208,... | collective-permute-start | bytes 442376 | tf_op jit(solution)/shard_map/ppermute | solution.py:265
  7.7 3.4 %collective-permute-start.1 = (bf16[3,64,384]{2,1,0:T(8,128)(2,1)}, bf16[3,64,384]{2,1,0:T(8,128)(2,1)S(1)}, u32[]{:S(2)}, u32[]{:S(2)}) collective-permute-start(bf16[3,64,384]{2,1,0:T(8,128)(2,1)} %get-tuple-element.16), channel_id=1, source_target_pairs={{192,1},{32,3},{0,5},{224,7},{200,9},{40,11},{8,13},{232,15},{208,... | collective-permute-start | bytes 442376 | tf_op jit(solution)/shard_map/ppermute | solution.py:265
  11.1 0.0 collective-permute-done
  11.2 3.0 %collective-permute-done.1 = bf16[3,64,384]{2,1,0:T(8,128)(2,1)S(1)} collective-permute-done((bf16[3,64,384]{2,1,0:T(8,128)(2,1)}, bf16[3,64,384]{2,1,0:T(8,128)(2,1)S(1)}, u32[]{:S(2)}, u32[]{:S(2)}) %collective-permute-start.1) | collective-permute-done | bytes 147488 | tf_op jit(solution)/shard_map/ppermute | solution.py:265
  14.2 2.8 %collective-permute-start.4 = (bf16[3,64,384]{2,1,0:T(8,128)(2,1)S(1)}, bf16[3,64,384]{2,1,0:T(8,128)(2,1)S(1)}, u32[]{:S(2)}, u32[]{:S(2)}) collective-permute-start(bf16[3,64,384]{2,1,0:T(8,128)(2,1)S(1)} %add.8.refs_4_), channel_id=1, source_target_pairs={{0,24},{8,0},{16,8},{24,16},{32,56},{40,32},{48,40},{56,48},{64,88... | collective-permute-start | bytes 442376 | tf_op jit(solution)/shard_map/ppermute | solution.py:229
  17.0 0.0 collective-permute-start.3
  17.0 2.3 %collective-permute-start.2 = (bf16[3,64,384]{2,1,0:T(8,128)(2,1)S(1)}, bf16[3,64,384]{2,1,0:T(8,128)(2,1)S(1)}, u32[]{:S(2)}, u32[]{:S(2)}) collective-permute-start(bf16[3,64,384]{2,1,0:T(8,128)(2,1)S(1)} %add.8.refs_4_), channel_id=1, source_target_pairs={{0,16},{8,24},{16,0},{24,8},{32,48},{40,56},{48,32},{56,40},{64,80... | collective-permute-start | bytes 442376 | tf_op jit(solution)/shard_map/ppermute | solution.py:229
  19.3 0.0 copy-done.4
  19.3 0.1 copy.9.refs_1_
  19.4 1.9 %collective-permute-done.4.refs_7_ = bf16[3,64,384]{2,1,0:T(8,128)(2,1)S(1)} collective-permute-done((bf16[3,64,384]{2,1,0:T(8,128)(2,1)S(1)}, bf16[3,64,384]{2,1,0:T(8,128)(2,1)S(1)}, u32[]{:S(2)}, u32[]{:S(2)}) %collective-permute-start.4) | collective-permute-done | bytes 147488 | tf_op jit(solution)/shard_map/ppermute | solution.py:229
  21.3 3.7 %collective-permute-done.3.refs_5_ = bf16[3,64,384]{2,1,0:T(8,128)(2,1)S(1)} collective-permute-done((bf16[3,64,384]{2,1,0:T(8,128)(2,1)S(1)}, bf16[3,64,384]{2,1,0:T(8,128)(2,1)S(1)}, u32[]{:S(2)}, u32[]{:S(2)}) %collective-permute-start.3) | collective-permute-done | bytes 147488 | tf_op jit(solution)/shard_map/ppermute | solution.py:229
  25.0 0.0 collective-permute-done.2.refs_6_
  25.0 0.0 copy-start.1
  25.0 0.0 copy-start.3
  25.0 2.8 %collective-permute-start.5 = (bf16[1,128,384]{2,1,0:T(8,128)(2,1)S(1)}, bf16[1,128,384]{2,1,0:T(8,128)(2,1)S(1)}, u32[]{:S(2)}, u32[]{:S(2)}) collective-permute-start(bf16[1,128,384]{2,1,0:T(8,128)(2,1)S(1)} %pad_maximum_fusion.2), channel_id=1, source_target_pairs={{0,32},{8,40},{16,240},{24,248},{32,64},{40,72},{48,16},{56,24},{6... | collective-permute-start | bytes 294920 | tf_op jit(solution)/shard_map/ppermute | solution.py:270
  27.9 4.3 %collective-permute-done.5.refs_3_ = bf16[1,128,384]{2,1,0:T(8,128)(2,1)S(1)} collective-permute-done((bf16[1,128,384]{2,1,0:T(8,128)(2,1)S(1)}, bf16[1,128,384]{2,1,0:T(8,128)(2,1)S(1)}, u32[]{:S(2)}, u32[]{:S(2)}) %collective-permute-start.5) | collective-permute-done | bytes 98336 | tf_op jit(solution)/shard_map/ppermute | solution.py:270
  32.1 0.0 copy-done
  32.1 0.0 copy-done.2
  32.1 2.1 %audio_side.1 = (bf16[64,512]{1,0:T(8,128)(2,1)S(1)}, bf16[64,512]{1,0:T(8,128)(2,1)S(1)}, bf16[64,512]{1,0:T(8,128)(2,1)S(1)}, bf16[64,512]{1,0:T(8,128)(2,1)S(1)}, bf16[64,512]{1,0:T(8,128)(2,1)S(1)}) custom-call(s32[2]{0:T(128)S(1)} %copy-done.2, s32[32,2]{1,0:T(8,128)S(1)} %copy.9.refs_1_, bf16[2,512,384]{2,1,0:T(8,128)(2,1)S(1)} %copy-done, ...), custom_call_target="tpu_custom_call" | custom-call | tf_op jit(solution)/shard_map/audio_side/pallas_call | solution.py:280
  34.2 5.8 %collective-permute-start.6 = (bf16[64,512]{1,0:T(8,128)(2,1)S(1)}, bf16[64,512]{1,0:T(8,128)(2,1)S(1)}, u32[]{:S(2)}, u32[]{:S(2)}) collective-permute-start(bf16[64,512]{1,0:T(8,128)(2,1)S(1)} %get-tuple-element.18), channel_id=1, source_target_pairs={{0,240},{8,248},{16,0},{24,8},{32,16},{40,24},{48,32},{56,40},{64,... | collective-permute-start | bytes 196616 | tf_op jit(solution)/shard_map/ppermute | solution.py:224
  40.0 0.0 collective-permute-start.7
  40.0 2.0 %collective-permute-start.8 = (bf16[64,512]{1,0:T(8,128)(2,1)S(1)}, bf16[64,512]{1,0:T(8,128)(2,1)S(1)}, u32[]{:S(2)}, u32[]{:S(2)}) collective-permute-start(bf16[64,512]{1,0:T(8,128)(2,1)S(1)} %get-tuple-element.21), channel_id=1, source_target_pairs={{0,8},{8,16},{16,24},{24,32},{32,40},{40,48},{48,56},{56,64},{64,7... | collective-permute-start | bytes 196616 | tf_op jit(solution)/shard_map/ppermute | solution.py:224
  42.0 0.3 collective-permute-start.9
  42.3 0.0 collective-permute-start.13
  42.3 0.0 collective-permute-done.6.refs_0_
  42.3 2.3 %collective-permute-done.7.refs_1_ = bf16[64,512]{1,0:T(8,128)(2,1)S(1)} collective-permute-done((bf16[64,512]{1,0:T(8,128)(2,1)S(1)}, bf16[64,512]{1,0:T(8,128)(2,1)S(1)}, u32[]{:S(2)}, u32[]{:S(2)}) %collective-permute-start.7) | collective-permute-done | bytes 65568 | tf_op jit(solution)/shard_map/ppermute | solution.py:224
  44.6 4.0 %collective-permute-done.8.refs_3_ = bf16[64,512]{1,0:T(8,128)(2,1)S(1)} collective-permute-done((bf16[64,512]{1,0:T(8,128)(2,1)S(1)}, bf16[64,512]{1,0:T(8,128)(2,1)S(1)}, u32[]{:S(2)}, u32[]{:S(2)}) %collective-permute-start.8) | collective-permute-done | bytes 65568 | tf_op jit(solution)/shard_map/ppermute | solution.py:224
  48.6 1.3 %collective-permute-done.9.refs_4_ = bf16[64,512]{1,0:T(8,128)(2,1)S(1)} collective-permute-done((bf16[64,512]{1,0:T(8,128)(2,1)S(1)}, bf16[64,512]{1,0:T(8,128)(2,1)S(1)}, u32[]{:S(2)}, u32[]{:S(2)}) %collective-permute-start.9) | collective-permute-done | bytes 65568 | tf_op jit(solution)/shard_map/ppermute | solution.py:224
  49.9 0.4 merge.1
  50.3 0.1 collective-permute-start.12
  50.4 2.4 %collective-permute-start.11 = (bf16[64,384]{1,0:T(8,128)(2,1)S(1)}, bf16[64,384]{1,0:T(8,128)(2,1)S(1)}, u32[]{:S(2)}, u32[]{:S(2)}) collective-permute-start(bf16[64,384]{1,0:T(8,128)(2,1)S(1)} %merge.1), channel_id=1, source_target_pairs={{0,16},{8,24},{16,0},{24,8},{32,48},{40,56},{48,32},{56,40},{64,80... | collective-permute-start | bytes 147464 | tf_op jit(solution)/shard_map/ppermute | solution.py:229
  52.8 0.0 collective-permute-start.10
  52.8 1.7 %collective-permute-done.12 = bf16[64,384]{1,0:T(8,128)(2,1)S(1)} collective-permute-done((bf16[64,384]{1,0:T(8,128)(2,1)S(1)}, bf16[64,384]{1,0:T(8,128)(2,1)S(1)}, u32[]{:S(2)}, u32[]{:S(2)}) %collective-permute-start.12) | collective-permute-done | bytes 49184 | tf_op jit(solution)/shard_map/ppermute | solution.py:229
  54.5 1.6 %collective-permute-done.11 = bf16[64,384]{1,0:T(8,128)(2,1)S(1)} collective-permute-done((bf16[64,384]{1,0:T(8,128)(2,1)S(1)}, bf16[64,384]{1,0:T(8,128)(2,1)S(1)}, u32[]{:S(2)}, u32[]{:S(2)}) %collective-permute-start.11) | collective-permute-done | bytes 49184 | tf_op jit(solution)/shard_map/ppermute | solution.py:229
  56.1 2.0 %collective-permute-done.10 = bf16[64,384]{1,0:T(8,128)(2,1)S(1)} collective-permute-done((bf16[64,384]{1,0:T(8,128)(2,1)S(1)}, bf16[64,384]{1,0:T(8,128)(2,1)S(1)}, u32[]{:S(2)}, u32[]{:S(2)}) %collective-permute-start.10) | collective-permute-done | bytes 49184 | tf_op jit(solution)/shard_map/ppermute | solution.py:229
  58.1 0.0 collective-permute-done.13.refs_3_
  58.1 2.0 %collective-permute-start.14 = (bf16[256,384]{1,0:T(8,128)(2,1)S(1)}, bf16[256,384]{1,0:T(8,128)(2,1)S(1)}, u32[]{:S(2)}, u32[]{:S(2)}) collective-permute-start(bf16[256,384]{1,0:T(8,128)(2,1)S(1)} %pad_maximum_fusion.1.refs_0_), channel_id=1, source_target_pairs={{0,160},{8,168},{16,176},{24,184},{32,192},{40,200},{48,208},{56,2... | collective-permute-start | bytes 589832 | tf_op jit(solution)/shard_map/ppermute | solution.py:224
  60.2 0.3 collective-permute-start.17
  60.5 2.1 %collective-permute-start.20 = (bf16[256,384]{1,0:T(8,128)(2,1)S(1)}, bf16[256,384]{1,0:T(8,128)(2,1)S(1)}, u32[]{:S(2)}, u32[]{:S(2)}) collective-permute-start(bf16[256,384]{1,0:T(8,128)(2,1)S(1)} %pad_maximum_fusion.1.refs_0_), channel_id=1, source_target_pairs={{0,32},{8,40},{16,48},{24,56},{32,64},{40,72},{48,80},{56,88},{64,... | collective-permute-start | bytes 589832 | tf_op jit(solution)/shard_map/ppermute | solution.py:224
  62.6 1.1 %collective-permute-start.19 = (bf16[256,384]{1,0:T(8,128)(2,1)S(1)}, bf16[256,384]{1,0:T(8,128)(2,1)S(1)}, u32[]{:S(2)}, u32[]{:S(2)}) collective-permute-start(bf16[256,384]{1,0:T(8,128)(2,1)S(1)} %pad_maximum_fusion.1.refs_0_), channel_id=1, source_target_pairs={{0,224},{8,232},{16,240},{24,248},{32,0},{40,8},{48,16},{56,24},{6... | collective-permute-start | bytes 589832 | tf_op jit(solution)/shard_map/ppermute | solution.py:224
  63.7 0.0 copy-done.1
  63.7 0.0 copy-done.3
  63.7 3.4 %video_side.1 = bf16[512,384]{1,0:T(8,128)(2,1)} custom-call(s32[32]{0:T(128)S(1)} %copy-done.3, s32[32,2]{1,0:T(8,128)S(1)} %copy.9.refs_1_, bf16[512,384]{1,0:T(8,128)(2,1)S(1)} %copy-done.1, bf16[2,128,384]{2,1,0:T(8,128)(2,1)S(1)} %collective-permute-done.13.refs_3_, bf16[3,64,384]{2,1,0:T(8,128)(2,1)S(1)} %add.8.refs_4_, ...), custom_call_target="tpu_custom_call" | custom-call | tf_op jit(solution)/shard_map/video_side/pallas_call | solution.py:306
  67.2 6.2 %collective-permute-done.14.refs_1_ = bf16[256,384]{1,0:T(8,128)(2,1)S(1)} collective-permute-done((bf16[256,384]{1,0:T(8,128)(2,1)S(1)}, bf16[256,384]{1,0:T(8,128)(2,1)S(1)}, u32[]{:S(2)}, u32[]{:S(2)}) %collective-permute-start.14) | collective-permute-done | bytes 196640 | tf_op jit(solution)/shard_map/ppermute | solution.py:224
  73.4 0.0 collective-permute-done.17.refs_2_
  73.4 0.0 collective-permute-start.18
  73.4 0.0 collective-permute-start.16
  73.4 3.3 %collective-permute-start.15 = (bf16[256,384]{1,0:T(8,128)(2,1)S(1)}, bf16[256,384]{1,0:T(8,128)(2,1)S(1)}, u32[]{:S(2)}, u32[]{:S(2)}) collective-permute-start(bf16[256,384]{1,0:T(8,128)(2,1)S(1)} %collective-permute-done.14.refs_1_), channel_id=1, source_target_pairs={{0,224},{8,232},{16,240},{24,248},{32,0},{40,8},{48,16},{56,24},{6... | collective-permute-start | bytes 589832 | tf_op jit(solution)/shard_map/ppermute | solution.py:224
  76.7 0.0 collective-permute-done.20.refs_4_
  76.7 0.0 collective-permute-done.19.refs_3_
  76.7 1.1 %assemble.2.refs_3_ = bf16[2048,384]{1,0:T(8,128)(2,1)} custom-call(bf16[256,384]{1,0:T(8,128)(2,1)S(1)} %pad_maximum_fusion.1.refs_0_, bf16[256,384]{1,0:T(8,128)(2,1)S(1)} %collective-permute-done.14.refs_1_, bf16[256,384]{1,0:T(8,128)(2,1)S(1)} %collective-permute-done.17.refs_2_, bf16[256,384]{1,0:T(8,128)(2,1)S(1)} %collective-permute-done.19.refs_3_, ...), custom_call_target="tpu_custom_call" | custom-call | tf_op jit(solution)/shard_map/assemble/pallas_call | solution.py:324
  77.8 2.5 %collective-permute-done.18.refs_2_ = bf16[256,384]{1,0:T(8,128)(2,1)S(1)} collective-permute-done((bf16[256,384]{1,0:T(8,128)(2,1)S(1)}, bf16[256,384]{1,0:T(8,128)(2,1)S(1)}, u32[]{:S(2)}, u32[]{:S(2)}) %collective-permute-start.18) | collective-permute-done | bytes 196640 | tf_op jit(solution)/shard_map/ppermute | solution.py:224
  80.3 2.1 %collective-permute-done.16.refs_1_ = bf16[256,384]{1,0:T(8,128)(2,1)S(1)} collective-permute-done((bf16[256,384]{1,0:T(8,128)(2,1)S(1)}, bf16[256,384]{1,0:T(8,128)(2,1)S(1)}, u32[]{:S(2)}, u32[]{:S(2)}) %collective-permute-start.16) | collective-permute-done | bytes 196640 | tf_op jit(solution)/shard_map/ppermute | solution.py:224
  82.4 0.0 collective-permute-done.15.refs_0_
  82.4 0.9 %assemble.3 = bf16[2048,384]{1,0:T(8,128)(2,1)} custom-call(bf16[256,384]{1,0:T(8,128)(2,1)S(1)} %collective-permute-done.15.refs_0_, bf16[256,384]{1,0:T(8,128)(2,1)S(1)} %collective-permute-done.16.refs_1_, bf16[256,384]{1,0:T(8,128)(2,1)S(1)} %collective-permute-done.18.refs_2_, bf16[2048,384]{1,0:T(8,128)(2,1)} %assemble.2.refs_3_), custom_call_target="tpu_custom_call", output_to_operand_aliasing={{}: (3, {})} | custom-call | tf_op jit(solution)/shard_map/assemble/pallas_call | solution.py:324
  (5 shorter events, 0.1 us)
Async XLA Ops:
  0.6 18.7 %copy-start.4 = (s32[32,2]{0,1:T(2,128)S(1)}, s32[32,2]{0,1:T(2,128)}, u32[]{:S(2)}) copy-start(s32[32,2]{0,1:T(2,128)} %param.11) | copy-start | bytes 772
  2.4 29.8 %copy-start = (bf16[2,512,384]{2,1,0:T(8,128)(2,1)S(1)}, bf16[2,512,384]{2,1,0:T(8,128)(2,1)}, u32[]{:S(2)}) copy-start(bf16[2,512,384]{2,1,0:T(8,128)(2,1)} %refs_2_.2) | copy-start | bytes 2359300
  2.4 29.8 %copy-start.2 = (s32[2]{0:T(128)S(1)}, s32[2]{0:T(128)}, u32[]{:S(2)}) copy-start(s32[2]{0:T(128)} %refs_0_.2) | copy-start | bytes 28
  2.4 8.8 %collective-permute-start = (bf16[3,64,384]{2,1,0:T(8,128)(2,1)}, bf16[3,64,384]{2,1,0:T(8,128)(2,1)S(1)}, u32[]{:S(2)}, u32[]{:S(2)}) collective-permute-start(bf16[3,64,384]{2,1,0:T(8,128)(2,1)} %get-tuple-element.15), channel_id=1, source_target_pairs={{192,0},{32,2},{0,4},{224,6},{200,8},{40,10},{8,12},{232,14},{208,... | collective-permute-start | bytes 442376 | tf_op jit(solution)/shard_map/ppermute | solution.py:265
  7.7 6.4 %collective-permute-start.1 = (bf16[3,64,384]{2,1,0:T(8,128)(2,1)}, bf16[3,64,384]{2,1,0:T(8,128)(2,1)S(1)}, u32[]{:S(2)}, u32[]{:S(2)}) collective-permute-start(bf16[3,64,384]{2,1,0:T(8,128)(2,1)} %get-tuple-element.16), channel_id=1, source_target_pairs={{192,1},{32,3},{0,5},{224,7},{200,9},{40,11},{8,13},{232,15},{208,... | collective-permute-start | bytes 442376 | tf_op jit(solution)/shard_map/ppermute | solution.py:265
  14.2 7.1 %collective-permute-start.4 = (bf16[3,64,384]{2,1,0:T(8,128)(2,1)S(1)}, bf16[3,64,384]{2,1,0:T(8,128)(2,1)S(1)}, u32[]{:S(2)}, u32[]{:S(2)}) collective-permute-start(bf16[3,64,384]{2,1,0:T(8,128)(2,1)S(1)} %add.8.refs_4_), channel_id=1, source_target_pairs={{0,24},{8,0},{16,8},{24,16},{32,56},{40,32},{48,40},{56,48},{64,88... | collective-permute-start | bytes 442376 | tf_op jit(solution)/shard_map/ppermute | solution.py:229
  17.0 7.9 %collective-permute-start.3 = (bf16[3,64,384]{2,1,0:T(8,128)(2,1)S(1)}, bf16[3,64,384]{2,1,0:T(8,128)(2,1)S(1)}, u32[]{:S(2)}, u32[]{:S(2)}) collective-permute-start(bf16[3,64,384]{2,1,0:T(8,128)(2,1)S(1)} %add.8.refs_4_), channel_id=1, source_target_pairs={{0,8},{8,16},{16,24},{24,0},{32,40},{40,48},{48,56},{56,32},{64,72... | collective-permute-start | bytes 442376 | tf_op jit(solution)/shard_map/ppermute | solution.py:229
  17.0 7.9 %collective-permute-start.2 = (bf16[3,64,384]{2,1,0:T(8,128)(2,1)S(1)}, bf16[3,64,384]{2,1,0:T(8,128)(2,1)S(1)}, u32[]{:S(2)}, u32[]{:S(2)}) collective-permute-start(bf16[3,64,384]{2,1,0:T(8,128)(2,1)S(1)} %add.8.refs_4_), channel_id=1, source_target_pairs={{0,16},{8,24},{16,0},{24,8},{32,48},{40,56},{48,32},{56,40},{64,80... | collective-permute-start | bytes 442376 | tf_op jit(solution)/shard_map/ppermute | solution.py:229
  25.0 38.7 %copy-start.1 = (bf16[512,384]{1,0:T(8,128)(2,1)S(1)}, bf16[512,384]{1,0:T(8,128)(2,1)}, u32[]{:S(2)}) copy-start(bf16[512,384]{1,0:T(8,128)(2,1)} %refs_2_.3) | copy-start | bytes 1179652
  25.0 38.7 %copy-start.3 = (s32[32]{0:T(128)S(1)}, s32[32]{0:T(128)}, u32[]{:S(2)}) copy-start(s32[32]{0:T(128)} %refs_0_.3) | copy-start | bytes 388
  25.0 7.1 %collective-permute-start.5 = (bf16[1,128,384]{2,1,0:T(8,128)(2,1)S(1)}, bf16[1,128,384]{2,1,0:T(8,128)(2,1)S(1)}, u32[]{:S(2)}, u32[]{:S(2)}) collective-permute-start(bf16[1,128,384]{2,1,0:T(8,128)(2,1)S(1)} %pad_maximum_fusion.2), channel_id=1, source_target_pairs={{0,32},{8,40},{16,240},{24,248},{32,64},{40,72},{48,16},{56,24},{6... | collective-permute-start | bytes 294920 | tf_op jit(solution)/shard_map/ppermute | solution.py:270
  34.2 8.1 %collective-permute-start.6 = (bf16[64,512]{1,0:T(8,128)(2,1)S(1)}, bf16[64,512]{1,0:T(8,128)(2,1)S(1)}, u32[]{:S(2)}, u32[]{:S(2)}) collective-permute-start(bf16[64,512]{1,0:T(8,128)(2,1)S(1)} %get-tuple-element.18), channel_id=1, source_target_pairs={{0,240},{8,248},{16,0},{24,8},{32,16},{40,24},{48,32},{56,40},{64,... | collective-permute-start | bytes 196616 | tf_op jit(solution)/shard_map/ppermute | solution.py:224
  40.0 4.6 %collective-permute-start.7 = (bf16[64,512]{1,0:T(8,128)(2,1)S(1)}, bf16[64,512]{1,0:T(8,128)(2,1)S(1)}, u32[]{:S(2)}, u32[]{:S(2)}) collective-permute-start(bf16[64,512]{1,0:T(8,128)(2,1)S(1)} %get-tuple-element.19), channel_id=1, source_target_pairs={{0,248},{8,0},{16,8},{24,16},{32,24},{40,32},{48,40},{56,48},{64,5... | collective-permute-start | bytes 196616 | tf_op jit(solution)/shard_map/ppermute | solution.py:224
  40.0 8.6 %collective-permute-start.8 = (bf16[64,512]{1,0:T(8,128)(2,1)S(1)}, bf16[64,512]{1,0:T(8,128)(2,1)S(1)}, u32[]{:S(2)}, u32[]{:S(2)}) collective-permute-start(bf16[64,512]{1,0:T(8,128)(2,1)S(1)} %get-tuple-element.21), channel_id=1, source_target_pairs={{0,8},{8,16},{16,24},{24,32},{32,40},{40,48},{48,56},{56,64},{64,7... | collective-permute-start | bytes 196616 | tf_op jit(solution)/shard_map/ppermute | solution.py:224
  42.0 7.9 %collective-permute-start.9 = (bf16[64,512]{1,0:T(8,128)(2,1)S(1)}, bf16[64,512]{1,0:T(8,128)(2,1)S(1)}, u32[]{:S(2)}, u32[]{:S(2)}) collective-permute-start(bf16[64,512]{1,0:T(8,128)(2,1)S(1)} %get-tuple-element.22), channel_id=1, source_target_pairs={{0,16},{8,24},{16,32},{24,40},{32,48},{40,56},{48,64},{56,72},{64,... | collective-permute-start | bytes 196616 | tf_op jit(solution)/shard_map/ppermute | solution.py:224
  42.3 15.8 %collective-permute-start.13 = (bf16[2,128,384]{2,1,0:T(8,128)(2,1)S(1)}, bf16[2,128,384]{2,1,0:T(8,128)(2,1)S(1)}, u32[]{:S(2)}, u32[]{:S(2)}) collective-permute-start(bf16[2,128,384]{2,1,0:T(8,128)(2,1)S(1)} %pad_maximum_fusion), channel_id=1, source_target_pairs={{0,32},{8,40},{16,240},{24,248},{32,64},{40,72},{48,16},{56,24},{6... | collective-permute-start | bytes 589832 | tf_op jit(solution)/shard_map/ppermute | solution.py:270
  50.3 4.2 %collective-permute-start.12 = (bf16[64,384]{1,0:T(8,128)(2,1)S(1)}, bf16[64,384]{1,0:T(8,128)(2,1)S(1)}, u32[]{:S(2)}, u32[]{:S(2)}) collective-permute-start(bf16[64,384]{1,0:T(8,128)(2,1)S(1)} %merge.1), channel_id=1, source_target_pairs={{0,24},{8,0},{16,8},{24,16},{32,56},{40,32},{48,40},{56,48},{64,88... | collective-permute-start | bytes 147464 | tf_op jit(solution)/shard_map/ppermute | solution.py:229
  50.4 5.7 %collective-permute-start.11 = (bf16[64,384]{1,0:T(8,128)(2,1)S(1)}, bf16[64,384]{1,0:T(8,128)(2,1)S(1)}, u32[]{:S(2)}, u32[]{:S(2)}) collective-permute-start(bf16[64,384]{1,0:T(8,128)(2,1)S(1)} %merge.1), channel_id=1, source_target_pairs={{0,16},{8,24},{16,0},{24,8},{32,48},{40,56},{48,32},{56,40},{64,80... | collective-permute-start | bytes 147464 | tf_op jit(solution)/shard_map/ppermute | solution.py:229
  52.8 5.3 %collective-permute-start.10 = (bf16[64,384]{1,0:T(8,128)(2,1)S(1)}, bf16[64,384]{1,0:T(8,128)(2,1)S(1)}, u32[]{:S(2)}, u32[]{:S(2)}) collective-permute-start(bf16[64,384]{1,0:T(8,128)(2,1)S(1)} %merge.1), channel_id=1, source_target_pairs={{0,8},{8,16},{16,24},{24,0},{32,40},{40,48},{48,56},{56,32},{64,72... | collective-permute-start | bytes 147464 | tf_op jit(solution)/shard_map/ppermute | solution.py:229
  58.1 15.3 %collective-permute-start.14 = (bf16[256,384]{1,0:T(8,128)(2,1)S(1)}, bf16[256,384]{1,0:T(8,128)(2,1)S(1)}, u32[]{:S(2)}, u32[]{:S(2)}) collective-permute-start(bf16[256,384]{1,0:T(8,128)(2,1)S(1)} %pad_maximum_fusion.1.refs_0_), channel_id=1, source_target_pairs={{0,160},{8,168},{16,176},{24,184},{32,192},{40,200},{48,208},{56,2... | collective-permute-start | bytes 589832 | tf_op jit(solution)/shard_map/ppermute | solution.py:224
  60.2 13.2 %collective-permute-start.17 = (bf16[256,384]{1,0:T(8,128)(2,1)S(1)}, bf16[256,384]{1,0:T(8,128)(2,1)S(1)}, u32[]{:S(2)}, u32[]{:S(2)}) collective-permute-start(bf16[256,384]{1,0:T(8,128)(2,1)S(1)} %pad_maximum_fusion.1.refs_0_), channel_id=1, source_target_pairs={{0,64},{8,72},{16,80},{24,88},{32,96},{40,104},{48,112},{56,120},{... | collective-permute-start | bytes 589832 | tf_op jit(solution)/shard_map/ppermute | solution.py:224
  60.5 16.2 %collective-permute-start.20 = (bf16[256,384]{1,0:T(8,128)(2,1)S(1)}, bf16[256,384]{1,0:T(8,128)(2,1)S(1)}, u32[]{:S(2)}, u32[]{:S(2)}) collective-permute-start(bf16[256,384]{1,0:T(8,128)(2,1)S(1)} %pad_maximum_fusion.1.refs_0_), channel_id=1, source_target_pairs={{0,32},{8,40},{16,48},{24,56},{32,64},{40,72},{48,80},{56,88},{64,... | collective-permute-start | bytes 589832 | tf_op jit(solution)/shard_map/ppermute | solution.py:224
  62.6 14.1 %collective-permute-start.19 = (bf16[256,384]{1,0:T(8,128)(2,1)S(1)}, bf16[256,384]{1,0:T(8,128)(2,1)S(1)}, u32[]{:S(2)}, u32[]{:S(2)}) collective-permute-start(bf16[256,384]{1,0:T(8,128)(2,1)S(1)} %pad_maximum_fusion.1.refs_0_), channel_id=1, source_target_pairs={{0,224},{8,232},{16,240},{24,248},{32,0},{40,8},{48,16},{56,24},{6... | collective-permute-start | bytes 589832 | tf_op jit(solution)/shard_map/ppermute | solution.py:224
  73.4 6.9 %collective-permute-start.18 = (bf16[256,384]{1,0:T(8,128)(2,1)S(1)}, bf16[256,384]{1,0:T(8,128)(2,1)S(1)}, u32[]{:S(2)}, u32[]{:S(2)}) collective-permute-start(bf16[256,384]{1,0:T(8,128)(2,1)S(1)} %collective-permute-done.17.refs_2_), channel_id=1, source_target_pairs={{0,32},{8,40},{16,48},{24,56},{32,64},{40,72},{48,80},{56,88},{64,... | collective-permute-start | bytes 589832 | tf_op jit(solution)/shard_map/ppermute | solution.py:224
  73.4 9.0 %collective-permute-start.16 = (bf16[256,384]{1,0:T(8,128)(2,1)S(1)}, bf16[256,384]{1,0:T(8,128)(2,1)S(1)}, u32[]{:S(2)}, u32[]{:S(2)}) collective-permute-start(bf16[256,384]{1,0:T(8,128)(2,1)S(1)} %collective-permute-done.14.refs_1_), channel_id=1, source_target_pairs={{0,32},{8,40},{16,48},{24,56},{32,64},{40,72},{48,80},{56,88},{64,... | collective-permute-start | bytes 589832 | tf_op jit(solution)/shard_map/ppermute | solution.py:224
  73.4 9.0 %collective-permute-start.15 = (bf16[256,384]{1,0:T(8,128)(2,1)S(1)}, bf16[256,384]{1,0:T(8,128)(2,1)S(1)}, u32[]{:S(2)}, u32[]{:S(2)}) collective-permute-start(bf16[256,384]{1,0:T(8,128)(2,1)S(1)} %collective-permute-done.14.refs_1_), channel_id=1, source_target_pairs={{0,224},{8,232},{16,240},{24,248},{32,0},{40,8},{48,16},{56,24},{6... | collective-permute-start | bytes 589832 | tf_op jit(solution)/shard_map/ppermute | solution.py:224

commit v5 on v4

--- a/solution.py
+++ b/solution.py
@@ -273,10 +273,15 @@
     slots = [own] + [along_x(own, k) for k in range(1, XS)]
 
     odd = lax.axis_index("video") % 2 == 1
-    near = [jnp.where(odd, slots[at + 2], slots[at + 1]) for at in range(REACH)]
-    near = jnp.concatenate(near, axis=1)
-    edge, near_kv = lax.optimization_barrier((between_lines(near[:1], XS), near[1:]))
-    edge_kv = between_lines(near_kv, XS)
+
+    def near(held):
+        pairs = [jnp.where(odd, held[at + 2], held[at + 1]) for at in range(REACH)]
+        return between_lines(jnp.concatenate(pairs, axis=1), XS)
+
+    edge, *later_kv = lax.optimization_barrier(
+        (near([slot[:1] for slot in slots]), *[slot[1:] for slot in slots])
+    )
+    edge_kv = near(later_kv)
     parts = pl.pallas_call(
         lambda *refs: audio_kernel(scale, *refs),
         out_shape=(jax.ShapeDtypeStruct((ABS, columns + 128), bf16),) * 5,

time: 83.6 us -> 83.6 us (level)
  no operation moved by 1% of the time
where the time goes in v5:
time: 83.6 us; the launch traced here: 83.4 us
  starting transfers between devices  36.2 us (43%)
  waiting for transfers between devices  36.2 us (43%)
  Pallas kernels  9.67 us (12%)
  between operations  0.99 us (1%)
    ppermute x11, waiting for transfers between devices, shifted(): return lax.ppermute(value, 'video', [(v, (v + step) % n) for v in range(n)])  18.2 us
    ppermute x11, starting transfers between devices, shifted(): return lax.ppermute(value, 'video', [(v, (v + step) % n) for v in range(n)])  17 us
    ppermute x6, waiting for transfers between devices, along_x(): return lax.ppermute(value, 'video', pairs)  10.9 us
    ppermute x2, starting transfers between devices, to_core(): return lax.ppermute(value, BOTH, pairs)  8.75 us
    ppermute x6, starting transfers between devices, along_x(): return lax.ppermute(value, 'video', pairs)  7.56 us
    ppermute x2, waiting for transfers between devices, between_lines(): return lax.ppermute(value, 'video', pairs)  4.12 us
    pallas_call x1, Pallas kernels, local(): pl.pallas_call(lambda *refs: video_kernel(scale, *refs), out_shape=jax.Sh...  3.45 us
    ppermute x2, waiting for transfers between devices, to_core(): return lax.ppermute(value, BOTH, pairs)  2.99 us
  transfers between devices with their start and end apart: 21, of which 13 were waited for; matrix products, arithmetic and copies ran while one was open for 0% of the time, Pallas kernels for 6%

profile of v5, /device:TPU:8, one launch (start us, length us, event | category | flops | bytes accessed | tf_op | source)
XLA Modules:
  0.0 83.4 jit_solution(15487662391343268335)
XLA Ops:
  0.6 0.0 copy-start.4
  0.6 0.0 copy-start.2
  0.7 1.7 %pack.1 = (bf16[3,64,384]{2,1,0:T(8,128)(2,1)}, bf16[3,64,384]{2,1,0:T(8,128)(2,1)}) custom-call(bf16[3,256,3072]{2,1,0:T(8,128)(2,1)} %src.1), custom_call_target="tpu_custom_call" | custom-call | tf_op jit(solution)/shard_map/pack/pallas_call | solution.py:248
  2.4 0.0 copy-start
  2.4 5.3 %collective-permute-start = (bf16[3,64,384]{2,1,0:T(8,128)(2,1)}, bf16[3,64,384]{2,1,0:T(8,128)(2,1)S(1)}, u32[]{:S(2)}, u32[]{:S(2)}) collective-permute-start(bf16[3,64,384]{2,1,0:T(8,128)(2,1)} %get-tuple-element.17), channel_id=1, source_target_pairs={{192,0},{32,2},{0,4},{224,6},{200,8},{40,10},{8,12},{232,14},{208,... | collective-permute-start | bytes 442376 | tf_op jit(solution)/shard_map/ppermute | solution.py:265
  7.7 3.4 %collective-permute-start.1 = (bf16[3,64,384]{2,1,0:T(8,128)(2,1)}, bf16[3,64,384]{2,1,0:T(8,128)(2,1)S(1)}, u32[]{:S(2)}, u32[]{:S(2)}) collective-permute-start(bf16[3,64,384]{2,1,0:T(8,128)(2,1)} %get-tuple-element.18), channel_id=1, source_target_pairs={{192,1},{32,3},{0,5},{224,7},{200,9},{40,11},{8,13},{232,15},{208,... | collective-permute-start | bytes 442376 | tf_op jit(solution)/shard_map/ppermute | solution.py:265
  11.1 0.0 collective-permute-done
  11.2 3.0 %collective-permute-done.1 = bf16[3,64,384]{2,1,0:T(8,128)(2,1)S(1)} collective-permute-done((bf16[3,64,384]{2,1,0:T(8,128)(2,1)}, bf16[3,64,384]{2,1,0:T(8,128)(2,1)S(1)}, u32[]{:S(2)}, u32[]{:S(2)}) %collective-permute-start.1) | collective-permute-done | bytes 147488 | tf_op jit(solution)/shard_map/ppermute | solution.py:265
  14.2 2.8 %collective-permute-start.4 = (bf16[3,64,384]{2,1,0:T(8,128)(2,1)S(1)}, bf16[3,64,384]{2,1,0:T(8,128)(2,1)S(1)}, u32[]{:S(2)}, u32[]{:S(2)}) collective-permute-start(bf16[3,64,384]{2,1,0:T(8,128)(2,1)S(1)} %add.8.refs_4_), channel_id=1, source_target_pairs={{0,24},{8,0},{16,8},{24,16},{32,56},{40,32},{48,40},{56,48},{64,88... | collective-permute-start | bytes 442376 | tf_op jit(solution)/shard_map/ppermute | solution.py:229
  17.0 0.0 collective-permute-start.3
  17.0 2.3 %collective-permute-start.2 = (bf16[3,64,384]{2,1,0:T(8,128)(2,1)S(1)}, bf16[3,64,384]{2,1,0:T(8,128)(2,1)S(1)}, u32[]{:S(2)}, u32[]{:S(2)}) collective-permute-start(bf16[3,64,384]{2,1,0:T(8,128)(2,1)S(1)} %add.8.refs_4_), channel_id=1, source_target_pairs={{0,16},{8,24},{16,0},{24,8},{32,48},{40,56},{48,32},{56,40},{64,80... | collective-permute-start | bytes 442376 | tf_op jit(solution)/shard_map/ppermute | solution.py:229
  19.3 2.0 %collective-permute-done.4.refs_7_ = bf16[3,64,384]{2,1,0:T(8,128)(2,1)S(1)} collective-permute-done((bf16[3,64,384]{2,1,0:T(8,128)(2,1)S(1)}, bf16[3,64,384]{2,1,0:T(8,128)(2,1)S(1)}, u32[]{:S(2)}, u32[]{:S(2)}) %collective-permute-start.4) | collective-permute-done | bytes 147488 | tf_op jit(solution)/shard_map/ppermute | solution.py:229
  21.3 3.7 %collective-permute-done.3.refs_5_ = bf16[3,64,384]{2,1,0:T(8,128)(2,1)S(1)} collective-permute-done((bf16[3,64,384]{2,1,0:T(8,128)(2,1)S(1)}, bf16[3,64,384]{2,1,0:T(8,128)(2,1)S(1)}, u32[]{:S(2)}, u32[]{:S(2)}) %collective-permute-start.3) | collective-permute-done | bytes 147488 | tf_op jit(solution)/shard_map/ppermute | solution.py:229
  25.0 0.0 collective-permute-done.2.refs_6_
  25.0 2.8 %collective-permute-start.5 = (bf16[1,128,384]{2,1,0:T(8,128)(2,1)S(1)}, bf16[1,128,384]{2,1,0:T(8,128)(2,1)S(1)}, u32[]{:S(2)}, u32[]{:S(2)}) collective-permute-start(bf16[1,128,384]{2,1,0:T(8,128)(2,1)S(1)} %pad_maximum_fusion.2), channel_id=1, source_target_pairs={{0,32},{8,40},{16,240},{24,248},{32,64},{40,72},{48,16},{56,24},{6... | collective-permute-start | bytes 294920 | tf_op jit(solution)/shard_map/ppermute | solution.py:270
  27.8 0.0 copy-done.4
  27.8 0.1 copy.9.refs_1_
  28.0 0.0 copy-start.1
  28.0 0.0 copy-start.3
  28.0 4.1 %collective-permute-done.5.refs_3_ = bf16[1,128,384]{2,1,0:T(8,128)(2,1)S(1)} collective-permute-done((bf16[1,128,384]{2,1,0:T(8,128)(2,1)S(1)}, bf16[1,128,384]{2,1,0:T(8,128)(2,1)S(1)}, u32[]{:S(2)}, u32[]{:S(2)}) %collective-permute-start.5) | collective-permute-done | bytes 98336 | tf_op jit(solution)/shard_map/ppermute | solution.py:270
  32.1 0.0 copy-done.2
  32.1 0.0 copy-done
  32.1 2.1 %audio_side.1 = (bf16[64,512]{1,0:T(8,128)(2,1)S(1)}, bf16[64,512]{1,0:T(8,128)(2,1)S(1)}, bf16[64,512]{1,0:T(8,128)(2,1)S(1)}, bf16[64,512]{1,0:T(8,128)(2,1)S(1)}, bf16[64,512]{1,0:T(8,128)(2,1)S(1)}) custom-call(s32[2]{0:T(128)S(1)} %copy-done.2, s32[32,2]{1,0:T(8,128)S(1)} %copy.9.refs_1_, bf16[2,512,384]{2,1,0:T(8,128)(2,1)S(1)} %copy-done, ...), custom_call_target="tpu_custom_call" | custom-call | tf_op jit(solution)/shard_map/audio_side/pallas_call | solution.py:285
  34.2 5.8 %collective-permute-start.6 = (bf16[64,512]{1,0:T(8,128)(2,1)S(1)}, bf16[64,512]{1,0:T(8,128)(2,1)S(1)}, u32[]{:S(2)}, u32[]{:S(2)}) collective-permute-start(bf16[64,512]{1,0:T(8,128)(2,1)S(1)} %get-tuple-element.20), channel_id=1, source_target_pairs={{0,240},{8,248},{16,0},{24,8},{32,16},{40,24},{48,32},{56,40},{64,... | collective-permute-start | bytes 196616 | tf_op jit(solution)/shard_map/ppermute | solution.py:224
  40.0 0.0 collective-permute-start.7
  40.0 2.0 %collective-permute-start.8 = (bf16[64,512]{1,0:T(8,128)(2,1)S(1)}, bf16[64,512]{1,0:T(8,128)(2,1)S(1)}, u32[]{:S(2)}, u32[]{:S(2)}) collective-permute-start(bf16[64,512]{1,0:T(8,128)(2,1)S(1)} %get-tuple-element.23), channel_id=1, source_target_pairs={{0,8},{8,16},{16,24},{24,32},{32,40},{40,48},{48,56},{56,64},{64,7... | collective-permute-start | bytes 196616 | tf_op jit(solution)/shard_map/ppermute | solution.py:224
  42.0 0.3 collective-permute-start.9
  42.3 0.1 collective-permute-start.13
  42.4 0.0 collective-permute-done.6.refs_0_
  42.4 2.2 %collective-permute-done.7.refs_1_ = bf16[64,512]{1,0:T(8,128)(2,1)S(1)} collective-permute-done((bf16[64,512]{1,0:T(8,128)(2,1)S(1)}, bf16[64,512]{1,0:T(8,128)(2,1)S(1)}, u32[]{:S(2)}, u32[]{:S(2)}) %collective-permute-start.7) | collective-permute-done | bytes 65568 | tf_op jit(solution)/shard_map/ppermute | solution.py:224
  44.6 4.0 %collective-permute-done.8.refs_3_ = bf16[64,512]{1,0:T(8,128)(2,1)S(1)} collective-permute-done((bf16[64,512]{1,0:T(8,128)(2,1)S(1)}, bf16[64,512]{1,0:T(8,128)(2,1)S(1)}, u32[]{:S(2)}, u32[]{:S(2)}) %collective-permute-start.8) | collective-permute-done | bytes 65568 | tf_op jit(solution)/shard_map/ppermute | solution.py:224
  48.5 1.3 %collective-permute-done.9.refs_4_ = bf16[64,512]{1,0:T(8,128)(2,1)S(1)} collective-permute-done((bf16[64,512]{1,0:T(8,128)(2,1)S(1)}, bf16[64,512]{1,0:T(8,128)(2,1)S(1)}, u32[]{:S(2)}, u32[]{:S(2)}) %collective-permute-start.9) | collective-permute-done | bytes 65568 | tf_op jit(solution)/shard_map/ppermute | solution.py:224
  49.9 0.4 merge.1
  50.3 0.1 collective-permute-start.12
  50.4 2.3 %collective-permute-start.11 = (bf16[64,384]{1,0:T(8,128)(2,1)S(1)}, bf16[64,384]{1,0:T(8,128)(2,1)S(1)}, u32[]{:S(2)}, u32[]{:S(2)}) collective-permute-start(bf16[64,384]{1,0:T(8,128)(2,1)S(1)} %merge.1), channel_id=1, source_target_pairs={{0,16},{8,24},{16,0},{24,8},{32,48},{40,56},{48,32},{56,40},{64,80... | collective-permute-start | bytes 147464 | tf_op jit(solution)/shard_map/ppermute | solution.py:229
  52.7 0.0 collective-permute-start.10
  52.7 1.7 %collective-permute-done.12 = bf16[64,384]{1,0:T(8,128)(2,1)S(1)} collective-permute-done((bf16[64,384]{1,0:T(8,128)(2,1)S(1)}, bf16[64,384]{1,0:T(8,128)(2,1)S(1)}, u32[]{:S(2)}, u32[]{:S(2)}) %collective-permute-start.12) | collective-permute-done | bytes 49184 | tf_op jit(solution)/shard_map/ppermute | solution.py:229
  54.5 1.6 %collective-permute-done.11 = bf16[64,384]{1,0:T(8,128)(2,1)S(1)} collective-permute-done((bf16[64,384]{1,0:T(8,128)(2,1)S(1)}, bf16[64,384]{1,0:T(8,128)(2,1)S(1)}, u32[]{:S(2)}, u32[]{:S(2)}) %collective-permute-start.11) | collective-permute-done | bytes 49184 | tf_op jit(solution)/shard_map/ppermute | solution.py:229
  56.1 2.0 %collective-permute-done.10 = bf16[64,384]{1,0:T(8,128)(2,1)S(1)} collective-permute-done((bf16[64,384]{1,0:T(8,128)(2,1)S(1)}, bf16[64,384]{1,0:T(8,128)(2,1)S(1)}, u32[]{:S(2)}, u32[]{:S(2)}) %collective-permute-start.10) | collective-permute-done | bytes 49184 | tf_op jit(solution)/shard_map/ppermute | solution.py:229
  58.1 0.0 collective-permute-done.13.refs_3_
  58.1 2.0 %collective-permute-start.14 = (bf16[256,384]{1,0:T(8,128)(2,1)S(1)}, bf16[256,384]{1,0:T(8,128)(2,1)S(1)}, u32[]{:S(2)}, u32[]{:S(2)}) collective-permute-start(bf16[256,384]{1,0:T(8,128)(2,1)S(1)} %pad_maximum_fusion.refs_0_), channel_id=1, source_target_pairs={{0,160},{8,168},{16,176},{24,184},{32,192},{40,200},{48,208},{56,2... | collective-permute-start | bytes 589832 | tf_op jit(solution)/shard_map/ppermute | solution.py:224
  60.1 0.3 collective-permute-start.17
  60.5 2.1 %collective-permute-start.20 = (bf16[256,384]{1,0:T(8,128)(2,1)S(1)}, bf16[256,384]{1,0:T(8,128)(2,1)S(1)}, u32[]{:S(2)}, u32[]{:S(2)}) collective-permute-start(bf16[256,384]{1,0:T(8,128)(2,1)S(1)} %pad_maximum_fusion.refs_0_), channel_id=1, source_target_pairs={{0,32},{8,40},{16,48},{24,56},{32,64},{40,72},{48,80},{56,88},{64,... | collective-permute-start | bytes 589832 | tf_op jit(solution)/shard_map/ppermute | solution.py:224
  62.5 1.2 %collective-permute-start.19 = (bf16[256,384]{1,0:T(8,128)(2,1)S(1)}, bf16[256,384]{1,0:T(8,128)(2,1)S(1)}, u32[]{:S(2)}, u32[]{:S(2)}) collective-permute-start(bf16[256,384]{1,0:T(8,128)(2,1)S(1)} %pad_maximum_fusion.refs_0_), channel_id=1, source_target_pairs={{0,224},{8,232},{16,240},{24,248},{32,0},{40,8},{48,16},{56,24},{6... | collective-permute-start | bytes 589832 | tf_op jit(solution)/shard_map/ppermute | solution.py:224
  63.7 0.0 copy-done.1
  63.7 0.0 copy-done.3
  63.7 3.5 %video_side.1 = bf16[512,384]{1,0:T(8,128)(2,1)} custom-call(s32[32]{0:T(128)S(1)} %copy-done.3, s32[32,2]{1,0:T(8,128)S(1)} %copy.9.refs_1_, bf16[512,384]{1,0:T(8,128)(2,1)S(1)} %copy-done.1, bf16[2,128,384]{2,1,0:T(8,128)(2,1)S(1)} %collective-permute-done.13.refs_3_, bf16[3,64,384]{2,1,0:T(8,128)(2,1)S(1)} %add.8.refs_4_, ...), custom_call_target="tpu_custom_call" | custom-call | tf_op jit(solution)/shard_map/video_side/pallas_call | solution.py:311
  67.2 6.1 %collective-permute-done.14.refs_1_ = bf16[256,384]{1,0:T(8,128)(2,1)S(1)} collective-permute-done((bf16[256,384]{1,0:T(8,128)(2,1)S(1)}, bf16[256,384]{1,0:T(8,128)(2,1)S(1)}, u32[]{:S(2)}, u32[]{:S(2)}) %collective-permute-start.14) | collective-permute-done | bytes 196640 | tf_op jit(solution)/shard_map/ppermute | solution.py:224
  73.3 0.0 collective-permute-done.17.refs_2_
  73.3 0.0 collective-permute-start.18
  73.3 0.0 collective-permute-start.16
  73.3 3.3 %collective-permute-start.15 = (bf16[256,384]{1,0:T(8,128)(2,1)S(1)}, bf16[256,384]{1,0:T(8,128)(2,1)S(1)}, u32[]{:S(2)}, u32[]{:S(2)}) collective-permute-start(bf16[256,384]{1,0:T(8,128)(2,1)S(1)} %collective-permute-done.14.refs_1_), channel_id=1, source_target_pairs={{0,224},{8,232},{16,240},{24,248},{32,0},{40,8},{48,16},{56,24},{6... | collective-permute-start | bytes 589832 | tf_op jit(solution)/shard_map/ppermute | solution.py:224
  76.6 0.0 collective-permute-done.20.refs_4_
  76.6 0.0 collective-permute-done.19.refs_3_
  76.6 1.1 %assemble.2.refs_3_ = bf16[2048,384]{1,0:T(8,128)(2,1)} custom-call(bf16[256,384]{1,0:T(8,128)(2,1)S(1)} %pad_maximum_fusion.refs_0_, bf16[256,384]{1,0:T(8,128)(2,1)S(1)} %collective-permute-done.14.refs_1_, bf16[256,384]{1,0:T(8,128)(2,1)S(1)} %collective-permute-done.17.refs_2_, bf16[256,384]{1,0:T(8,128)(2,1)S(1)} %collective-permute-done.19.refs_3_, ...), custom_call_target="tpu_custom_call" | custom-call | tf_op jit(solution)/shard_map/assemble/pallas_call | solution.py:329
  77.7 2.5 %collective-permute-done.18.refs_2_ = bf16[256,384]{1,0:T(8,128)(2,1)S(1)} collective-permute-done((bf16[256,384]{1,0:T(8,128)(2,1)S(1)}, bf16[256,384]{1,0:T(8,128)(2,1)S(1)}, u32[]{:S(2)}, u32[]{:S(2)}) %collective-permute-start.18) | collective-permute-done | bytes 196640 | tf_op jit(solution)/shard_map/ppermute | solution.py:224
  80.2 2.1 %collective-permute-done.16.refs_1_ = bf16[256,384]{1,0:T(8,128)(2,1)S(1)} collective-permute-done((bf16[256,384]{1,0:T(8,128)(2,1)S(1)}, bf16[256,384]{1,0:T(8,128)(2,1)S(1)}, u32[]{:S(2)}, u32[]{:S(2)}) %collective-permute-start.16) | collective-permute-done | bytes 196640 | tf_op jit(solution)/shard_map/ppermute | solution.py:224
  82.3 0.0 collective-permute-done.15.refs_0_
  82.3 0.9 %assemble.3 = bf16[2048,384]{1,0:T(8,128)(2,1)} custom-call(bf16[256,384]{1,0:T(8,128)(2,1)S(1)} %collective-permute-done.15.refs_0_, bf16[256,384]{1,0:T(8,128)(2,1)S(1)} %collective-permute-done.16.refs_1_, bf16[256,384]{1,0:T(8,128)(2,1)S(1)} %collective-permute-done.18.refs_2_, bf16[2048,384]{1,0:T(8,128)(2,1)} %assemble.2.refs_3_), custom_call_target="tpu_custom_call", output_to_operand_aliasing={{}: (3, {})} | custom-call | tf_op jit(solution)/shard_map/assemble/pallas_call | solution.py:329
  (9 shorter events, 0.2 us)
Async XLA Ops:
  0.6 27.2 %copy-start.4 = (s32[32,2]{0,1:T(2,128)S(1)}, s32[32,2]{0,1:T(2,128)}, u32[]{:S(2)}) copy-start(s32[32,2]{0,1:T(2,128)} %param.11) | copy-start | bytes 772
  0.6 31.5 %copy-start.2 = (s32[2]{0:T(128)S(1)}, s32[2]{0:T(128)}, u32[]{:S(2)}) copy-start(s32[2]{0:T(128)} %refs_0_.2) | copy-start | bytes 28
  2.4 29.7 %copy-start = (bf16[2,512,384]{2,1,0:T(8,128)(2,1)S(1)}, bf16[2,512,384]{2,1,0:T(8,128)(2,1)}, u32[]{:S(2)}) copy-start(bf16[2,512,384]{2,1,0:T(8,128)(2,1)} %refs_2_.2) | copy-start | bytes 2359300
  2.4 8.8 %collective-permute-start = (bf16[3,64,384]{2,1,0:T(8,128)(2,1)}, bf16[3,64,384]{2,1,0:T(8,128)(2,1)S(1)}, u32[]{:S(2)}, u32[]{:S(2)}) collective-permute-start(bf16[3,64,384]{2,1,0:T(8,128)(2,1)} %get-tuple-element.17), channel_id=1, source_target_pairs={{192,0},{32,2},{0,4},{224,6},{200,8},{40,10},{8,12},{232,14},{208,... | collective-permute-start | bytes 442376 | tf_op jit(solution)/shard_map/ppermute | solution.py:265
  7.7 6.4 %collective-permute-start.1 = (bf16[3,64,384]{2,1,0:T(8,128)(2,1)}, bf16[3,64,384]{2,1,0:T(8,128)(2,1)S(1)}, u32[]{:S(2)}, u32[]{:S(2)}) collective-permute-start(bf16[3,64,384]{2,1,0:T(8,128)(2,1)} %get-tuple-element.18), channel_id=1, source_target_pairs={{192,1},{32,3},{0,5},{224,7},{200,9},{40,11},{8,13},{232,15},{208,... | collective-permute-start | bytes 442376 | tf_op jit(solution)/shard_map/ppermute | solution.py:265
  14.2 7.1 %collective-permute-start.4 = (bf16[3,64,384]{2,1,0:T(8,128)(2,1)S(1)}, bf16[3,64,384]{2,1,0:T(8,128)(2,1)S(1)}, u32[]{:S(2)}, u32[]{:S(2)}) collective-permute-start(bf16[3,64,384]{2,1,0:T(8,128)(2,1)S(1)} %add.8.refs_4_), channel_id=1, source_target_pairs={{0,24},{8,0},{16,8},{24,16},{32,56},{40,32},{48,40},{56,48},{64,88... | collective-permute-start | bytes 442376 | tf_op jit(solution)/shard_map/ppermute | solution.py:229
  17.0 7.9 %collective-permute-start.3 = (bf16[3,64,384]{2,1,0:T(8,128)(2,1)S(1)}, bf16[3,64,384]{2,1,0:T(8,128)(2,1)S(1)}, u32[]{:S(2)}, u32[]{:S(2)}) collective-permute-start(bf16[3,64,384]{2,1,0:T(8,128)(2,1)S(1)} %add.8.refs_4_), channel_id=1, source_target_pairs={{0,8},{8,16},{16,24},{24,0},{32,40},{40,48},{48,56},{56,32},{64,72... | collective-permute-start | bytes 442376 | tf_op jit(solution)/shard_map/ppermute | solution.py:229
  17.0 7.9 %collective-permute-start.2 = (bf16[3,64,384]{2,1,0:T(8,128)(2,1)S(1)}, bf16[3,64,384]{2,1,0:T(8,128)(2,1)S(1)}, u32[]{:S(2)}, u32[]{:S(2)}) collective-permute-start(bf16[3,64,384]{2,1,0:T(8,128)(2,1)S(1)} %add.8.refs_4_), channel_id=1, source_target_pairs={{0,16},{8,24},{16,0},{24,8},{32,48},{40,56},{48,32},{56,40},{64,80... | collective-permute-start | bytes 442376 | tf_op jit(solution)/shard_map/ppermute | solution.py:229
  25.0 7.1 %collective-permute-start.5 = (bf16[1,128,384]{2,1,0:T(8,128)(2,1)S(1)}, bf16[1,128,384]{2,1,0:T(8,128)(2,1)S(1)}, u32[]{:S(2)}, u32[]{:S(2)}) collective-permute-start(bf16[1,128,384]{2,1,0:T(8,128)(2,1)S(1)} %pad_maximum_fusion.2), channel_id=1, source_target_pairs={{0,32},{8,40},{16,240},{24,248},{32,64},{40,72},{48,16},{56,24},{6... | collective-permute-start | bytes 294920 | tf_op jit(solution)/shard_map/ppermute | solution.py:270
  28.0 35.7 %copy-start.1 = (bf16[512,384]{1,0:T(8,128)(2,1)S(1)}, bf16[512,384]{1,0:T(8,128)(2,1)}, u32[]{:S(2)}) copy-start(bf16[512,384]{1,0:T(8,128)(2,1)} %refs_2_.3) | copy-start | bytes 1179652
  28.0 35.7 %copy-start.3 = (s32[32]{0:T(128)S(1)}, s32[32]{0:T(128)}, u32[]{:S(2)}) copy-start(s32[32]{0:T(128)} %refs_0_.3) | copy-start | bytes 388
  34.2 8.2 %collective-permute-start.6 = (bf16[64,512]{1,0:T(8,128)(2,1)S(1)}, bf16[64,512]{1,0:T(8,128)(2,1)S(1)}, u32[]{:S(2)}, u32[]{:S(2)}) collective-permute-start(bf16[64,512]{1,0:T(8,128)(2,1)S(1)} %get-tuple-element.20), channel_id=1, source_target_pairs={{0,240},{8,248},{16,0},{24,8},{32,16},{40,24},{48,32},{56,40},{64,... | collective-permute-start | bytes 196616 | tf_op jit(solution)/shard_map/ppermute | solution.py:224
  40.0 4.6 %collective-permute-start.7 = (bf16[64,512]{1,0:T(8,128)(2,1)S(1)}, bf16[64,512]{1,0:T(8,128)(2,1)S(1)}, u32[]{:S(2)}, u32[]{:S(2)}) collective-permute-start(bf16[64,512]{1,0:T(8,128)(2,1)S(1)} %get-tuple-element.21), channel_id=1, source_target_pairs={{0,248},{8,0},{16,8},{24,16},{32,24},{40,32},{48,40},{56,48},{64,5... | collective-permute-start | bytes 196616 | tf_op jit(solution)/shard_map/ppermute | solution.py:224
  40.0 8.6 %collective-permute-start.8 = (bf16[64,512]{1,0:T(8,128)(2,1)S(1)}, bf16[64,512]{1,0:T(8,128)(2,1)S(1)}, u32[]{:S(2)}, u32[]{:S(2)}) collective-permute-start(bf16[64,512]{1,0:T(8,128)(2,1)S(1)} %get-tuple-element.23), channel_id=1, source_target_pairs={{0,8},{8,16},{16,24},{24,32},{32,40},{40,48},{48,56},{56,64},{64,7... | collective-permute-start | bytes 196616 | tf_op jit(solution)/shard_map/ppermute | solution.py:224
  42.0 7.9 %collective-permute-start.9 = (bf16[64,512]{1,0:T(8,128)(2,1)S(1)}, bf16[64,512]{1,0:T(8,128)(2,1)S(1)}, u32[]{:S(2)}, u32[]{:S(2)}) collective-permute-start(bf16[64,512]{1,0:T(8,128)(2,1)S(1)} %get-tuple-element.24), channel_id=1, source_target_pairs={{0,16},{8,24},{16,32},{24,40},{32,48},{40,56},{48,64},{56,72},{64,... | collective-permute-start | bytes 196616 | tf_op jit(solution)/shard_map/ppermute | solution.py:224
  42.3 15.7 %collective-permute-start.13 = (bf16[2,128,384]{2,1,0:T(8,128)(2,1)S(1)}, bf16[2,128,384]{2,1,0:T(8,128)(2,1)S(1)}, u32[]{:S(2)}, u32[]{:S(2)}) collective-permute-start(bf16[2,128,384]{2,1,0:T(8,128)(2,1)S(1)} %pad_maximum_fusion.1), channel_id=1, source_target_pairs={{0,32},{8,40},{16,240},{24,248},{32,64},{40,72},{48,16},{56,24},{6... | collective-permute-start | bytes 589832 | tf_op jit(solution)/shard_map/ppermute | solution.py:270
  50.3 4.2 %collective-permute-start.12 = (bf16[64,384]{1,0:T(8,128)(2,1)S(1)}, bf16[64,384]{1,0:T(8,128)(2,1)S(1)}, u32[]{:S(2)}, u32[]{:S(2)}) collective-permute-start(bf16[64,384]{1,0:T(8,128)(2,1)S(1)} %merge.1), channel_id=1, source_target_pairs={{0,24},{8,0},{16,8},{24,16},{32,56},{40,32},{48,40},{56,48},{64,88... | collective-permute-start | bytes 147464 | tf_op jit(solution)/shard_map/ppermute | solution.py:229
  50.4 5.7 %collective-permute-start.11 = (bf16[64,384]{1,0:T(8,128)(2,1)S(1)}, bf16[64,384]{1,0:T(8,128)(2,1)S(1)}, u32[]{:S(2)}, u32[]{:S(2)}) collective-permute-start(bf16[64,384]{1,0:T(8,128)(2,1)S(1)} %merge.1), channel_id=1, source_target_pairs={{0,16},{8,24},{16,0},{24,8},{32,48},{40,56},{48,32},{56,40},{64,80... | collective-permute-start | bytes 147464 | tf_op jit(solution)/shard_map/ppermute | solution.py:229
  52.7 5.3 %collective-permute-start.10 = (bf16[64,384]{1,0:T(8,128)(2,1)S(1)}, bf16[64,384]{1,0:T(8,128)(2,1)S(1)}, u32[]{:S(2)}, u32[]{:S(2)}) collective-permute-start(bf16[64,384]{1,0:T(8,128)(2,1)S(1)} %merge.1), channel_id=1, source_target_pairs={{0,8},{8,16},{16,24},{24,0},{32,40},{40,48},{48,56},{56,32},{64,72... | collective-permute-start | bytes 147464 | tf_op jit(solution)/shard_map/ppermute | solution.py:229
  58.1 15.2 %collective-permute-start.14 = (bf16[256,384]{1,0:T(8,128)(2,1)S(1)}, bf16[256,384]{1,0:T(8,128)(2,1)S(1)}, u32[]{:S(2)}, u32[]{:S(2)}) collective-permute-start(bf16[256,384]{1,0:T(8,128)(2,1)S(1)} %pad_maximum_fusion.refs_0_), channel_id=1, source_target_pairs={{0,160},{8,168},{16,176},{24,184},{32,192},{40,200},{48,208},{56,2... | collective-permute-start | bytes 589832 | tf_op jit(solution)/shard_map/ppermute | solution.py:224
  60.1 13.2 %collective-permute-start.17 = (bf16[256,384]{1,0:T(8,128)(2,1)S(1)}, bf16[256,384]{1,0:T(8,128)(2,1)S(1)}, u32[]{:S(2)}, u32[]{:S(2)}) collective-permute-start(bf16[256,384]{1,0:T(8,128)(2,1)S(1)} %pad_maximum_fusion.refs_0_), channel_id=1, source_target_pairs={{0,64},{8,72},{16,80},{24,88},{32,96},{40,104},{48,112},{56,120},{... | collective-permute-start | bytes 589832 | tf_op jit(solution)/shard_map/ppermute | solution.py:224
  60.5 16.1 %collective-permute-start.20 = (bf16[256,384]{1,0:T(8,128)(2,1)S(1)}, bf16[256,384]{1,0:T(8,128)(2,1)S(1)}, u32[]{:S(2)}, u32[]{:S(2)}) collective-permute-start(bf16[256,384]{1,0:T(8,128)(2,1)S(1)} %pad_maximum_fusion.refs_0_), channel_id=1, source_target_pairs={{0,32},{8,40},{16,48},{24,56},{32,64},{40,72},{48,80},{56,88},{64,... | collective-permute-start | bytes 589832 | tf_op jit(solution)/shard_map/ppermute | solution.py:224
  62.5 14.0 %collective-permute-start.19 = (bf16[256,384]{1,0:T(8,128)(2,1)S(1)}, bf16[256,384]{1,0:T(8,128)(2,1)S(1)}, u32[]{:S(2)}, u32[]{:S(2)}) collective-permute-start(bf16[256,384]{1,0:T(8,128)(2,1)S(1)} %pad_maximum_fusion.refs_0_), channel_id=1, source_target_pairs={{0,224},{8,232},{16,240},{24,248},{32,0},{40,8},{48,16},{56,24},{6... | collective-permute-start | bytes 589832 | tf_op jit(solution)/shard_map/ppermute | solution.py:224
  73.3 6.9 %collective-permute-start.18 = (bf16[256,384]{1,0:T(8,128)(2,1)S(1)}, bf16[256,384]{1,0:T(8,128)(2,1)S(1)}, u32[]{:S(2)}, u32[]{:S(2)}) collective-permute-start(bf16[256,384]{1,0:T(8,128)(2,1)S(1)} %collective-permute-done.17.refs_2_), channel_id=1, source_target_pairs={{0,32},{8,40},{16,48},{24,56},{32,64},{40,72},{48,80},{56,88},{64,... | collective-permute-start | bytes 589832 | tf_op jit(solution)/shard_map/ppermute | solution.py:224
  73.3 9.0 %collective-permute-start.16 = (bf16[256,384]{1,0:T(8,128)(2,1)S(1)}, bf16[256,384]{1,0:T(8,128)(2,1)S(1)}, u32[]{:S(2)}, u32[]{:S(2)}) collective-permute-start(bf16[256,384]{1,0:T(8,128)(2,1)S(1)} %collective-permute-done.14.refs_1_), channel_id=1, source_target_pairs={{0,32},{8,40},{16,48},{24,56},{32,64},{40,72},{48,80},{56,88},{64,... | collective-permute-start | bytes 589832 | tf_op jit(solution)/shard_map/ppermute | solution.py:224
  73.3 9.0 %collective-permute-start.15 = (bf16[256,384]{1,0:T(8,128)(2,1)S(1)}, bf16[256,384]{1,0:T(8,128)(2,1)S(1)}, u32[]{:S(2)}, u32[]{:S(2)}) collective-permute-start(bf16[256,384]{1,0:T(8,128)(2,1)S(1)} %collective-permute-done.14.refs_1_), channel_id=1, source_target_pairs={{0,224},{8,232},{16,240},{24,248},{32,0},{40,8},{48,16},{56,24},{6... | collective-permute-start | bytes 589832 | tf_op jit(solution)/shard_map/ppermute | solution.py:224
